TPU v7x, 512 devices: a whole 4x4x16 slice. The times are simulated.
512 devices in a mesh: dp: 32 (over z_hi, x, y), ctx: 16 (over z_lo, core).
Axes of the slice: x: 4, y: 4, z: 16 (z_hi: 2, z_lo: 8; z = z_hi * 8 + z_lo), core: 2. Of those that a mesh axis runs over, the one named last changes fastest.
Arguments:
- query_rows: bfloat16 [32, 1024, 4096], P('dp', 'ctx'), may hold values from -40 to 40
- key_rows: bfloat16 [32, 1024, 4096], P('dp', 'ctx'), may hold values from -40 to 40
- value_rows: bfloat16 [32, 1024, 4096], P('dp', 'ctx'), may hold values from -6 to 6
- query_tangent: bfloat16 [32, 1024, 4096], P('dp', 'ctx'), may hold values from -6 to 6
- key_tangent: bfloat16 [32, 1024, 4096], P('dp', 'ctx'), may hold values from -6 to 6
- value_tangent: bfloat16 [32, 1024, 4096], P('dp', 'ctx'), may hold values from -6 to 6
- query_gain: bfloat16 [4096], P('dp'), may hold values from 1.1953125 to 2.390625
- key_gain: bfloat16 [4096], P('dp'), may hold values from 1.1953125 to 2.390625
Outputs:
- attended: bfloat16 [32, 1024, 4096], P('dp', 'ctx')
- attended_tangent: bfloat16 [32, 1024, 4096], P('dp', 'ctx')
All inputs are finite; a program needn't handle non-finite values.
Results may differ from a plain program's by a relative error of at most 0.0065.
The roundings to bfloat16 on the way count: a program that leaves them out, or rounds other values in their place, can miss the bound.
Values may be sent and summed in bfloat16 or wider, within the bound.
No kernel may reach another device: no remote copies, remote signals or barrier semaphores. Data moves between devices by JAX's collectives and lax.ppermute only.
A program may use at most 64 MiB of HBM per device.

v0:
```python
import jax
import jax.numpy as jnp
from jax import lax
from jax.sharding import PartitionSpec as P

HEAD_DIM = 128


CONTRACT = (((1,), (1,)), ((), ()))


def normalize(rows_in, tangent_in, gain_full):
    values = rows_in.astype(jnp.float32)
    tangent = tangent_in.astype(jnp.float32)
    gain_f = gain_full.astype(jnp.float32)
    inverse = lax.rsqrt(jnp.mean(values * values, axis=-1, keepdims=True) + 1e-06)
    cross = jnp.mean(values * tangent, axis=-1, keepdims=True)
    normed = (values * inverse * gain_f).astype(jnp.bfloat16)
    normed_tangent = (
        (tangent * inverse - values * (inverse * inverse * inverse) * cross) * gain_f
    ).astype(jnp.bfloat16)
    return (normed, normed_tangent)


def single_head(operands):
    queries, queries_dot, keys_in, keys_dot, values, values_dot = operands
    total = queries.shape[0]
    block = min(512, total)
    factor = queries.shape[-1] ** (-0.5)

    def one_block(pair):
        query_block, query_block_dot = pair
        scores = (
            lax.dot_general(query_block, keys_in, CONTRACT, preferred_element_type=jnp.float32)
            * factor
        )
        scores_dot = (
            lax.dot_general(query_block_dot, keys_in, CONTRACT, preferred_element_type=jnp.float32)
            + lax.dot_general(query_block, keys_dot, CONTRACT, preferred_element_type=jnp.float32)
        ) * factor
        peak = jnp.max(scores, axis=-1, keepdims=True)
        exponent = jnp.exp(scores - peak)
        weights = exponent / jnp.sum(exponent, axis=-1, keepdims=True)
        weights_dot = weights * (scores_dot - jnp.sum(weights * scores_dot, axis=-1, keepdims=True))
        probs = weights.astype(jnp.bfloat16)
        probs_dot = weights_dot.astype(jnp.bfloat16)
        output = jnp.dot(probs, values, preferred_element_type=jnp.float32)
        output_dot = jnp.dot(probs_dot, values, preferred_element_type=jnp.float32) + jnp.dot(
            probs, values_dot, preferred_element_type=jnp.float32
        )
        return (output.astype(jnp.bfloat16), output_dot.astype(jnp.bfloat16))

    blocked = (
        queries.reshape(total // block, block, queries.shape[-1]),
        queries_dot.reshape(total // block, block, queries.shape[-1]),
    )
    output, output_dot = lax.map(one_block, blocked)
    return (output.reshape(total, values.shape[-1]), output_dot.reshape(total, values.shape[-1]))


def attend(pieces):
    heads_first = tuple((jnp.moveaxis(piece, 1, 0) for piece in pieces))
    output, output_dot = lax.map(single_head, heads_first)
    return (jnp.moveaxis(output, 0, 1), jnp.moveaxis(output_dot, 0, 1))


def finish(pieces):
    flat_pieces = tuple((piece[:, 0] for piece in pieces))
    output, output_dot = attend(flat_pieces)
    output = output[:, None]
    output_dot = output_dot[:, None]
    return (
        lax.all_to_all(output, "ctx", split_axis=0, concat_axis=1, tiled=True),
        lax.all_to_all(output_dot, "ctx", split_axis=0, concat_axis=1, tiled=True),
    )


def local(
    query_rows,
    key_rows,
    value_rows,
    query_tangent,
    key_tangent,
    value_tangent,
    query_gain,
    key_gain,
):
    gathered_query, gathered_key = (
        lax.all_gather(query_gain, "dp", axis=0, tiled=True),
        lax.all_gather(key_gain, "dp", axis=0, tiled=True),
    )
    rows = query_rows.shape[1]
    width = query_rows.shape[2]
    groups = lax.axis_size("ctx")
    per_group = width // (groups * HEAD_DIM)

    def split_heads(array):
        return array.reshape(rows, groups, per_group, HEAD_DIM)

    query_normed, query_dot = normalize(query_rows[0], query_tangent[0], gathered_query)
    key_normed, key_dot = normalize(key_rows[0], key_tangent[0], gathered_key)
    query_split = split_heads(query_normed)
    query_dot_split = split_heads(query_dot)
    key_split = split_heads(key_normed)
    key_dot_split = split_heads(key_dot)
    value_split = split_heads(value_rows[0])
    value_dot_split = split_heads(value_tangent[0])
    attended, attended_tangent = finish(
        (
            lax.all_to_all(query_split, "ctx", split_axis=1, concat_axis=0, tiled=True),
            lax.all_to_all(query_dot_split, "ctx", split_axis=1, concat_axis=0, tiled=True),
            lax.all_to_all(key_split, "ctx", split_axis=1, concat_axis=0, tiled=True),
            lax.all_to_all(key_dot_split, "ctx", split_axis=1, concat_axis=0, tiled=True),
            lax.all_to_all(value_split, "ctx", split_axis=1, concat_axis=0, tiled=True),
            lax.all_to_all(value_dot_split, "ctx", split_axis=1, concat_axis=0, tiled=True),
        )
    )
    return (attended.reshape(1, rows, width), attended_tangent.reshape(1, rows, width))


def solution(mesh):
    in_specs = (
        P("dp", "ctx", None),
        P("dp", "ctx", None),
        P("dp", "ctx", None),
        P("dp", "ctx", None),
        P("dp", "ctx", None),
        P("dp", "ctx", None),
        P("dp"),
        P("dp"),
    )
    out_specs = (P("dp", "ctx", None), P("dp", "ctx", None))
    return jax.shard_map(local, mesh=mesh, in_specs=in_specs, out_specs=out_specs, check_vma=False)
```

profile of v0, /device:TPU:1, one launch (start us, length us, event | category | flops | bytes accessed | tf_op | source)
XLA Modules:
  0.0 612.1 jit_solution(5960608164137804768)
XLA Ops:
  0.7 2.1 reshape.159
  2.8 1.5 multiply_reduce_fusion.4
  5.4 149.6 %all-gather = bf16[32,1,128]{2,1,0:T(2,128)(2,1)S(1)} all-gather(bf16[1,1,128]{2,1,0:T(2,128)(2,1)S(1)} %bitcast.153), channel_id=1, replica_groups=mesh['dp'=32,'ctx'=16] {'dp'}, dimensions={0}, use_global_device_ids=true | all-gather | bytes 8448 | tf_op jit(solution)/shard_map/all_gather | solution.py:89
  155.1 1.2 fusion.27
  157.3 19.9 %all-to-all-start = ((bf16[64,16,2,128]{3,0,2,1:T(8,128)(2,1)}), bf16[64,16,2,128]{3,0,2,1:T(8,128)(2,1)S(1)}, u32[]{:S(2)}, u32[]{:S(2)}) async-start(bf16[64,16,2,128]{3,0,2,1:T(8,128)(2,1)} %copy.44), calls=%async_computation | async-start | bytes 1048576 | tf_op jit(solution)/shard_map/all_to_all | solution.py:110
  178.2 25.1 %all-to-all-done = bf16[64,16,2,128]{3,0,2,1:T(8,128)(2,1)S(1)} async-done(((bf16[64,16,2,128]{3,0,2,1:T(8,128)(2,1)}), bf16[64,16,2,128]{3,0,2,1:T(8,128)(2,1)S(1)}, u32[]{:S(2)}, u32[]{:S(2)}) %all-to-all-start) | async-done | bytes 524320 | tf_op jit(solution)/shard_map/all_to_all | solution.py:110
  204.2 7.2 %all-to-all-start.1 = ((bf16[64,16,2,128]{3,0,2,1:T(8,128)(2,1)}), bf16[64,16,2,128]{3,0,2,1:T(8,128)(2,1)}, u32[]{:S(2)}, u32[]{:S(2)}) async-start(bf16[64,16,2,128]{3,0,2,1:T(8,128)(2,1)} %copy.48), calls=%async_computation.1 | async-start | bytes 1048576 | tf_op jit(solution)/shard_map/all_to_all | solution.py:111
  213.5 137.8 %all-gather.1 = bf16[32,1,128]{2,1,0:T(2,128)(2,1)S(1)} all-gather(bf16[1,1,128]{2,1,0:T(2,128)(2,1)S(1)} %bitcast.154), channel_id=1, replica_groups=mesh['dp'=32,'ctx'=16] {'dp'}, dimensions={0}, use_global_device_ids=true | all-gather | bytes 8448 | tf_op jit(solution)/shard_map/all_gather | solution.py:90
  353.0 33.0 %all-to-all-start.2 = ((bf16[64,16,2,128]{3,0,2,1:T(8,128)(2,1)}), bf16[64,16,2,128]{3,0,2,1:T(8,128)(2,1)S(1)}, u32[]{:S(2)}, u32[]{:S(2)}) async-start(bf16[64,16,2,128]{3,0,2,1:T(8,128)(2,1)} %copy.52), calls=%async_computation.2 | async-start | bytes 1048576 | tf_op jit(solution)/shard_map/all_to_all | solution.py:112
  387.1 25.2 %all-to-all-done.2 = bf16[64,16,2,128]{3,0,2,1:T(8,128)(2,1)S(1)} async-done(((bf16[64,16,2,128]{3,0,2,1:T(8,128)(2,1)}), bf16[64,16,2,128]{3,0,2,1:T(8,128)(2,1)S(1)}, u32[]{:S(2)}, u32[]{:S(2)}) %all-to-all-start.2) | async-done | bytes 524320 | tf_op jit(solution)/shard_map/all_to_all | solution.py:112
  412.2 7.2 %all-to-all-start.3 = ((bf16[64,16,2,128]{3,0,2,1:T(8,128)(2,1)}), bf16[64,16,2,128]{3,0,2,1:T(8,128)(2,1)S(1)}, u32[]{:S(2)}, u32[]{:S(2)}) async-start(bf16[64,16,2,128]{3,0,2,1:T(8,128)(2,1)} %copy.56), calls=%async_computation.3 | async-start | bytes 1048576 | tf_op jit(solution)/shard_map/all_to_all | solution.py:113
  420.8 24.8 %all-to-all-done.3 = bf16[64,16,2,128]{3,0,2,1:T(8,128)(2,1)S(1)} async-done(((bf16[64,16,2,128]{3,0,2,1:T(8,128)(2,1)}), bf16[64,16,2,128]{3,0,2,1:T(8,128)(2,1)S(1)}, u32[]{:S(2)}, u32[]{:S(2)}) %all-to-all-start.3) | async-done | bytes 524320 | tf_op jit(solution)/shard_map/all_to_all | solution.py:113
  445.6 7.2 %all-to-all-start.4 = ((bf16[64,16,2,128]{3,0,2,1:T(8,128)(2,1)}), bf16[64,16,2,128]{3,0,2,1:T(8,128)(2,1)S(1)}, u32[]{:S(2)}, u32[]{:S(2)}) async-start(bf16[64,16,2,128]{3,0,2,1:T(8,128)(2,1)} %copy.58), calls=%async_computation.4 | async-start | bytes 1048576 | tf_op jit(solution)/shard_map/all_to_all | solution.py:114
  454.1 24.8 %all-to-all-done.4 = bf16[64,16,2,128]{3,0,2,1:T(8,128)(2,1)S(1)} async-done(((bf16[64,16,2,128]{3,0,2,1:T(8,128)(2,1)}), bf16[64,16,2,128]{3,0,2,1:T(8,128)(2,1)S(1)}, u32[]{:S(2)}, u32[]{:S(2)}) %all-to-all-start.4) | async-done | bytes 524320 | tf_op jit(solution)/shard_map/all_to_all | solution.py:114
  478.9 7.2 %all-to-all-start.5 = ((bf16[64,16,2,128]{3,0,2,1:T(8,128)(2,1)}), bf16[64,16,2,128]{3,0,2,1:T(8,128)(2,1)}, u32[]{:S(2)}, u32[]{:S(2)}) async-start(bf16[64,16,2,128]{3,0,2,1:T(8,128)(2,1)} %copy.60), calls=%async_computation.5 | async-start | bytes 1048576 | tf_op jit(solution)/shard_map/all_to_all | solution.py:115
  489.8 22.6 %all-to-all-done.5 = bf16[64,16,2,128]{3,0,2,1:T(8,128)(2,1)} async-done(((bf16[64,16,2,128]{3,0,2,1:T(8,128)(2,1)}), bf16[64,16,2,128]{3,0,2,1:T(8,128)(2,1)}, u32[]{:S(2)}, u32[]{:S(2)}) %all-to-all-start.5) | async-done | bytes 524320 | tf_op jit(solution)/shard_map/all_to_all | solution.py:115
  512.3 1.9 copy.61
  514.2 27.2 %while.25 = (s32[]{:T(128)}, bf16[2,1024,128]{2,1,0:T(8,128)(2,1)}, bf16[2,1024,128]{2,1,0:T(8,128)(2,1)}, bf16[2,1024,128]{2,1,0:T(8,128)(2,1)S(1)}, bf16[2,102...) while((s32[]{:T(128)}, bf16[2,1024,128]{2,1,0:T(8,128)(2,1)}, ...), condition=%wide.region_10.11_spmd, body=%wide.region_4.10_spmd.sunk | while | flops 814414336 | bytes 30030684 | solution.py:63
  518.2 8.8 %while.26 = (s32[]{:T(128)}, bf16[2,512,128]{2,1,0:T(8,128)(2,1)S(1)}, bf16[2,512,128]{2,1,0:T(8,128)(2,1)S(1)}, bf16[2,512,128]{2,1,0:T(8,128)(2,1)S(1)}, bf16[...) while((s32[]{:T(128)}, ...), condition=%wide.region_9.9_spmd, body=%wide.region_5.8_spmd.sunk | while | flops 814414336 | bytes 25835640 | solution.py:57
  519.7 1.3 multiply_reduce_fusion.9
  524.1 1.3 multiply_reduce_fusion.9
  531.8 8.8 %while.26 = (s32[]{:T(128)}, bf16[2,512,128]{2,1,0:T(8,128)(2,1)S(1)}, bf16[2,512,128]{2,1,0:T(8,128)(2,1)S(1)}, bf16[2,512,128]{2,1,0:T(8,128)(2,1)S(1)}, bf16[...) while((s32[]{:T(128)}, ...), condition=%wide.region_9.9_spmd, body=%wide.region_5.8_spmd.sunk | while | flops 814414336 | bytes 25835640 | solution.py:57
  533.3 1.3 multiply_reduce_fusion.9
  537.7 1.3 multiply_reduce_fusion.9
  541.4 2.4 copy.87
  543.9 7.2 %all-to-all-start.6 = ((bf16[1024,1,2,128]{3,2,1,0:T(2,128)(2,1)}), bf16[1024,1,2,128]{3,2,1,0:T(2,128)(2,1)S(1)}, u32[]{:S(2)}, u32[]{:S(2)}) async-start(bf16[1024,1,2,128]{3,2,1,0:T(2,128)(2,1)} %bitcast.106), calls=%async_computation.6 | async-start | bytes 1048576 | tf_op jit(solution)/shard_map/all_to_all | solution.py:73
  551.1 1.3 copy.86
  552.4 24.8 %all-to-all-done.6 = bf16[1024,1,2,128]{3,2,1,0:T(2,128)(2,1)S(1)} async-done(((bf16[1024,1,2,128]{3,2,1,0:T(2,128)(2,1)}), bf16[1024,1,2,128]{3,2,1,0:T(2,128)(2,1)S(1)}, u32[]{:S(2)}, u32[]{:S(2)}) %all-to-all-start.6) | async-done | bytes 524320 | tf_op jit(solution)/shard_map/all_to_all | solution.py:73
  577.2 7.2 %all-to-all-start.7 = ((bf16[1024,1,2,128]{3,2,1,0:T(2,128)(2,1)}), bf16[1024,1,2,128]{3,2,1,0:T(2,128)(2,1)S(1)}, u32[]{:S(2)}, u32[]{:S(2)}) async-start(bf16[1024,1,2,128]{3,2,1,0:T(2,128)(2,1)} %bitcast.105), calls=%async_computation.7 | async-start | bytes 1048576 | tf_op jit(solution)/shard_map/all_to_all | solution.py:74
  584.8 1.2 reshape.157
  585.9 24.6 %all-to-all-done.7 = bf16[1024,1,2,128]{3,2,1,0:T(2,128)(2,1)S(1)} async-done(((bf16[1024,1,2,128]{3,2,1,0:T(2,128)(2,1)}), bf16[1024,1,2,128]{3,2,1,0:T(2,128)(2,1)S(1)}, u32[]{:S(2)}, u32[]{:S(2)}) %all-to-all-start.7) | async-done | bytes 524320 | tf_op jit(solution)/shard_map/all_to_all | solution.py:74
  610.9 1.2 reshape.158
  (95 shorter events, 37.7 us)
Async XLA Ops:
  0.6 3.7 copy-start
  0.6 4.8 copy-start.9
  156.3 20.9 %copy-start.3 = (bf16[64,16,2,128]{3,1,2,0:T(8,128)(2,1)S(1)}, bf16[64,16,2,128]{3,1,2,0:T(8,128)(2,1)}, u32[]{:S(2)}) copy-start(bf16[64,16,2,128]{3,1,2,0:T(8,128)(2,1)} %get-tuple-element.149) | copy-start | bytes 1572868
  156.3 55.0 %copy-start.2 = (bf16[1,64,4096]{2,1,0:T(8,128)(2,1)S(1)}, bf16[1,64,4096]{2,1,0:T(8,128)(2,1)}, u32[]{:S(2)}) copy-start(bf16[1,64,4096]{2,1,0:T(8,128)(2,1)} %param.13) | copy-start | bytes 1572868
  157.3 46.1 %all-to-all-start = ((bf16[64,16,2,128]{3,0,2,1:T(8,128)(2,1)}), bf16[64,16,2,128]{3,0,2,1:T(8,128)(2,1)S(1)}, u32[]{:S(2)}, u32[]{:S(2)}) async-start(bf16[64,16,2,128]{3,0,2,1:T(8,128)(2,1)} %copy.44), calls=%async_computation | async-start | bytes 1048576 | tf_op jit(solution)/shard_map/all_to_all | solution.py:110
  177.2 35.2 %copy-start.1 = (bf16[1,64,4096]{2,1,0:T(8,128)(2,1)S(1)}, bf16[1,64,4096]{2,1,0:T(8,128)(2,1)}, u32[]{:S(2)}) copy-start(bf16[1,64,4096]{2,1,0:T(8,128)(2,1)} %param.16) | copy-start | bytes 1572868
  178.2 35.2 %copy-start.10 = (bf16[128]{0:T(256)(128)(2,1)S(1)}, bf16[128]{0:T(256)(128)(2,1)}, u32[]{:S(2)}) copy-start(bf16[128]{0:T(256)(128)(2,1)} %param.19) | copy-start | bytes 772
  203.4 0.8 copy-start.4
  204.2 148.9 %all-to-all-start.1 = ((bf16[64,16,2,128]{3,0,2,1:T(8,128)(2,1)}), bf16[64,16,2,128]{3,0,2,1:T(8,128)(2,1)}, u32[]{:S(2)}, u32[]{:S(2)}) async-start(bf16[64,16,2,128]{3,0,2,1:T(8,128)(2,1)} %copy.48), calls=%async_computation.1 | async-start | bytes 1048576 | tf_op jit(solution)/shard_map/all_to_all | solution.py:111
  352.0 67.4 %copy-start.6 = (bf16[1,64,4096]{2,1,0:T(8,128)(2,1)S(1)}, bf16[1,64,4096]{2,1,0:T(8,128)(2,1)}, u32[]{:S(2)}) copy-start(bf16[1,64,4096]{2,1,0:T(8,128)(2,1)} %param.14) | copy-start | bytes 1572868
  353.0 59.2 %all-to-all-start.2 = ((bf16[64,16,2,128]{3,0,2,1:T(8,128)(2,1)}), bf16[64,16,2,128]{3,0,2,1:T(8,128)(2,1)S(1)}, u32[]{:S(2)}, u32[]{:S(2)}) async-start(bf16[64,16,2,128]{3,0,2,1:T(8,128)(2,1)} %copy.52), calls=%async_computation.2 | async-start | bytes 1048576 | tf_op jit(solution)/shard_map/all_to_all | solution.py:112
  387.1 65.7 %copy-start.7 = (bf16[1,64,4096]{2,1,0:T(8,128)(2,1)S(1)}, bf16[1,64,4096]{2,1,0:T(8,128)(2,1)}, u32[]{:S(2)}) copy-start(bf16[1,64,4096]{2,1,0:T(8,128)(2,1)} %param.17) | copy-start | bytes 1572868
  412.2 33.3 %all-to-all-start.3 = ((bf16[64,16,2,128]{3,0,2,1:T(8,128)(2,1)}), bf16[64,16,2,128]{3,0,2,1:T(8,128)(2,1)S(1)}, u32[]{:S(2)}, u32[]{:S(2)}) async-start(bf16[64,16,2,128]{3,0,2,1:T(8,128)(2,1)} %copy.56), calls=%async_computation.3 | async-start | bytes 1048576 | tf_op jit(solution)/shard_map/all_to_all | solution.py:113
  420.8 65.3 %copy-start.5 = (bf16[64,16,2,128]{3,0,2,1:T(8,128)(2,1)S(1)}, bf16[64,16,2,128]{3,0,2,1:T(8,128)(2,1)}, u32[]{:S(2)}) copy-start(bf16[64,16,2,128]{3,0,2,1:T(8,128)(2,1)} %copy-done.4) | copy-start | bytes 1572868
  445.6 33.3 %all-to-all-start.4 = ((bf16[64,16,2,128]{3,0,2,1:T(8,128)(2,1)}), bf16[64,16,2,128]{3,0,2,1:T(8,128)(2,1)S(1)}, u32[]{:S(2)}, u32[]{:S(2)}) async-start(bf16[64,16,2,128]{3,0,2,1:T(8,128)(2,1)} %copy.58), calls=%async_computation.4 | async-start | bytes 1048576 | tf_op jit(solution)/shard_map/all_to_all | solution.py:114
  478.9 33.4 %all-to-all-start.5 = ((bf16[64,16,2,128]{3,0,2,1:T(8,128)(2,1)}), bf16[64,16,2,128]{3,0,2,1:T(8,128)(2,1)}, u32[]{:S(2)}, u32[]{:S(2)}) async-start(bf16[64,16,2,128]{3,0,2,1:T(8,128)(2,1)} %copy.60), calls=%async_computation.5 | async-start | bytes 1048576 | tf_op jit(solution)/shard_map/all_to_all | solution.py:115
  541.4 9.6 %copy-start.8 = (bf16[2,1024,128]{2,1,0:T(8,128)(2,1)S(1)}, bf16[2,1024,128]{2,1,0:T(8,128)(2,1)}, u32[]{:S(2)}) copy-start(bf16[2,1024,128]{2,1,0:T(8,128)(2,1)} %get-tuple-element.99) | copy-start | bytes 1572868
  543.9 33.4 %all-to-all-start.6 = ((bf16[1024,1,2,128]{3,2,1,0:T(2,128)(2,1)}), bf16[1024,1,2,128]{3,2,1,0:T(2,128)(2,1)S(1)}, u32[]{:S(2)}, u32[]{:S(2)}) async-start(bf16[1024,1,2,128]{3,2,1,0:T(2,128)(2,1)} %bitcast.106), calls=%async_computation.6 | async-start | bytes 1048576 | tf_op jit(solution)/shard_map/all_to_all | solution.py:73
  577.2 33.3 %all-to-all-start.7 = ((bf16[1024,1,2,128]{3,2,1,0:T(2,128)(2,1)}), bf16[1024,1,2,128]{3,2,1,0:T(2,128)(2,1)S(1)}, u32[]{:S(2)}, u32[]{:S(2)}) async-start(bf16[1024,1,2,128]{3,2,1,0:T(2,128)(2,1)} %bitcast.105), calls=%async_computation.7 | async-start | bytes 1048576 | tf_op jit(solution)/shard_map/all_to_all | solution.py:74
where the time goes:
time: 613 us; the launch traced here: 612 us
  blocking collectives  287 us (47%)
  waiting for transfers between devices  172 us (28%)
  starting transfers between devices  96 us (16%)
  local copies, waits for them, and re-layouts  34.8 us (6%)
  matrix products  15.3 us (2%)
    all_gather x1, blocking collectives, local(): lax.all_gather(query_gain, 'dp', axis=0, tiled=True)  150 us
    all_gather x1, blocking collectives, local(): lax.all_gather(key_gain, 'dp', axis=0, tiled=True)  138 us
    all_to_all x1, starting transfers between devices, local(): lax.all_to_all(key_split, 'ctx', split_axis=1, concat_axis=0, tiled=True)  33 us
    all_to_all x1, waiting for transfers between devices, local(): lax.all_to_all(key_split, 'ctx', split_axis=1, concat_axis=0, tiled=True)  25.2 us
    all_to_all x1, waiting for transfers between devices, local(): lax.all_to_all(query_split, 'ctx', split_axis=1, concat_axis=0, tiled=True)  25.1 us
    all_to_all x1, waiting for transfers between devices, finish(): lax.all_to_all(output, 'ctx', split_axis=0, concat_axis=1, tiled=True)  24.8 us
    all_to_all x1, waiting for transfers between devices, local(): lax.all_to_all(key_dot_split, 'ctx', split_axis=1, concat_axis=0, tiled=T...  24.8 us
    all_to_all x1, waiting for transfers between devices, local(): lax.all_to_all(value_split, 'ctx', split_axis=1, concat_axis=0, tiled=True)  24.8 us
  transfers between devices with their start and end apart: 8, of which 7 were waited for; matrix products, arithmetic and copies ran while one was open for 2% of the time, Pallas kernels for 0%

commit v1 on v0

v1 whole, which is shorter than its diff:
```python
import jax
import jax.numpy as jnp
from jax import lax
from jax.experimental import pallas as pl
from jax.experimental.pallas import tpu as pltpu
from jax.sharding import PartitionSpec as P

HEAD_DIM = 128
CHIPS = 8
HEADS_PER_CHIP = 4
TOKENS = 64
FEATURES = HEADS_PER_CHIP * HEAD_DIM
STAT_ROWS = 16
ARRAYS = 6
ROWS = ARRAYS * HEADS_PER_CHIP * TOKENS + STAT_ROWS
LOG2E = 1.4426950408889634
VMEM = 56 * 1024 * 1024


def vmem_spec():
    return pl.BlockSpec(memory_space=pltpu.VMEM)


def smem_spec():
    return pl.BlockSpec(memory_space=pltpu.SMEM)


def params():
    return pltpu.CompilerParams(vmem_limit_bytes=VMEM)


def pack_kernel(chip_ref, *refs):
    ins, outs = refs[:ARRAYS], refs[ARRAYS:]
    chip = chip_ref[0]
    columns = []
    for values_ref, tangent_ref in ((ins[0], ins[1]), (ins[2], ins[3])):
        square = jnp.zeros((TOKENS, HEAD_DIM), jnp.float32)
        cross = jnp.zeros((TOKENS, HEAD_DIM), jnp.float32)
        width = values_ref.shape[1]
        for start in range(0, width, HEAD_DIM):
            values = values_ref[:, start : start + HEAD_DIM].astype(jnp.float32)
            tangent = tangent_ref[:, start : start + HEAD_DIM].astype(jnp.float32)
            square += values * values
            cross += values * tangent
        mean_square = jnp.sum(square, axis=1, keepdims=True) / width
        columns.append(lax.rsqrt(mean_square + 1e-06))
        columns.append(jnp.sum(cross, axis=1, keepdims=True) / width)
    lane = lax.broadcasted_iota(jnp.int32, (TOKENS, HEAD_DIM), 1)
    table = jnp.zeros((TOKENS, HEAD_DIM), jnp.float32)
    for index, column in enumerate(columns):
        rest = column
        for part in range(3):
            piece = rest.astype(jnp.bfloat16).astype(jnp.float32)
            rest = rest - piece
            table = jnp.where(lane == part * 4 + index, piece, table)
    table = jnp.concatenate([table, jnp.zeros((HEAD_DIM - TOKENS, HEAD_DIM), jnp.float32)], axis=0)
    stats = jnp.transpose(table)[:STAT_ROWS].astype(jnp.bfloat16)
    for step in range(CHIPS):
        target = jnp.bitwise_xor(chip, step)
        for array in range(ARRAYS):
            for head in range(HEADS_PER_CHIP):
                row = (array * HEADS_PER_CHIP + head) * TOKENS
                column = pl.multiple_of(target * FEATURES + head * HEAD_DIM, HEAD_DIM)
                outs[step][row : row + TOKENS, :] = ins[array][:, pl.ds(column, HEAD_DIM)]
        outs[step][ROWS - STAT_ROWS : ROWS, :] = stats


def norm_kernel(gain_ref, *refs):
    blocks, (query_ref, kv_ref) = refs[:CHIPS], refs[CHIPS:]
    for step in range(CHIPS):
        block = blocks[step]
        parts = block[ROWS - STAT_ROWS : ROWS, :].astype(jnp.float32)
        rows = parts[0:4] + (parts[4:8] + parts[8:12])
        rows = jnp.concatenate([rows, jnp.zeros((HEAD_DIM - 4, HEAD_DIM), jnp.float32)], axis=0)
        columns = jnp.transpose(rows)[:TOKENS]
        where = pl.ds(step * TOKENS, TOKENS)

        def rows_of(array, head, block=block):
            row = (array * HEADS_PER_CHIP + head) * TOKENS
            return block[row : row + TOKENS, :]

        for norm, target in ((0, query_ref), (1, kv_ref)):
            inverse = columns[:, 2 * norm : 2 * norm + 1]
            cross = columns[:, 2 * norm + 1 : 2 * norm + 2]
            cube = inverse * inverse * inverse
            for head in range(HEADS_PER_CHIP):
                gain = gain_ref[norm, head : head + 1, :].astype(jnp.float32)
                values = rows_of(2 * norm, head).astype(jnp.float32)
                tangent = rows_of(2 * norm + 1, head).astype(jnp.float32)
                normed = values * inverse * gain
                normed_tangent = (tangent * inverse - values * cube * cross) * gain
                target[0, head, where, :] = normed.astype(jnp.bfloat16)
                target[1, head, where, :] = normed_tangent.astype(jnp.bfloat16)
        for head in range(HEADS_PER_CHIP):
            kv_ref[2, head, where, :] = rows_of(4, head)
            kv_ref[3, head, where, :] = rows_of(5, head)


QUERY_BLOCK = 256
CONTRACT = (((1,), (1,)), ((), ()))


def attend_kernel(query_ref, own_ref, other_ref, *outs):
    factor = HEAD_DIM**-0.5

    def head_step(head, carry):
        def both(index):
            return jnp.concatenate([own_ref[index, head], other_ref[index, head]], axis=0)

        keys, keys_dot, values, values_dot = both(0), both(1), both(2), both(3)
        keys_pair = jnp.concatenate([keys, keys_dot], axis=1)
        values_pair = jnp.concatenate([values, values_dot], axis=1)
        total = query_ref.shape[2]
        for start in range(0, total, QUERY_BLOCK):
            queries = query_ref[0, head, start : start + QUERY_BLOCK, :]
            queries_dot = query_ref[1, head, start : start + QUERY_BLOCK, :]
            queries_pair = jnp.concatenate([queries_dot, queries], axis=1)
            scores = lax.dot_general(queries, keys, CONTRACT, preferred_element_type=jnp.float32)
            scores_dot = lax.dot_general(
                queries_pair, keys_pair, CONTRACT, preferred_element_type=jnp.float32
            )
            peak = jnp.max(scores, axis=1, keepdims=True)
            exponent = jnp.exp2((scores - peak) * (factor * LOG2E))
            scale = 1.0 / jnp.sum(exponent, axis=1, keepdims=True)
            weights = exponent * scale
            mean = jnp.sum(weights * scores_dot, axis=1, keepdims=True)
            weights_dot = (weights * factor) * (scores_dot - mean)
            probs = weights.astype(jnp.bfloat16)
            probs_dot = weights_dot.astype(jnp.bfloat16)
            pair = jnp.dot(probs, values_pair, preferred_element_type=jnp.float32)
            output_dot = jnp.dot(probs_dot, values, preferred_element_type=jnp.float32)
            output = pair[:, :HEAD_DIM].astype(jnp.bfloat16)
            output_dot = (output_dot + pair[:, HEAD_DIM:]).astype(jnp.bfloat16)
            for piece in range(QUERY_BLOCK // TOKENS):
                out = outs[start // TOKENS + piece]
                row = pl.multiple_of(head * TOKENS, TOKENS)
                rows = slice(piece * TOKENS, (piece + 1) * TOKENS)
                out[0, pl.ds(row, TOKENS), :] = output[rows]
                out[1, pl.ds(row, TOKENS), :] = output_dot[rows]
        return carry

    lax.fori_loop(0, HEADS_PER_CHIP, head_step, 0)


def unpack_kernel(chip_ref, *refs):
    blocks, outs = refs[:CHIPS], refs[CHIPS:]
    chip = chip_ref[0]
    for step in range(CHIPS):
        source = jnp.bitwise_xor(chip, step)
        for index in range(2):
            for head in range(HEADS_PER_CHIP):
                column = pl.multiple_of(source * FEATURES + head * HEAD_DIM, HEAD_DIM)
                rows = slice(head * TOKENS, (head + 1) * TOKENS)
                outs[index][:, pl.ds(column, HEAD_DIM)] = blocks[step][index, rows, :]


def exchange(block, step):
    pairs = [(place, place ^ (2 * step)) for place in range(2 * CHIPS)]
    return lax.ppermute(block, "ctx", pairs)


def swap(block):
    return lax.ppermute(block, "ctx", [(place, place ^ 1) for place in range(2 * CHIPS)])


def local(
    query_rows,
    key_rows,
    value_rows,
    query_tangent,
    key_tangent,
    value_tangent,
    query_gain,
    key_gain,
):
    rows, width = query_rows.shape[1:]
    chip = (lax.axis_index("ctx") // 2).astype(jnp.int32)
    chip_ref = chip.reshape(1)

    shards = lax.axis_size("dp")
    gains = jnp.stack([query_gain, key_gain])
    gains = jnp.broadcast_to(gains[None], (shards, *gains.shape))
    gains = lax.all_to_all(gains, "dp", 0, 0, tiled=True)
    gains = jnp.moveaxis(gains, 0, 1).reshape(2, width // HEAD_DIM, HEAD_DIM)
    gains = lax.dynamic_slice_in_dim(gains, chip * HEADS_PER_CHIP, HEADS_PER_CHIP, axis=1)

    blocks = pl.pallas_call(
        pack_kernel,
        out_shape=[jax.ShapeDtypeStruct((ROWS, HEAD_DIM), jnp.bfloat16)] * CHIPS,
        in_specs=[smem_spec()] + [vmem_spec()] * ARRAYS,
        out_specs=[vmem_spec()] * CHIPS,
        compiler_params=params(),
        name="pack",
    )(
        chip_ref,
        query_rows[0],
        query_tangent[0],
        key_rows[0],
        key_tangent[0],
        value_rows[0],
        value_tangent[0],
    )
    arrived = [blocks[0]] + [exchange(blocks[step], step) for step in range(1, CHIPS)]

    many = CHIPS * TOKENS
    queries, own = pl.pallas_call(
        norm_kernel,
        out_shape=[
            jax.ShapeDtypeStruct((2, HEADS_PER_CHIP, many, HEAD_DIM), jnp.bfloat16),
            jax.ShapeDtypeStruct((4, HEADS_PER_CHIP, many, HEAD_DIM), jnp.bfloat16),
        ],
        in_specs=[vmem_spec()] * (1 + CHIPS),
        out_specs=[vmem_spec()] * 2,
        compiler_params=params(),
        name="norm",
    )(gains, *arrived)
    other = swap(own)

    outs = pl.pallas_call(
        attend_kernel,
        out_shape=[
            jax.ShapeDtypeStruct((2, HEADS_PER_CHIP * TOKENS, HEAD_DIM), jnp.bfloat16)
        ] * CHIPS,
        in_specs=[vmem_spec()] * 3,
        out_specs=[vmem_spec()] * CHIPS,
        compiler_params=params(),
        name="attend",
    )(queries, own, other)
    back = [outs[0]] + [exchange(outs[step], step) for step in range(1, CHIPS)]

    attended, attended_tangent = pl.pallas_call(
        unpack_kernel,
        out_shape=[jax.ShapeDtypeStruct((rows, width), jnp.bfloat16)] * 2,
        in_specs=[smem_spec()] + [vmem_spec()] * CHIPS,
        out_specs=[vmem_spec()] * 2,
        compiler_params=params(),
        name="unpack",
    )(chip_ref, *back)
    return attended[None], attended_tangent[None]


def solution(mesh):
    rows = P("dp", "ctx", None)
    return jax.shard_map(
        local,
        mesh=mesh,
        in_specs=(rows,) * 6 + (P("dp"), P("dp")),
        out_specs=(rows, rows),
        check_vma=False,
    )
```

time: 613 us -> 248 us (0.40)
  the two profiles are of different devices: /device:TPU:1 before, /device:TPU:96 now
where the time goes in v1:
time: 248 us
  waiting for transfers between devices  143 us (58%)
  starting transfers between devices  77.4 us (31%)
  Pallas kernels  22.2 us (9%)
  local copies, waits for them, and re-layouts  3.93 us (2%)
    ppermute x14, waiting for transfers between devices, exchange(): return lax.ppermute(block, 'ctx', pairs)  122 us
    ppermute x14, starting transfers between devices, exchange(): return lax.ppermute(block, 'ctx', pairs)  61.1 us
    all_to_all x1, waiting for transfers between devices, local(): gains = lax.all_to_all(gains, 'dp', 0, 0, tiled=True)  16.9 us
    all_to_all x1, starting transfers between devices, local(): gains = lax.all_to_all(gains, 'dp', 0, 0, tiled=True)  14.5 us
    pallas_call x1, Pallas kernels, local(): pl.pallas_call(attend_kernel, out_shape=[jax.ShapeDtypeStruct((2, HEADS_P...  11.1 us
  transfers between devices with their start and end apart: 16, of which 10 were waited for; matrix products, arithmetic and copies ran while one was open for 0% of the time, Pallas kernels for 0%

profile of v1, /device:TPU:96, one launch (start us, length us, event | category | flops | bytes accessed | tf_op | source)
XLA Modules:
  0.0 247.7 jit_solution(1362021065173849516)
XLA Ops:
  0.7 4.4 %pack.1 = (bf16[1552,128]{1,0:T(8,128)(2,1)}, bf16[1552,128]{1,0:T(8,128)(2,1)}, bf16[1552,128]{1,0:T(8,128)(2,1)}, bf16[1552,128]{1,0:T(8,128)(2,1)}, bf16[1552...) custom-call(s32[1]{0:T(128)} %bitcast.chip_ref, ...), custom_call_target="tpu_custom_call" | custom-call | tf_op jit(solution)/shard_map/pack/pallas_call | solution.py:187
  5.0 2.0 collective-permute-start
  7.0 6.9 %collective-permute-start.1 = (bf16[1552,128]{1,0:T(8,128)(2,1)}, bf16[1552,128]{1,0:T(8,128)(2,1)S(1)}, u32[]{:S(2)}, u32[]{:S(2)}) collective-permute-start(bf16[1552,128]{1,0:T(8,128)(2,1)} %get-tuple-element.24), channel_id=1, source_target_pairs={{0,4},{1,5},{2,6},{3,7},{4,0},{5,1},{6,2},{7,3},{8,12},{9,13},{10,... | collective-permute-start | bytes 1191944 | tf_op jit(solution)/shard_map/ppermute | solution.py:159
  14.0 1.9 collective-permute-start.2
  15.9 8.3 %collective-permute-start.3 = (bf16[1552,128]{1,0:T(8,128)(2,1)}, bf16[1552,128]{1,0:T(8,128)(2,1)S(1)}, u32[]{:S(2)}, u32[]{:S(2)}) collective-permute-start(bf16[1552,128]{1,0:T(8,128)(2,1)} %get-tuple-element.26), channel_id=1, source_target_pairs={{0,8},{1,9},{2,10},{3,11},{4,12},{5,13},{6,14},{7,15},{8,0},{9,1},... | collective-permute-start | bytes 1191944 | tf_op jit(solution)/shard_map/ppermute | solution.py:159
  24.3 1.9 collective-permute-start.4
  26.2 5.5 %collective-permute-start.5 = (bf16[1552,128]{1,0:T(8,128)(2,1)}, bf16[1552,128]{1,0:T(8,128)(2,1)S(1)}, u32[]{:S(2)}, u32[]{:S(2)}) collective-permute-start(bf16[1552,128]{1,0:T(8,128)(2,1)} %get-tuple-element.28), channel_id=1, source_target_pairs={{0,12},{1,13},{2,14},{3,15},{4,8},{5,9},{6,10},{7,11},{8,4},{9,5},... | collective-permute-start | bytes 1191944 | tf_op jit(solution)/shard_map/ppermute | solution.py:159
  31.7 42.7 %collective-permute-done.1.refs_2_ = bf16[1552,128]{1,0:T(8,128)(2,1)S(1)} collective-permute-done((bf16[1552,128]{1,0:T(8,128)(2,1)}, bf16[1552,128]{1,0:T(8,128)(2,1)S(1)}, u32[]{:S(2)}, u32[]{:S(2)}) %collective-permute-start.1) | collective-permute-done | bytes 397344 | tf_op jit(solution)/shard_map/ppermute | solution.py:159
  74.4 6.3 %collective-permute-start.6 = (bf16[1552,128]{1,0:T(8,128)(2,1)}, bf16[1552,128]{1,0:T(8,128)(2,1)S(1)}, u32[]{:S(2)}, u32[]{:S(2)}) collective-permute-start(bf16[1552,128]{1,0:T(8,128)(2,1)} %get-tuple-element.29), channel_id=1, source_target_pairs={{0,14},{1,15},{2,12},{3,13},{4,10},{5,11},{6,8},{7,9},{8,6},{9,7},... | collective-permute-start | bytes 1191944 | tf_op jit(solution)/shard_map/ppermute | solution.py:159
  81.3 14.5 %all-to-all-start = ((bf16[32,2,128]{2,1,0:T(2,128)(2,1)}), bf16[32,2,128]{2,1,0:T(2,128)(2,1)S(1)}, u32[]{:S(2)}, u32[]{:S(2)}) async-start(bf16[32,2,128]{2,1,0:T(2,128)(2,1)} %broadcast_in_dim.12), calls=%async_computation | async-start | bytes 32768 | tf_op jit(solution)/shard_map/all_to_all | solution.py:183
  95.8 16.9 %all-to-all-done = bf16[32,2,128]{2,1,0:T(2,128)(2,1)S(1)} async-done(((bf16[32,2,128]{2,1,0:T(2,128)(2,1)}), bf16[32,2,128]{2,1,0:T(2,128)(2,1)S(1)}, u32[]{:S(2)}, u32[]{:S(2)}) %all-to-all-start) | async-done | bytes 16416 | tf_op jit(solution)/shard_map/all_to_all | solution.py:183
  113.3 31.3 %collective-permute-done.4.refs_5_ = bf16[1552,128]{1,0:T(8,128)(2,1)S(1)} collective-permute-done((bf16[1552,128]{1,0:T(8,128)(2,1)}, bf16[1552,128]{1,0:T(8,128)(2,1)S(1)}, u32[]{:S(2)}, u32[]{:S(2)}) %collective-permute-start.4) | collective-permute-done | bytes 397344 | tf_op jit(solution)/shard_map/ppermute | solution.py:159
  144.6 8.5 %collective-permute-done.5.refs_6_ = bf16[1552,128]{1,0:T(8,128)(2,1)S(1)} collective-permute-done((bf16[1552,128]{1,0:T(8,128)(2,1)}, bf16[1552,128]{1,0:T(8,128)(2,1)S(1)}, u32[]{:S(2)}, u32[]{:S(2)}) %collective-permute-start.5) | collective-permute-done | bytes 397344 | tf_op jit(solution)/shard_map/ppermute | solution.py:159
  153.1 7.3 %collective-permute-done.6.refs_7_ = bf16[1552,128]{1,0:T(8,128)(2,1)S(1)} collective-permute-done((bf16[1552,128]{1,0:T(8,128)(2,1)}, bf16[1552,128]{1,0:T(8,128)(2,1)S(1)}, u32[]{:S(2)}, u32[]{:S(2)}) %collective-permute-start.6) | collective-permute-done | bytes 397344 | tf_op jit(solution)/shard_map/ppermute | solution.py:159
  160.5 0.7 copy-done.7
  161.2 4.2 %norm.1 = (bf16[2,4,512,128]{3,2,1,0:T(8,128)(2,1)}, bf16[4,4,512,128]{3,2,1,0:T(8,128)(2,1)}) custom-call(bf16[2,4,128]{2,1,0:T(4,128)(2,1)} %bitcast.20, bf16[1552,128]{1,0:T(8,128)(2,1)} %get-tuple-element.22.refs_0_, bf16[1552,128]{1,0:T(8,128)(2,1)} %copy-done.1, bf16[1552,128]{1,0:T(8,128)(2,1)} %copy-done.2, bf16[1552,128]{1,0:T(8,128)(2,1)} %copy-done.3, ...), custom_call_target="tpu_custom_call" | custom-call | tf_op jit(solution)/shard_map/norm/pallas_call | solution.py:206
  165.5 1.9 collective-permute-start.7
  167.4 4.3 %collective-permute-done.7.other_ref = bf16[4,4,512,128]{3,2,1,0:T(8,128)(2,1)S(1)} collective-permute-done((bf16[4,4,512,128]{3,2,1,0:T(8,128)(2,1)}, bf16[4,4,512,128]{3,2,1,0:T(8,128)(2,1)S(1)}, u32[]{:S(2)}, u32[]{:S(2)}) %collective-permute-start.7) | collective-permute-done | bytes 2097184 | tf_op jit(solution)/shard_map/ppermute | solution.py:163
  171.7 1.3 copy-done
  173.0 11.1 %attend.1 = (bf16[2,256,128]{2,1,0:T(8,128)(2,1)}, bf16[2,256,128]{2,1,0:T(8,128)(2,1)}, bf16[2,256,128]{2,1,0:T(8,128)(2,1)}, bf16[2,256,128]{2,1,0:T(8,128)(2,...) custom-call(bf16[2,4,512,128]{3,2,1,0:T(8,128)(2,1)} %get-tuple-elem, ...), custom_call_target="tpu_custom_call" | custom-call | tf_op jit(solution)/shard_map/attend/pallas_call | solution.py:219
  184.1 1.9 collective-permute-start.8
  186.0 1.9 collective-permute-start.9
  187.9 6.3 %collective-permute-start.10 = (bf16[2,256,128]{2,1,0:T(8,128)(2,1)}, bf16[2,256,128]{2,1,0:T(8,128)(2,1)S(1)}, u32[]{:S(2)}, u32[]{:S(2)}) collective-permute-start(bf16[2,256,128]{2,1,0:T(8,128)(2,1)} %get-tuple-element.35), channel_id=1, source_target_pairs={{0,6},{1,7},{2,4},{3,5},{4,2},{5,3},{6,0},{7,1},{8,14},{9,15},{10,... | collective-permute-start | bytes 393224 | tf_op jit(solution)/shard_map/ppermute | solution.py:159
  194.2 4.9 %collective-permute-start.11 = (bf16[2,256,128]{2,1,0:T(8,128)(2,1)}, bf16[2,256,128]{2,1,0:T(8,128)(2,1)S(1)}, u32[]{:S(2)}, u32[]{:S(2)}) collective-permute-start(bf16[2,256,128]{2,1,0:T(8,128)(2,1)} %get-tuple-element.36), channel_id=1, source_target_pairs={{0,8},{1,9},{2,10},{3,11},{4,12},{5,13},{6,14},{7,15},{8,0},{9,1},... | collective-permute-start | bytes 393224 | tf_op jit(solution)/shard_map/ppermute | solution.py:159
  199.2 2.5 collective-permute-start.12
  201.7 8.7 %collective-permute-start.13 = (bf16[2,256,128]{2,1,0:T(8,128)(2,1)}, bf16[2,256,128]{2,1,0:T(8,128)(2,1)S(1)}, u32[]{:S(2)}, u32[]{:S(2)}) collective-permute-start(bf16[2,256,128]{2,1,0:T(8,128)(2,1)} %get-tuple-element.38), channel_id=1, source_target_pairs={{0,12},{1,13},{2,14},{3,15},{4,8},{5,9},{6,10},{7,11},{8,4},{9,5},... | collective-permute-start | bytes 393224 | tf_op jit(solution)/shard_map/ppermute | solution.py:159
  210.4 1.9 collective-permute-start.14
  212.4 23.9 %collective-permute-done.11.refs_4_ = bf16[2,256,128]{2,1,0:T(8,128)(2,1)S(1)} collective-permute-done((bf16[2,256,128]{2,1,0:T(8,128)(2,1)}, bf16[2,256,128]{2,1,0:T(8,128)(2,1)S(1)}, u32[]{:S(2)}, u32[]{:S(2)}) %collective-permute-start.11) | collective-permute-done | bytes 131104 | tf_op jit(solution)/shard_map/ppermute | solution.py:159
  236.3 2.8 %collective-permute-done.12.refs_5_ = bf16[2,256,128]{2,1,0:T(8,128)(2,1)S(1)} collective-permute-done((bf16[2,256,128]{2,1,0:T(8,128)(2,1)}, bf16[2,256,128]{2,1,0:T(8,128)(2,1)S(1)}, u32[]{:S(2)}, u32[]{:S(2)}) %collective-permute-start.12) | collective-permute-done | bytes 131104 | tf_op jit(solution)/shard_map/ppermute | solution.py:159
  239.1 2.8 %collective-permute-done.13.refs_6_ = bf16[2,256,128]{2,1,0:T(8,128)(2,1)S(1)} collective-permute-done((bf16[2,256,128]{2,1,0:T(8,128)(2,1)}, bf16[2,256,128]{2,1,0:T(8,128)(2,1)S(1)}, u32[]{:S(2)}, u32[]{:S(2)}) %collective-permute-start.13) | collective-permute-done | bytes 131104 | tf_op jit(solution)/shard_map/ppermute | solution.py:159
  241.9 2.7 %collective-permute-done.14.refs_7_ = bf16[2,256,128]{2,1,0:T(8,128)(2,1)S(1)} collective-permute-done((bf16[2,256,128]{2,1,0:T(8,128)(2,1)}, bf16[2,256,128]{2,1,0:T(8,128)(2,1)S(1)}, u32[]{:S(2)}, u32[]{:S(2)}) %collective-permute-start.14) | collective-permute-done | bytes 131104 | tf_op jit(solution)/shard_map/ppermute | solution.py:159
  245.2 2.5 %unpack.1 = (bf16[64,4096]{1,0:T(8,128)(2,1)}, bf16[64,4096]{1,0:T(8,128)(2,1)}) custom-call(s32[1]{0:T(128)} %bitcast.chip_ref, bf16[2,256,128]{2,1,0:T(8,128)(2,1)} %get-tuple-element.32.refs_0_, bf16[2,256,128]{2,1,0:T(8,128)(2,1)} %copy-done.8, bf16[2,256,128]{2,1,0:T(8,128)(2,1)} %copy-done.9, bf16[2,256,128]{2,1,0:T(8,128)(2,1)} %copy-done.10, ...), custom_call_target="tpu_custom_call" | custom-call | tf_op jit(solution)/shard_map/unpack/pallas_call | solution.py:231
  (42 shorter events, 1.9 us)
Async XLA Ops:
  0.6 80.1 %copy-start.15 = (bf16[128]{0:T(256)(128)(2,1)S(1)}, bf16[128]{0:T(256)(128)(2,1)}, u32[]{:S(2)}) copy-start(bf16[128]{0:T(256)(128)(2,1)} %param.15) | copy-start | bytes 772
  0.6 80.1 %copy-start.16 = (bf16[128]{0:T(256)(128)(2,1)S(1)}, bf16[128]{0:T(256)(128)(2,1)}, u32[]{:S(2)}) copy-start(bf16[128]{0:T(256)(128)(2,1)} %param.14) | copy-start | bytes 772
  5.0 21.2 %collective-permute-start = (bf16[1552,128]{1,0:T(8,128)(2,1)}, bf16[1552,128]{1,0:T(8,128)(2,1)S(1)}, u32[]{:S(2)}, u32[]{:S(2)}) collective-permute-start(bf16[1552,128]{1,0:T(8,128)(2,1)} %get-tuple-element.23), channel_id=1, source_target_pairs={{0,2},{1,3},{2,0},{3,1},{4,6},{5,7},{6,4},{7,5},{8,10},{9,11},{10,... | collective-permute-start | bytes 1191944 | tf_op jit(solution)/shard_map/ppermute | solution.py:159
  7.0 67.3 %collective-permute-start.1 = (bf16[1552,128]{1,0:T(8,128)(2,1)}, bf16[1552,128]{1,0:T(8,128)(2,1)S(1)}, u32[]{:S(2)}, u32[]{:S(2)}) collective-permute-start(bf16[1552,128]{1,0:T(8,128)(2,1)} %get-tuple-element.24), channel_id=1, source_target_pairs={{0,4},{1,5},{2,6},{3,7},{4,0},{5,1},{6,2},{7,3},{8,12},{9,13},{10,... | collective-permute-start | bytes 1191944 | tf_op jit(solution)/shard_map/ppermute | solution.py:159
  14.0 99.3 %collective-permute-start.2 = (bf16[1552,128]{1,0:T(8,128)(2,1)}, bf16[1552,128]{1,0:T(8,128)(2,1)S(1)}, u32[]{:S(2)}, u32[]{:S(2)}) collective-permute-start(bf16[1552,128]{1,0:T(8,128)(2,1)} %get-tuple-element.25), channel_id=1, source_target_pairs={{0,6},{1,7},{2,4},{3,5},{4,2},{5,3},{6,0},{7,1},{8,14},{9,15},{10,... | collective-permute-start | bytes 1191944 | tf_op jit(solution)/shard_map/ppermute | solution.py:159
  15.9 97.4 %collective-permute-start.3 = (bf16[1552,128]{1,0:T(8,128)(2,1)}, bf16[1552,128]{1,0:T(8,128)(2,1)S(1)}, u32[]{:S(2)}, u32[]{:S(2)}) collective-permute-start(bf16[1552,128]{1,0:T(8,128)(2,1)} %get-tuple-element.26), channel_id=1, source_target_pairs={{0,8},{1,9},{2,10},{3,11},{4,12},{5,13},{6,14},{7,15},{8,0},{9,1},... | collective-permute-start | bytes 1191944 | tf_op jit(solution)/shard_map/ppermute | solution.py:159
  24.3 120.4 %collective-permute-start.4 = (bf16[1552,128]{1,0:T(8,128)(2,1)}, bf16[1552,128]{1,0:T(8,128)(2,1)S(1)}, u32[]{:S(2)}, u32[]{:S(2)}) collective-permute-start(bf16[1552,128]{1,0:T(8,128)(2,1)} %get-tuple-element.27), channel_id=1, source_target_pairs={{0,10},{1,11},{2,8},{3,9},{4,14},{5,15},{6,12},{7,13},{8,2},{9,3},... | collective-permute-start | bytes 1191944 | tf_op jit(solution)/shard_map/ppermute | solution.py:159
  26.2 134.3 %copy-start.1 = (bf16[1552,128]{1,0:T(8,128)(2,1)}, bf16[1552,128]{1,0:T(8,128)(2,1)S(1)}, u32[]{:S(2)}) copy-start(bf16[1552,128]{1,0:T(8,128)(2,1)S(1)} %collective-permute-done.refs_1_) | copy-start | bytes 1191940
  26.2 126.9 %collective-permute-start.5 = (bf16[1552,128]{1,0:T(8,128)(2,1)}, bf16[1552,128]{1,0:T(8,128)(2,1)S(1)}, u32[]{:S(2)}, u32[]{:S(2)}) collective-permute-start(bf16[1552,128]{1,0:T(8,128)(2,1)} %get-tuple-element.28), channel_id=1, source_target_pairs={{0,12},{1,13},{2,14},{3,15},{4,8},{5,9},{6,10},{7,11},{8,4},{9,5},... | collective-permute-start | bytes 1191944 | tf_op jit(solution)/shard_map/ppermute | solution.py:159
  74.4 86.1 %copy-start.2 = (bf16[1552,128]{1,0:T(8,128)(2,1)}, bf16[1552,128]{1,0:T(8,128)(2,1)S(1)}, u32[]{:S(2)}) copy-start(bf16[1552,128]{1,0:T(8,128)(2,1)S(1)} %collective-permute-done.1.refs_2_) | copy-start | bytes 1191940
  74.4 86.1 %collective-permute-start.6 = (bf16[1552,128]{1,0:T(8,128)(2,1)}, bf16[1552,128]{1,0:T(8,128)(2,1)S(1)}, u32[]{:S(2)}, u32[]{:S(2)}) collective-permute-start(bf16[1552,128]{1,0:T(8,128)(2,1)} %get-tuple-element.29), channel_id=1, source_target_pairs={{0,14},{1,15},{2,12},{3,13},{4,10},{5,11},{6,8},{7,9},{8,6},{9,7},... | collective-permute-start | bytes 1191944 | tf_op jit(solution)/shard_map/ppermute | solution.py:159
  81.3 31.4 %all-to-all-start = ((bf16[32,2,128]{2,1,0:T(2,128)(2,1)}), bf16[32,2,128]{2,1,0:T(2,128)(2,1)S(1)}, u32[]{:S(2)}, u32[]{:S(2)}) async-start(bf16[32,2,128]{2,1,0:T(2,128)(2,1)} %broadcast_in_dim.12), calls=%async_computation | async-start | bytes 32768 | tf_op jit(solution)/shard_map/all_to_all | solution.py:183
  113.3 47.2 %copy-start.3 = (bf16[1552,128]{1,0:T(8,128)(2,1)}, bf16[1552,128]{1,0:T(8,128)(2,1)S(1)}, u32[]{:S(2)}) copy-start(bf16[1552,128]{1,0:T(8,128)(2,1)S(1)} %collective-permute-done.2.refs_3_) | copy-start | bytes 1191940
  113.3 47.2 %copy-start.4 = (bf16[1552,128]{1,0:T(8,128)(2,1)}, bf16[1552,128]{1,0:T(8,128)(2,1)S(1)}, u32[]{:S(2)}) copy-start(bf16[1552,128]{1,0:T(8,128)(2,1)S(1)} %collective-permute-done.3.refs_4_) | copy-start | bytes 1191940
  144.6 15.9 %copy-start.5 = (bf16[1552,128]{1,0:T(8,128)(2,1)}, bf16[1552,128]{1,0:T(8,128)(2,1)S(1)}, u32[]{:S(2)}) copy-start(bf16[1552,128]{1,0:T(8,128)(2,1)S(1)} %collective-permute-done.4.refs_5_) | copy-start | bytes 1191940
  153.1 7.4 %copy-start.6 = (bf16[1552,128]{1,0:T(8,128)(2,1)}, bf16[1552,128]{1,0:T(8,128)(2,1)S(1)}, u32[]{:S(2)}) copy-start(bf16[1552,128]{1,0:T(8,128)(2,1)S(1)} %collective-permute-done.5.refs_6_) | copy-start | bytes 1191940
  160.5 0.8 copy-start.7
  165.5 6.3 %collective-permute-start.7 = (bf16[4,4,512,128]{3,2,1,0:T(8,128)(2,1)}, bf16[4,4,512,128]{3,2,1,0:T(8,128)(2,1)S(1)}, u32[]{:S(2)}, u32[]{:S(2)}) collective-permute-start(bf16[4,4,512,128]{3,2,1,0:T(8,128)(2,1)} %get-tuple-element.31.own_ref), channel_id=1, source_target_pairs={{0,1},{1,0},{2,3},{3,2},{4,5},{5,4},{6,7},{7,6},{8,9},{9,8},{10,11... | collective-permute-start | bytes 6291464 | tf_op jit(solution)/shard_map/ppermute | solution.py:163
  171.7 1.3 copy-start
  184.1 17.5 %collective-permute-start.8 = (bf16[2,256,128]{2,1,0:T(8,128)(2,1)}, bf16[2,256,128]{2,1,0:T(8,128)(2,1)S(1)}, u32[]{:S(2)}, u32[]{:S(2)}) collective-permute-start(bf16[2,256,128]{2,1,0:T(8,128)(2,1)} %get-tuple-element.33), channel_id=1, source_target_pairs={{0,2},{1,3},{2,0},{3,1},{4,6},{5,7},{6,4},{7,5},{8,10},{9,11},{10,... | collective-permute-start | bytes 393224 | tf_op jit(solution)/shard_map/ppermute | solution.py:159
  186.0 24.4 %collective-permute-start.9 = (bf16[2,256,128]{2,1,0:T(8,128)(2,1)}, bf16[2,256,128]{2,1,0:T(8,128)(2,1)S(1)}, u32[]{:S(2)}, u32[]{:S(2)}) collective-permute-start(bf16[2,256,128]{2,1,0:T(8,128)(2,1)} %get-tuple-element.34), channel_id=1, source_target_pairs={{0,4},{1,5},{2,6},{3,7},{4,0},{5,1},{6,2},{7,3},{8,12},{9,13},{10,... | collective-permute-start | bytes 393224 | tf_op jit(solution)/shard_map/ppermute | solution.py:159
  187.9 24.4 %collective-permute-start.10 = (bf16[2,256,128]{2,1,0:T(8,128)(2,1)}, bf16[2,256,128]{2,1,0:T(8,128)(2,1)S(1)}, u32[]{:S(2)}, u32[]{:S(2)}) collective-permute-start(bf16[2,256,128]{2,1,0:T(8,128)(2,1)} %get-tuple-element.35), channel_id=1, source_target_pairs={{0,6},{1,7},{2,4},{3,5},{4,2},{5,3},{6,0},{7,1},{8,14},{9,15},{10,... | collective-permute-start | bytes 393224 | tf_op jit(solution)/shard_map/ppermute | solution.py:159
  194.2 42.1 %collective-permute-start.11 = (bf16[2,256,128]{2,1,0:T(8,128)(2,1)}, bf16[2,256,128]{2,1,0:T(8,128)(2,1)S(1)}, u32[]{:S(2)}, u32[]{:S(2)}) collective-permute-start(bf16[2,256,128]{2,1,0:T(8,128)(2,1)} %get-tuple-element.36), channel_id=1, source_target_pairs={{0,8},{1,9},{2,10},{3,11},{4,12},{5,13},{6,14},{7,15},{8,0},{9,1},... | collective-permute-start | bytes 393224 | tf_op jit(solution)/shard_map/ppermute | solution.py:159
  199.2 39.9 %collective-permute-start.12 = (bf16[2,256,128]{2,1,0:T(8,128)(2,1)}, bf16[2,256,128]{2,1,0:T(8,128)(2,1)S(1)}, u32[]{:S(2)}, u32[]{:S(2)}) collective-permute-start(bf16[2,256,128]{2,1,0:T(8,128)(2,1)} %get-tuple-element.37), channel_id=1, source_target_pairs={{0,10},{1,11},{2,8},{3,9},{4,14},{5,15},{6,12},{7,13},{8,2},{9,3},... | collective-permute-start | bytes 393224 | tf_op jit(solution)/shard_map/ppermute | solution.py:159
  201.7 42.9 %copy-start.8 = (bf16[2,256,128]{2,1,0:T(8,128)(2,1)}, bf16[2,256,128]{2,1,0:T(8,128)(2,1)S(1)}, u32[]{:S(2)}) copy-start(bf16[2,256,128]{2,1,0:T(8,128)(2,1)S(1)} %collective-permute-done.8.refs_1_) | copy-start | bytes 393220
  201.7 40.2 %collective-permute-start.13 = (bf16[2,256,128]{2,1,0:T(8,128)(2,1)}, bf16[2,256,128]{2,1,0:T(8,128)(2,1)S(1)}, u32[]{:S(2)}, u32[]{:S(2)}) collective-permute-start(bf16[2,256,128]{2,1,0:T(8,128)(2,1)} %get-tuple-element.38), channel_id=1, source_target_pairs={{0,12},{1,13},{2,14},{3,15},{4,8},{5,9},{6,10},{7,11},{8,4},{9,5},... | collective-permute-start | bytes 393224 | tf_op jit(solution)/shard_map/ppermute | solution.py:159
  210.4 34.2 %copy-start.9 = (bf16[2,256,128]{2,1,0:T(8,128)(2,1)}, bf16[2,256,128]{2,1,0:T(8,128)(2,1)S(1)}, u32[]{:S(2)}) copy-start(bf16[2,256,128]{2,1,0:T(8,128)(2,1)S(1)} %collective-permute-done.9.refs_2_) | copy-start | bytes 393220
  210.4 34.2 %collective-permute-start.14 = (bf16[2,256,128]{2,1,0:T(8,128)(2,1)}, bf16[2,256,128]{2,1,0:T(8,128)(2,1)S(1)}, u32[]{:S(2)}, u32[]{:S(2)}) collective-permute-start(bf16[2,256,128]{2,1,0:T(8,128)(2,1)} %get-tuple-element.39), channel_id=1, source_target_pairs={{0,14},{1,15},{2,12},{3,13},{4,10},{5,11},{6,8},{7,9},{8,6},{9,7},... | collective-permute-start | bytes 393224 | tf_op jit(solution)/shard_map/ppermute | solution.py:159
  212.4 32.2 %copy-start.10 = (bf16[2,256,128]{2,1,0:T(8,128)(2,1)}, bf16[2,256,128]{2,1,0:T(8,128)(2,1)S(1)}, u32[]{:S(2)}) copy-start(bf16[2,256,128]{2,1,0:T(8,128)(2,1)S(1)} %collective-permute-done.10.refs_3_) | copy-start | bytes 393220
  236.3 8.3 %copy-start.11 = (bf16[2,256,128]{2,1,0:T(8,128)(2,1)}, bf16[2,256,128]{2,1,0:T(8,128)(2,1)S(1)}, u32[]{:S(2)}) copy-start(bf16[2,256,128]{2,1,0:T(8,128)(2,1)S(1)} %collective-permute-done.11.refs_4_) | copy-start | bytes 393220
  239.1 5.5 %copy-start.12 = (bf16[2,256,128]{2,1,0:T(8,128)(2,1)}, bf16[2,256,128]{2,1,0:T(8,128)(2,1)S(1)}, u32[]{:S(2)}) copy-start(bf16[2,256,128]{2,1,0:T(8,128)(2,1)S(1)} %collective-permute-done.12.refs_5_) | copy-start | bytes 393220
  241.9 2.7 %copy-start.13 = (bf16[2,256,128]{2,1,0:T(8,128)(2,1)}, bf16[2,256,128]{2,1,0:T(8,128)(2,1)S(1)}, u32[]{:S(2)}) copy-start(bf16[2,256,128]{2,1,0:T(8,128)(2,1)S(1)} %collective-permute-done.13.refs_6_) | copy-start | bytes 393220
  (1 other events, 0.7 us)

commit v2 on v1

v2 whole, which is shorter than its diff:
```python
import functools

import jax
import jax.numpy as jnp
from jax import lax
from jax.experimental import pallas as pl
from jax.experimental.pallas import tpu as pltpu
from jax.sharding import PartitionSpec as P

HEAD_DIM = 128
CHIPS = 8
HEADS_PER_CHIP = 4
TOKENS = 64
FEATURES = HEADS_PER_CHIP * HEAD_DIM
BLOCK = HEADS_PER_CHIP * TOKENS
STAT_ROWS = 16
ARRAYS = 6
STEPS = (4, 1, 5, 2, 3, 6, 7, 0)
LATE = (5, 6)
EARLY = (0, 1, 2, 3, 4, 7)
ORDER = (0, 2, 5, 6, 1, 3, 4, 7)
PACK_MIB = 56
LOG2E = 1.4426950408889634
MIB = 1024 * 1024


def vmem(count):
    return [pl.BlockSpec(memory_space=pltpu.VMEM)] * count


def smem():
    return [pl.BlockSpec(memory_space=pltpu.SMEM)]


def params(mib):
    return pltpu.CompilerParams(vmem_limit_bytes=mib * MIB)


def shape(*sizes, dtype=jnp.bfloat16):
    return jax.ShapeDtypeStruct(sizes, dtype)


def statistics(pairs):
    columns = []
    for values_ref, tangent_ref in pairs:
        square = jnp.zeros((TOKENS, HEAD_DIM), jnp.float32)
        cross = jnp.zeros((TOKENS, HEAD_DIM), jnp.float32)
        width = values_ref.shape[1]
        for start in range(0, width, HEAD_DIM):
            values = values_ref[:, start : start + HEAD_DIM].astype(jnp.float32)
            tangent = tangent_ref[:, start : start + HEAD_DIM].astype(jnp.float32)
            square += values * values
            cross += values * tangent
        mean_square = jnp.sum(square, axis=1, keepdims=True) / width
        columns.append(lax.rsqrt(mean_square + 1e-06))
        columns.append(jnp.sum(cross, axis=1, keepdims=True) / width)
    lane = lax.broadcasted_iota(jnp.int32, (TOKENS, HEAD_DIM), 1)
    table = jnp.zeros((TOKENS, HEAD_DIM), jnp.float32)
    for index, column in enumerate(columns):
        rest = column
        for part in range(3):
            piece = rest.astype(jnp.bfloat16).astype(jnp.float32)
            rest = rest - piece
            table = jnp.where(lane == part * 4 + index, piece, table)
    table = jnp.concatenate([table, jnp.zeros((HEAD_DIM - TOKENS, HEAD_DIM), jnp.float32)], axis=0)
    return jnp.transpose(table)[:STAT_ROWS].astype(jnp.bfloat16)


def table_of(stats):
    parts = stats.astype(jnp.float32)
    rows = parts[0:4] + (parts[4:8] + parts[8:12])
    rows = jnp.concatenate([rows, jnp.zeros((HEAD_DIM - 4, HEAD_DIM), jnp.float32)], axis=0)
    return jnp.transpose(rows)[:TOKENS]


def normed(values, tangent, columns, which, gain):
    inverse = columns[:, 2 * which : 2 * which + 1]
    cross = columns[:, 2 * which + 1 : 2 * which + 2]
    cube = inverse * inverse * inverse
    values = values.astype(jnp.float32)
    tangent = tangent.astype(jnp.float32)
    gain = gain.astype(jnp.float32)
    rows = (values * inverse * gain).astype(jnp.bfloat16)
    return rows, ((tangent * inverse - values * cube * cross) * gain).astype(jnp.bfloat16)


def copy_columns(chip, arrays, out, place):
    target = jnp.bitwise_xor(chip, STEPS[place])
    for index, array in enumerate(arrays):
        for head in range(HEADS_PER_CHIP):
            column = pl.multiple_of(target * FEATURES + head * HEAD_DIM, HEAD_DIM)
            row = index * BLOCK + head * TOKENS
            out[row : row + TOKENS, :] = array[:, pl.ds(column, HEAD_DIM)]


def pack_kernel(chip_ref, *refs):
    arrays, outs, late = refs[:ARRAYS], refs[ARRAYS : ARRAYS + CHIPS], refs[ARRAYS + CHIPS :]
    stats = statistics((arrays[4:], arrays[:2]))
    for place, out in enumerate(outs):
        kept = arrays[:4] if place in LATE else arrays
        copy_columns(chip_ref[0], kept, out, place)
        out[len(kept) * BLOCK :, :] = stats
    for place, out in zip(LATE, late):
        copy_columns(chip_ref[0], arrays[4:], out, place)


def norm_kernel(gain_ref, *refs):
    blocks, (kv_ref, table_ref) = refs[:CHIPS], refs[CHIPS:]
    for place, block in enumerate(blocks):
        where = pl.ds(place * TOKENS, TOKENS)
        columns = table_of(block[block.shape[0] - STAT_ROWS :, :])
        table_ref[where, :] = columns
        for head in range(HEADS_PER_CHIP):
            rows = [block[i * BLOCK + head * TOKENS :][:TOKENS] for i in range(4)]
            rows[:2] = normed(rows[0], rows[1], columns, 1, gain_ref[1, head : head + 1, :])
            for index in range(4):
                kv_ref[index, head, where, :] = rows[index]


CONTRACT = (((1,), (1,)), ((), ()))


def attend_kernel(places, gain_ref, table_ref, own_ref, other_ref, *refs):
    blocks, outs = refs[: len(places)], refs[len(places) :]
    factor = HEAD_DIM**-0.5
    for head in range(HEADS_PER_CHIP):

        def both(index, head=head):
            return jnp.concatenate([own_ref[index, head], other_ref[index, head]], axis=0)

        keys, keys_dot, values, values_dot = both(0), both(1), both(2), both(3)
        keys_pair = jnp.concatenate([keys, keys_dot], axis=1)
        values_pair = jnp.concatenate([values, values_dot], axis=1)
        token = slice(head * TOKENS, (head + 1) * TOKENS)
        tangent_token = slice(BLOCK + head * TOKENS, BLOCK + (head + 1) * TOKENS)
        pairs = []
        for place, block in zip(places, blocks):
            first = block.shape[0] - 2 * BLOCK if place in LATE else 4 * BLOCK
            rows = [block[first + i * BLOCK + head * TOKENS :][:TOKENS] for i in range(2)]
            columns = table_ref[place * TOKENS : (place + 1) * TOKENS, :]
            pairs.append(normed(*rows, columns, 0, gain_ref[0, head : head + 1, :]))
        queries = jnp.concatenate([pair[0] for pair in pairs], axis=0)
        queries_dot = jnp.concatenate([pair[1] for pair in pairs], axis=0)
        queries_pair = jnp.concatenate([queries_dot, queries], axis=1)
        scores = lax.dot_general(queries, keys, CONTRACT, preferred_element_type=jnp.float32)
        scores_dot = lax.dot_general(
            queries_pair, keys_pair, CONTRACT, preferred_element_type=jnp.float32
        )
        peak = jnp.max(scores, axis=1, keepdims=True)
        exponent = jnp.exp2((scores - peak) * (factor * LOG2E))
        scale = 1.0 / jnp.sum(exponent, axis=1, keepdims=True)
        weights = exponent * scale
        mean = jnp.sum(weights * scores_dot, axis=1, keepdims=True)
        weights_dot = (weights * factor) * (scores_dot - mean)
        probs = weights.astype(jnp.bfloat16)
        probs_dot = weights_dot.astype(jnp.bfloat16)
        pair = jnp.dot(probs, values_pair, preferred_element_type=jnp.float32)
        output_dot = jnp.dot(probs_dot, values, preferred_element_type=jnp.float32)
        output = pair[:, :HEAD_DIM].astype(jnp.bfloat16)
        output_dot = (output_dot + pair[:, HEAD_DIM:]).astype(jnp.bfloat16)
        for index, out in enumerate(outs):
            rows = slice(index * TOKENS, (index + 1) * TOKENS)
            out[token, :] = output[rows]
            out[tangent_token, :] = output_dot[rows]


def unpack_kernel(chip_ref, *refs):
    blocks, outs = refs[:CHIPS], refs[CHIPS:]
    for block, place in zip(blocks, ORDER):
        source = jnp.bitwise_xor(chip_ref[0], STEPS[place])
        for index, out in enumerate(outs):
            for head in range(HEADS_PER_CHIP):
                column = pl.multiple_of(source * FEATURES + head * HEAD_DIM, HEAD_DIM)
                row = index * BLOCK + head * TOKENS
                out[:, pl.ds(column, HEAD_DIM)] = block[row : row + TOKENS, :]


def exchange(block, step):
    pairs = [(place, place ^ (2 * step)) for place in range(2 * CHIPS)]
    return lax.ppermute(block, "ctx", pairs)


def swap(block):
    return lax.ppermute(block, "ctx", [(place, place ^ 1) for place in range(2 * CHIPS)])


def after(block, other):
    return lax.optimization_barrier((block, other))


def send(blocks, places=range(CHIPS)):
    steps = [STEPS[place] for place in places]
    return [exchange(block, step) if step else block for block, step in zip(blocks, steps)]


def gather_gains(gains, chip):
    shards = lax.axis_size("dp")
    gains = gains.reshape(2, -1, HEAD_DIM)
    place = lax.axis_index("dp")

    def partner(array, bit):
        return lax.ppermute(array, "dp", [(one, one ^ bit) for one in range(shards)])

    bit = 1
    while gains.shape[1] < HEADS_PER_CHIP:
        other = partner(gains, bit)
        mine_first = jnp.concatenate([gains, other], axis=1)
        mine_last = jnp.concatenate([other, gains], axis=1)
        gains = jnp.where(place & bit == 0, mine_first, mine_last)
        bit *= 2
    if gains.shape[1] > HEADS_PER_CHIP:
        return lax.dynamic_slice_in_dim(gains, chip * HEADS_PER_CHIP, HEADS_PER_CHIP, axis=1)
    wanted = chip * bit
    while bit < shards:
        gains = jnp.where((place ^ wanted) & bit == 0, gains, partner(gains, bit))
        bit *= 2
    return gains


def local(q, k, v, qd, kd, vd, query_gain, key_gain):
    q, k, v, qd, kd, vd = (array[0] for array in (q, k, v, qd, kd, vd))
    chip = (lax.axis_index("ctx") // 2).astype(jnp.int32)
    chip_ref = chip.reshape(1)

    sizes = [4 if place in LATE else ARRAYS for place in range(CHIPS)]
    blocks = pl.pallas_call(
        pack_kernel,
        out_shape=[shape(size * BLOCK + STAT_ROWS, HEAD_DIM) for size in sizes]
        + [shape(2 * BLOCK, HEAD_DIM)] * len(LATE),
        in_specs=smem() + vmem(ARRAYS),
        out_specs=vmem(CHIPS + len(LATE)),
        compiler_params=params(PACK_MIB),
        name="pack",
    )(chip_ref, k, kd, v, vd, q, qd)
    blocks, late = blocks[:CHIPS], blocks[CHIPS:]
    arrived = send(blocks[:5])
    for place, gate in zip(LATE, (1, 3)):
        block, arrived[gate] = after(blocks[place], arrived[gate])
        arrived.append(exchange(block, STEPS[place]))
    arrived.append(blocks[7])
    late = [exchange(block, STEPS[place]) for block, place in zip(late, LATE)]

    gains = jnp.stack([query_gain, key_gain])
    gains, arrived[2] = after(gains, arrived[2])
    gains = gather_gains(gains, chip)

    many = CHIPS * TOKENS
    own, table = pl.pallas_call(
        norm_kernel,
        out_shape=[
            shape(4, HEADS_PER_CHIP, many, HEAD_DIM),
            shape(many, HEAD_DIM, dtype=jnp.float32),
        ],
        in_specs=vmem(1 + CHIPS),
        out_specs=vmem(2),
        compiler_params=params(16),
        name="norm",
    )(gains, *arrived)
    other = swap(own)

    def attend(places, blocks):
        return pl.pallas_call(
            functools.partial(attend_kernel, places),
            out_shape=[shape(2 * BLOCK, HEAD_DIM)] * len(places),
            in_specs=vmem(4 + len(places)),
            out_specs=vmem(len(places)),
            compiler_params=params(32),
            name="attend",
        )(gains, table, own, other, *blocks)

    outs = dict(zip(EARLY, attend(EARLY, [arrived[place] for place in EARLY])))
    outs.update(zip(LATE, attend(LATE, late)))
    back = dict(zip(ORDER, send([outs[place] for place in ORDER], ORDER)))

    rows, width = q.shape
    attended, attended_tangent = pl.pallas_call(
        unpack_kernel,
        out_shape=[shape(rows, width)] * 2,
        in_specs=smem() + vmem(CHIPS),
        out_specs=vmem(2),
        compiler_params=params(16),
        name="unpack",
    )(chip_ref, *[back[place] for place in ORDER])
    return attended[None], attended_tangent[None]


def solution(mesh):
    rows = P("dp", "ctx", None)
    return jax.shard_map(
        local,
        mesh=mesh,
        in_specs=(rows,) * 6 + (P("dp"), P("dp")),
        out_specs=(rows, rows),
        check_vma=False,
    )
```

time: 248 us -> 236 us (0.952)
  the two profiles are of different devices: /device:TPU:96 before, /device:TPU:17 now
where the time goes in v2:
time: 236 us; the launch traced here: 235 us
  starting transfers between devices  131 us (56%)
  waiting for transfers between devices  87.9 us (37%)
  Pallas kernels  14.1 us (6%)
    ppermute x16, starting transfers between devices, exchange(): return lax.ppermute(block, 'ctx', pairs)  105 us
    ppermute x16, waiting for transfers between devices, exchange(): return lax.ppermute(block, 'ctx', pairs)  72.8 us
    ppermute x5, starting transfers between devices, partner(): lax.ppermute(array, 'dp', [(one, one ^ bit) for one in range(shards)])  21.8 us
    ppermute x5, waiting for transfers between devices, partner(): lax.ppermute(array, 'dp', [(one, one ^ bit) for one in range(shards)])  15.1 us
    pallas_call x2, Pallas kernels, attend(): pl.pallas_call(functools.partial(attend_kernel, places), out_shape=[shape...  8 us
  transfers between devices with their start and end apart: 22, of which 8 were waited for; matrix products, arithmetic and copies ran while one was open for 0% of the time, Pallas kernels for 3%

profile of v2, /device:TPU:17, one launch (start us, length us, event | category | flops | bytes accessed | tf_op | source)
XLA Modules:
  0.0 235.4 jit_solution(753316819177312992)
XLA Ops:
  0.7 4.3 %pack.1 = (bf16[1552,128]{1,0:T(8,128)(2,1)}, bf16[1552,128]{1,0:T(8,128)(2,1)}, bf16[1552,128]{1,0:T(8,128)(2,1)}, bf16[1552,128]{1,0:T(8,128)(2,1)}, bf16[1552...) custom-call(s32[1]{0:T(128)} %bitcast.chip_ref, ...), custom_call_target="tpu_custom_call" | custom-call | tf_op jit(solution)/shard_map/pack/pallas_call | solution.py:226
  4.9 10.2 %collective-permute-start = (bf16[1552,128]{1,0:T(8,128)(2,1)}, bf16[1552,128]{1,0:T(8,128)(2,1)S(1)}, u32[]{:S(2)}, u32[]{:S(2)}) collective-permute-start(bf16[1552,128]{1,0:T(8,128)(2,1)} %get-tuple-element.30), channel_id=1, source_target_pairs={{0,10},{1,11},{2,8},{3,9},{4,14},{5,15},{6,12},{7,13},{8,2},{9,3},... | collective-permute-start | bytes 1191944 | tf_op jit(solution)/shard_map/ppermute | solution.py:180
  15.1 26.2 %collective-permute-done.refs_2_ = bf16[1552,128]{1,0:T(8,128)(2,1)S(1)} collective-permute-done((bf16[1552,128]{1,0:T(8,128)(2,1)}, bf16[1552,128]{1,0:T(8,128)(2,1)S(1)}, u32[]{:S(2)}, u32[]{:S(2)}) %collective-permute-start) | collective-permute-done | bytes 397344 | tf_op jit(solution)/shard_map/ppermute | solution.py:180
  41.3 2.9 %collective-permute-start.1 = (bf16[2,1,128]{2,1,0:T(2,128)(2,1)S(1)}, bf16[2,1,128]{2,1,0:T(2,128)(2,1)S(1)}, u32[]{:S(2)}, u32[]{:S(2)}) collective-permute-start(bf16[2,1,128]{2,1,0:T(2,128)(2,1)S(1)} %copy.11), channel_id=1, source_target_pairs={{0,16},{16,0},{32,48},{48,32},{64,80},{80,64},{96,112},{112,96},{1... | collective-permute-start | bytes 1544 | tf_op jit(solution)/shard_map/ppermute | solution.py:202
  44.2 9.3 %collective-permute-start.7 = (bf16[1552,128]{1,0:T(8,128)(2,1)}, bf16[1552,128]{1,0:T(8,128)(2,1)S(1)}, u32[]{:S(2)}, u32[]{:S(2)}) collective-permute-start(bf16[1552,128]{1,0:T(8,128)(2,1)} %get-tuple-element.34), channel_id=1, source_target_pairs={{0,2},{1,3},{2,0},{3,1},{4,6},{5,7},{6,4},{7,5},{8,10},{9,11},{10,... | collective-permute-start | bytes 1191944 | tf_op jit(solution)/shard_map/ppermute | solution.py:180
  53.5 4.1 %collective-permute-start.8 = (bf16[1552,128]{1,0:T(8,128)(2,1)}, bf16[1552,128]{1,0:T(8,128)(2,1)S(1)}, u32[]{:S(2)}, u32[]{:S(2)}) collective-permute-start(bf16[1552,128]{1,0:T(8,128)(2,1)} %get-tuple-element.38), channel_id=1, source_target_pairs={{0,4},{1,5},{2,6},{3,7},{4,0},{5,1},{6,2},{7,3},{8,12},{9,13},{10,... | collective-permute-start | bytes 1191944 | tf_op jit(solution)/shard_map/ppermute | solution.py:180
  57.7 2.3 collective-permute-start.2
  59.9 3.8 %collective-permute-done.2 = bf16[2,2,128]{2,1,0:T(2,128)(2,1)S(1)} collective-permute-done((bf16[2,2,128]{2,1,0:T(2,128)(2,1)S(1)}, bf16[2,2,128]{2,1,0:T(2,128)(2,1)S(1)}, u32[]{:S(2)}, u32[]{:S(2)}) %collective-permute-start.2) | collective-permute-done | bytes 1056 | tf_op jit(solution)/shard_map/ppermute | solution.py:202
  63.8 3.1 %collective-permute-start.3 = (bf16[2,4,128]{2,1,0:T(4,128)(2,1)S(1)}, bf16[2,4,128]{2,1,0:T(4,128)(2,1)S(1)}, u32[]{:S(2)}, u32[]{:S(2)}) collective-permute-start(bf16[2,4,128]{2,1,0:T(4,128)(2,1)S(1)} %maximum_select_fusion), channel_id=1, source_target_pairs={{0,64},{16,80},{32,96},{48,112},{64,0},{80,16},{96,32},{112,48},{1... | collective-permute-start | bytes 6152 | tf_op jit(solution)/shard_map/ppermute | solution.py:202
  66.9 1.5 collective-permute-done.3
  68.4 4.6 %collective-permute-start.4 = (bf16[2,4,128]{2,1,0:T(4,128)(2,1)S(1)}, bf16[2,4,128]{2,1,0:T(4,128)(2,1)S(1)}, u32[]{:S(2)}, u32[]{:S(2)}) collective-permute-start(bf16[2,4,128]{2,1,0:T(4,128)(2,1)S(1)} %bitcast.30), channel_id=1, source_target_pairs={{0,128},{16,144},{32,160},{48,176},{64,192},{80,208},{96,224},{112... | collective-permute-start | bytes 6152 | tf_op jit(solution)/shard_map/ppermute | solution.py:202
  73.1 6.7 %collective-permute-start.6 = (bf16[1552,128]{1,0:T(8,128)(2,1)}, bf16[1552,128]{1,0:T(8,128)(2,1)S(1)}, u32[]{:S(2)}, u32[]{:S(2)}) collective-permute-start(bf16[1552,128]{1,0:T(8,128)(2,1)} %get-tuple-element.32), channel_id=1, source_target_pairs={{0,8},{1,9},{2,10},{3,11},{4,12},{5,13},{6,14},{7,15},{8,0},{9,1},... | collective-permute-start | bytes 1191944 | tf_op jit(solution)/shard_map/ppermute | solution.py:180
  79.8 2.5 %collective-permute-start.9 = (bf16[1552,128]{1,0:T(8,128)(2,1)}, bf16[1552,128]{1,0:T(8,128)(2,1)S(1)}, u32[]{:S(2)}, u32[]{:S(2)}) collective-permute-start(bf16[1552,128]{1,0:T(8,128)(2,1)} %get-tuple-element.40), channel_id=1, source_target_pairs={{0,6},{1,7},{2,4},{3,5},{4,2},{5,3},{6,0},{7,1},{8,14},{9,15},{10,... | collective-permute-start | bytes 1191944 | tf_op jit(solution)/shard_map/ppermute | solution.py:180
  82.3 3.4 %collective-permute-start.10 = (bf16[1040,128]{1,0:T(8,128)(2,1)}, bf16[1040,128]{1,0:T(8,128)(2,1)S(1)}, u32[]{:S(2)}, u32[]{:S(2)}) collective-permute-start(bf16[1040,128]{1,0:T(8,128)(2,1)} %get-tuple-element.41), channel_id=1, source_target_pairs={{0,12},{1,13},{2,14},{3,15},{4,8},{5,9},{6,10},{7,11},{8,4},{9,5},... | collective-permute-start | bytes 798728 | tf_op jit(solution)/shard_map/ppermute | solution.py:180
  85.7 7.9 %collective-permute-start.11 = (bf16[1040,128]{1,0:T(8,128)(2,1)}, bf16[1040,128]{1,0:T(8,128)(2,1)S(1)}, u32[]{:S(2)}, u32[]{:S(2)}) collective-permute-start(bf16[1040,128]{1,0:T(8,128)(2,1)} %get-tuple-element.42), channel_id=1, source_target_pairs={{0,14},{1,15},{2,12},{3,13},{4,10},{5,11},{6,8},{7,9},{8,6},{9,7},... | collective-permute-start | bytes 798728 | tf_op jit(solution)/shard_map/ppermute | solution.py:180
  93.7 8.8 %collective-permute-start.5 = (bf16[2,4,128]{2,1,0:T(4,128)(2,1)S(1)}, bf16[2,4,128]{2,1,0:T(4,128)(2,1)S(1)}, u32[]{:S(2)}, u32[]{:S(2)}) collective-permute-start(bf16[2,4,128]{2,1,0:T(4,128)(2,1)S(1)} %bitcast.32), channel_id=1, source_target_pairs={{0,256},{16,272},{32,288},{48,304},{64,320},{80,336},{96,352},{112... | collective-permute-start | bytes 6152 | tf_op jit(solution)/shard_map/ppermute | solution.py:202
  102.5 9.8 %collective-permute-done.5 = bf16[2,4,128]{2,1,0:T(4,128)(2,1)S(1)} collective-permute-done((bf16[2,4,128]{2,1,0:T(4,128)(2,1)S(1)}, bf16[2,4,128]{2,1,0:T(4,128)(2,1)S(1)}, u32[]{:S(2)}, u32[]{:S(2)}) %collective-permute-start.5) | collective-permute-done | bytes 2080 | tf_op jit(solution)/shard_map/ppermute | solution.py:202
  112.3 28.7 %collective-permute-done.9.refs_4_ = bf16[1552,128]{1,0:T(8,128)(2,1)S(1)} collective-permute-done((bf16[1552,128]{1,0:T(8,128)(2,1)}, bf16[1552,128]{1,0:T(8,128)(2,1)S(1)}, u32[]{:S(2)}, u32[]{:S(2)}) %collective-permute-start.9) | collective-permute-done | bytes 397344 | tf_op jit(solution)/shard_map/ppermute | solution.py:180
  142.6 4.5 %collective-permute-start.12 = (bf16[4,4,512,128]{3,2,1,0:T(8,128)(2,1)S(1)}, bf16[4,4,512,128]{3,2,1,0:T(8,128)(2,1)S(1)}, u32[]{:S(2)}, u32[]{:S(2)}) collective-permute-start(bf16[4,4,512,128]{3,2,1,0:T(8,128)(2,1)S(1)} %get-tuple-element.45.own_ref), channel_id=1, source_target_pairs={{0,1},{1,0},{2,3},{3,2},{4,5},{5,4},{6,7},{7,6},{8,9},{9,8},{10,11... | collective-permute-start | bytes 6291464 | tf_op jit(solution)/shard_map/ppermute | solution.py:184
  147.1 4.4 %collective-permute-start.15 = (bf16[512,128]{1,0:T(8,128)(2,1)S(1)}, bf16[512,128]{1,0:T(8,128)(2,1)S(1)}, u32[]{:S(2)}, u32[]{:S(2)}) collective-permute-start(bf16[512,128]{1,0:T(8,128)(2,1)S(1)} %copy-done.3), channel_id=1, source_target_pairs={{0,12},{1,13},{2,14},{3,15},{4,8},{5,9},{6,10},{7,11},{8,4},{9,5},... | collective-permute-start | bytes 393224 | tf_op jit(solution)/shard_map/ppermute | solution.py:180
  151.5 12.2 %collective-permute-start.16 = (bf16[512,128]{1,0:T(8,128)(2,1)S(1)}, bf16[512,128]{1,0:T(8,128)(2,1)S(1)}, u32[]{:S(2)}, u32[]{:S(2)}) collective-permute-start(bf16[512,128]{1,0:T(8,128)(2,1)S(1)} %copy-done.2), channel_id=1, source_target_pairs={{0,14},{1,15},{2,12},{3,13},{4,10},{5,11},{6,8},{7,9},{8,6},{9,7},... | collective-permute-start | bytes 393224 | tf_op jit(solution)/shard_map/ppermute | solution.py:180
  163.8 5.2 %attend.2 = (bf16[512,128]{1,0:T(8,128)(2,1)S(1)}, bf16[512,128]{1,0:T(8,128)(2,1)S(1)}, bf16[512,128]{1,0:T(8,128)(2,1)S(1)}, bf16[512,128]{1,0:T(8,128)(2,1)S(...) custom-call(bf16[2,4,128]{2,1,0:T(4,128)(2,1)S(1)} %bitcast.22, ...), custom_call_target="tpu_custom_call" | custom-call | tf_op jit(solution)/shard_map/attend/pallas_call | solution.py:262
  169.0 18.4 %collective-permute-start.13 = (bf16[512,128]{1,0:T(8,128)(2,1)S(1)}, bf16[512,128]{1,0:T(8,128)(2,1)S(1)}, u32[]{:S(2)}, u32[]{:S(2)}) collective-permute-start(bf16[512,128]{1,0:T(8,128)(2,1)S(1)} %get-tuple-element.46), channel_id=1, source_target_pairs={{0,8},{1,9},{2,10},{3,11},{4,12},{5,13},{6,14},{7,15},{8,0},{9,1},... | collective-permute-start | bytes 393224 | tf_op jit(solution)/shard_map/ppermute | solution.py:180
  187.4 3.1 %collective-permute-start.14 = (bf16[512,128]{1,0:T(8,128)(2,1)S(1)}, bf16[512,128]{1,0:T(8,128)(2,1)S(1)}, u32[]{:S(2)}, u32[]{:S(2)}) collective-permute-start(bf16[512,128]{1,0:T(8,128)(2,1)S(1)} %get-tuple-element.47), channel_id=1, source_target_pairs={{0,10},{1,11},{2,8},{3,9},{4,14},{5,15},{6,12},{7,13},{8,2},{9,3},... | collective-permute-start | bytes 393224 | tf_op jit(solution)/shard_map/ppermute | solution.py:180
  190.5 2.2 collective-permute-start.19
  192.7 7.3 %collective-permute-start.20 = (bf16[512,128]{1,0:T(8,128)(2,1)S(1)}, bf16[512,128]{1,0:T(8,128)(2,1)S(1)}, u32[]{:S(2)}, u32[]{:S(2)}) collective-permute-start(bf16[512,128]{1,0:T(8,128)(2,1)S(1)} %get-tuple-element.53), channel_id=1, source_target_pairs={{0,4},{1,5},{2,6},{3,7},{4,0},{5,1},{6,2},{7,3},{8,12},{9,13},{10,... | collective-permute-start | bytes 393224 | tf_op jit(solution)/shard_map/ppermute | solution.py:180
  200.0 1.9 collective-permute-start.21
  201.9 2.8 %attend.3 = (bf16[512,128]{1,0:T(8,128)(2,1)S(1)}, bf16[512,128]{1,0:T(8,128)(2,1)S(1)}) custom-call(bf16[2,4,128]{2,1,0:T(4,128)(2,1)S(1)} %bitcast.23, f32[512,128]{1,0:T(8,128)S(1)} %get-tuple-element.44.table_ref, bf16[4,4,512,128]{3,2,1,0:T(8,128)(2,1)S(1)} %get-tuple-element.45.own_ref, bf16[4,4,512,128]{3,2,1,0:T(8,128)(2,1)S(1)} %collective-permute-done.12.other_ref, ...), custom_call_target="tpu_custom_call" | custom-call | tf_op jit(solution)/shard_map/attend/pallas_call | solution.py:262
  204.7 3.0 %collective-permute-done.13.refs_0_ = bf16[512,128]{1,0:T(8,128)(2,1)S(1)} collective-permute-done((bf16[512,128]{1,0:T(8,128)(2,1)S(1)}, bf16[512,128]{1,0:T(8,128)(2,1)S(1)}, u32[]{:S(2)}, u32[]{:S(2)}) %collective-permute-start.13) | collective-permute-done | bytes 131104 | tf_op jit(solution)/shard_map/ppermute | solution.py:180
  207.7 3.8 %collective-permute-start.17 = (bf16[512,128]{1,0:T(8,128)(2,1)S(1)}, bf16[512,128]{1,0:T(8,128)(2,1)S(1)}, u32[]{:S(2)}, u32[]{:S(2)}) collective-permute-start(bf16[512,128]{1,0:T(8,128)(2,1)S(1)} %get-tuple-element.50), channel_id=1, source_target_pairs={{0,12},{1,13},{2,14},{3,15},{4,8},{5,9},{6,10},{7,11},{8,4},{9,5},... | collective-permute-start | bytes 393224 | tf_op jit(solution)/shard_map/ppermute | solution.py:180
  211.7 7.7 %collective-permute-start.18 = (bf16[512,128]{1,0:T(8,128)(2,1)S(1)}, bf16[512,128]{1,0:T(8,128)(2,1)S(1)}, u32[]{:S(2)}, u32[]{:S(2)}) collective-permute-start(bf16[512,128]{1,0:T(8,128)(2,1)S(1)} %get-tuple-element.51), channel_id=1, source_target_pairs={{0,14},{1,15},{2,12},{3,13},{4,10},{5,11},{6,8},{7,9},{8,6},{9,7},... | collective-permute-start | bytes 393224 | tf_op jit(solution)/shard_map/ppermute | solution.py:180
  219.3 14.8 %collective-permute-done.21.refs_6_ = bf16[512,128]{1,0:T(8,128)(2,1)S(1)} collective-permute-done((bf16[512,128]{1,0:T(8,128)(2,1)S(1)}, bf16[512,128]{1,0:T(8,128)(2,1)S(1)}, u32[]{:S(2)}, u32[]{:S(2)}) %collective-permute-start.21) | collective-permute-done | bytes 131104 | tf_op jit(solution)/shard_map/ppermute | solution.py:180
  (36 shorter events, 3.1 us)
Async XLA Ops:
  0.6 14.5 %copy-start.4 = (bf16[128]{0:T(256)(128)(2,1)S(1)}, bf16[128]{0:T(256)(128)(2,1)}, u32[]{:S(2)}) copy-start(bf16[128]{0:T(256)(128)(2,1)} %param.15) | copy-start | bytes 772
  0.6 14.5 %copy-start.5 = (bf16[128]{0:T(256)(128)(2,1)S(1)}, bf16[128]{0:T(256)(128)(2,1)}, u32[]{:S(2)}) copy-start(bf16[128]{0:T(256)(128)(2,1)} %param.14) | copy-start | bytes 772
  4.9 36.4 %collective-permute-start = (bf16[1552,128]{1,0:T(8,128)(2,1)}, bf16[1552,128]{1,0:T(8,128)(2,1)S(1)}, u32[]{:S(2)}, u32[]{:S(2)}) collective-permute-start(bf16[1552,128]{1,0:T(8,128)(2,1)} %get-tuple-element.30), channel_id=1, source_target_pairs={{0,10},{1,11},{2,8},{3,9},{4,14},{5,15},{6,12},{7,13},{8,2},{9,3},... | collective-permute-start | bytes 1191944 | tf_op jit(solution)/shard_map/ppermute | solution.py:180
  41.3 16.3 %collective-permute-start.1 = (bf16[2,1,128]{2,1,0:T(2,128)(2,1)S(1)}, bf16[2,1,128]{2,1,0:T(2,128)(2,1)S(1)}, u32[]{:S(2)}, u32[]{:S(2)}) collective-permute-start(bf16[2,1,128]{2,1,0:T(2,128)(2,1)S(1)} %copy.11), channel_id=1, source_target_pairs={{0,16},{16,0},{32,48},{48,32},{64,80},{80,64},{96,112},{112,96},{1... | collective-permute-start | bytes 1544 | tf_op jit(solution)/shard_map/ppermute | solution.py:202
  44.2 38.1 %collective-permute-start.7 = (bf16[1552,128]{1,0:T(8,128)(2,1)}, bf16[1552,128]{1,0:T(8,128)(2,1)S(1)}, u32[]{:S(2)}, u32[]{:S(2)}) collective-permute-start(bf16[1552,128]{1,0:T(8,128)(2,1)} %get-tuple-element.34), channel_id=1, source_target_pairs={{0,2},{1,3},{2,0},{3,1},{4,6},{5,7},{6,4},{7,5},{8,10},{9,11},{10,... | collective-permute-start | bytes 1191944 | tf_op jit(solution)/shard_map/ppermute | solution.py:180
  53.5 32.2 %collective-permute-start.8 = (bf16[1552,128]{1,0:T(8,128)(2,1)}, bf16[1552,128]{1,0:T(8,128)(2,1)S(1)}, u32[]{:S(2)}, u32[]{:S(2)}) collective-permute-start(bf16[1552,128]{1,0:T(8,128)(2,1)} %get-tuple-element.38), channel_id=1, source_target_pairs={{0,4},{1,5},{2,6},{3,7},{4,0},{5,1},{6,2},{7,3},{8,12},{9,13},{10,... | collective-permute-start | bytes 1191944 | tf_op jit(solution)/shard_map/ppermute | solution.py:180
  57.7 6.1 %collective-permute-start.2 = (bf16[2,2,128]{2,1,0:T(2,128)(2,1)S(1)}, bf16[2,2,128]{2,1,0:T(2,128)(2,1)S(1)}, u32[]{:S(2)}, u32[]{:S(2)}) collective-permute-start(bf16[2,2,128]{2,1,0:T(2,128)(2,1)S(1)} %broadcast_select_fusion), channel_id=1, source_target_pairs={{0,32},{16,48},{32,0},{48,16},{64,96},{80,112},{96,64},{112,80},{1... | collective-permute-start | bytes 3080 | tf_op jit(solution)/shard_map/ppermute | solution.py:202
  63.8 4.6 %collective-permute-start.3 = (bf16[2,4,128]{2,1,0:T(4,128)(2,1)S(1)}, bf16[2,4,128]{2,1,0:T(4,128)(2,1)S(1)}, u32[]{:S(2)}, u32[]{:S(2)}) collective-permute-start(bf16[2,4,128]{2,1,0:T(4,128)(2,1)S(1)} %maximum_select_fusion), channel_id=1, source_target_pairs={{0,64},{16,80},{32,96},{48,112},{64,0},{80,16},{96,32},{112,48},{1... | collective-permute-start | bytes 6152 | tf_op jit(solution)/shard_map/ppermute | solution.py:202
  68.4 25.2 %collective-permute-start.4 = (bf16[2,4,128]{2,1,0:T(4,128)(2,1)S(1)}, bf16[2,4,128]{2,1,0:T(4,128)(2,1)S(1)}, u32[]{:S(2)}, u32[]{:S(2)}) collective-permute-start(bf16[2,4,128]{2,1,0:T(4,128)(2,1)S(1)} %bitcast.30), channel_id=1, source_target_pairs={{0,128},{16,144},{32,160},{48,176},{64,192},{80,208},{96,224},{112... | collective-permute-start | bytes 6152 | tf_op jit(solution)/shard_map/ppermute | solution.py:202
  73.1 39.2 %collective-permute-start.6 = (bf16[1552,128]{1,0:T(8,128)(2,1)}, bf16[1552,128]{1,0:T(8,128)(2,1)S(1)}, u32[]{:S(2)}, u32[]{:S(2)}) collective-permute-start(bf16[1552,128]{1,0:T(8,128)(2,1)} %get-tuple-element.32), channel_id=1, source_target_pairs={{0,8},{1,9},{2,10},{3,11},{4,12},{5,13},{6,14},{7,15},{8,0},{9,1},... | collective-permute-start | bytes 1191944 | tf_op jit(solution)/shard_map/ppermute | solution.py:180
  79.8 61.2 %collective-permute-start.9 = (bf16[1552,128]{1,0:T(8,128)(2,1)}, bf16[1552,128]{1,0:T(8,128)(2,1)S(1)}, u32[]{:S(2)}, u32[]{:S(2)}) collective-permute-start(bf16[1552,128]{1,0:T(8,128)(2,1)} %get-tuple-element.40), channel_id=1, source_target_pairs={{0,6},{1,7},{2,4},{3,5},{4,2},{5,3},{6,0},{7,1},{8,14},{9,15},{10,... | collective-permute-start | bytes 1191944 | tf_op jit(solution)/shard_map/ppermute | solution.py:180
  82.3 58.6 %collective-permute-start.10 = (bf16[1040,128]{1,0:T(8,128)(2,1)}, bf16[1040,128]{1,0:T(8,128)(2,1)S(1)}, u32[]{:S(2)}, u32[]{:S(2)}) collective-permute-start(bf16[1040,128]{1,0:T(8,128)(2,1)} %get-tuple-element.41), channel_id=1, source_target_pairs={{0,12},{1,13},{2,14},{3,15},{4,8},{5,9},{6,10},{7,11},{8,4},{9,5},... | collective-permute-start | bytes 798728 | tf_op jit(solution)/shard_map/ppermute | solution.py:180
  85.7 55.2 %collective-permute-start.11 = (bf16[1040,128]{1,0:T(8,128)(2,1)}, bf16[1040,128]{1,0:T(8,128)(2,1)S(1)}, u32[]{:S(2)}, u32[]{:S(2)}) collective-permute-start(bf16[1040,128]{1,0:T(8,128)(2,1)} %get-tuple-element.42), channel_id=1, source_target_pairs={{0,14},{1,15},{2,12},{3,13},{4,10},{5,11},{6,8},{7,9},{8,6},{9,7},... | collective-permute-start | bytes 798728 | tf_op jit(solution)/shard_map/ppermute | solution.py:180
  93.7 18.6 %collective-permute-start.5 = (bf16[2,4,128]{2,1,0:T(4,128)(2,1)S(1)}, bf16[2,4,128]{2,1,0:T(4,128)(2,1)S(1)}, u32[]{:S(2)}, u32[]{:S(2)}) collective-permute-start(bf16[2,4,128]{2,1,0:T(4,128)(2,1)S(1)} %bitcast.32), channel_id=1, source_target_pairs={{0,256},{16,272},{32,288},{48,304},{64,320},{80,336},{96,352},{112... | collective-permute-start | bytes 6152 | tf_op jit(solution)/shard_map/ppermute | solution.py:202
  141.0 1.0 copy-start
  142.0 5.1 %copy-start.3 = (bf16[512,128]{1,0:T(8,128)(2,1)S(1)}, bf16[512,128]{1,0:T(8,128)(2,1)}, u32[]{:S(2)}) copy-start(bf16[512,128]{1,0:T(8,128)(2,1)} %get-tuple-element.48) | copy-start | bytes 393220
  142.0 9.5 %copy-start.2 = (bf16[512,128]{1,0:T(8,128)(2,1)S(1)}, bf16[512,128]{1,0:T(8,128)(2,1)}, u32[]{:S(2)}) copy-start(bf16[512,128]{1,0:T(8,128)(2,1)} %get-tuple-element.49) | copy-start | bytes 393220
  142.0 21.8 %copy-start.1 = (bf16[1552,128]{1,0:T(8,128)(2,1)S(1)}, bf16[1552,128]{1,0:T(8,128)(2,1)}, u32[]{:S(2)}) copy-start(bf16[1552,128]{1,0:T(8,128)(2,1)} %get-tuple-element.43.refs_7_.refs_5_) | copy-start | bytes 1191940
  142.6 21.1 %collective-permute-start.12 = (bf16[4,4,512,128]{3,2,1,0:T(8,128)(2,1)S(1)}, bf16[4,4,512,128]{3,2,1,0:T(8,128)(2,1)S(1)}, u32[]{:S(2)}, u32[]{:S(2)}) collective-permute-start(bf16[4,4,512,128]{3,2,1,0:T(8,128)(2,1)S(1)} %get-tuple-element.45.own_ref), channel_id=1, source_target_pairs={{0,1},{1,0},{2,3},{3,2},{4,5},{5,4},{6,7},{7,6},{8,9},{9,8},{10,11... | collective-permute-start | bytes 6291464 | tf_op jit(solution)/shard_map/ppermute | solution.py:184
  147.1 45.6 %collective-permute-start.15 = (bf16[512,128]{1,0:T(8,128)(2,1)S(1)}, bf16[512,128]{1,0:T(8,128)(2,1)S(1)}, u32[]{:S(2)}, u32[]{:S(2)}) collective-permute-start(bf16[512,128]{1,0:T(8,128)(2,1)S(1)} %copy-done.3), channel_id=1, source_target_pairs={{0,12},{1,13},{2,14},{3,15},{4,8},{5,9},{6,10},{7,11},{8,4},{9,5},... | collective-permute-start | bytes 393224 | tf_op jit(solution)/shard_map/ppermute | solution.py:180
  151.5 48.4 %collective-permute-start.16 = (bf16[512,128]{1,0:T(8,128)(2,1)S(1)}, bf16[512,128]{1,0:T(8,128)(2,1)S(1)}, u32[]{:S(2)}, u32[]{:S(2)}) collective-permute-start(bf16[512,128]{1,0:T(8,128)(2,1)S(1)} %copy-done.2), channel_id=1, source_target_pairs={{0,14},{1,15},{2,12},{3,13},{4,10},{5,11},{6,8},{7,9},{8,6},{9,7},... | collective-permute-start | bytes 393224 | tf_op jit(solution)/shard_map/ppermute | solution.py:180
  169.0 38.7 %collective-permute-start.13 = (bf16[512,128]{1,0:T(8,128)(2,1)S(1)}, bf16[512,128]{1,0:T(8,128)(2,1)S(1)}, u32[]{:S(2)}, u32[]{:S(2)}) collective-permute-start(bf16[512,128]{1,0:T(8,128)(2,1)S(1)} %get-tuple-element.46), channel_id=1, source_target_pairs={{0,8},{1,9},{2,10},{3,11},{4,12},{5,13},{6,14},{7,15},{8,0},{9,1},... | collective-permute-start | bytes 393224 | tf_op jit(solution)/shard_map/ppermute | solution.py:180
  187.4 24.3 %collective-permute-start.14 = (bf16[512,128]{1,0:T(8,128)(2,1)S(1)}, bf16[512,128]{1,0:T(8,128)(2,1)S(1)}, u32[]{:S(2)}, u32[]{:S(2)}) collective-permute-start(bf16[512,128]{1,0:T(8,128)(2,1)S(1)} %get-tuple-element.47), channel_id=1, source_target_pairs={{0,10},{1,11},{2,8},{3,9},{4,14},{5,15},{6,12},{7,13},{8,2},{9,3},... | collective-permute-start | bytes 393224 | tf_op jit(solution)/shard_map/ppermute | solution.py:180
  190.5 28.8 %collective-permute-start.19 = (bf16[512,128]{1,0:T(8,128)(2,1)S(1)}, bf16[512,128]{1,0:T(8,128)(2,1)S(1)}, u32[]{:S(2)}, u32[]{:S(2)}) collective-permute-start(bf16[512,128]{1,0:T(8,128)(2,1)S(1)} %get-tuple-element.52), channel_id=1, source_target_pairs={{0,2},{1,3},{2,0},{3,1},{4,6},{5,7},{6,4},{7,5},{8,10},{9,11},{10,... | collective-permute-start | bytes 393224 | tf_op jit(solution)/shard_map/ppermute | solution.py:180
  192.7 26.6 %collective-permute-start.20 = (bf16[512,128]{1,0:T(8,128)(2,1)S(1)}, bf16[512,128]{1,0:T(8,128)(2,1)S(1)}, u32[]{:S(2)}, u32[]{:S(2)}) collective-permute-start(bf16[512,128]{1,0:T(8,128)(2,1)S(1)} %get-tuple-element.53), channel_id=1, source_target_pairs={{0,4},{1,5},{2,6},{3,7},{4,0},{5,1},{6,2},{7,3},{8,12},{9,13},{10,... | collective-permute-start | bytes 393224 | tf_op jit(solution)/shard_map/ppermute | solution.py:180
  200.0 34.2 %collective-permute-start.21 = (bf16[512,128]{1,0:T(8,128)(2,1)S(1)}, bf16[512,128]{1,0:T(8,128)(2,1)S(1)}, u32[]{:S(2)}, u32[]{:S(2)}) collective-permute-start(bf16[512,128]{1,0:T(8,128)(2,1)S(1)} %get-tuple-element.54), channel_id=1, source_target_pairs={{0,6},{1,7},{2,4},{3,5},{4,2},{5,3},{6,0},{7,1},{8,14},{9,15},{10,... | collective-permute-start | bytes 393224 | tf_op jit(solution)/shard_map/ppermute | solution.py:180
  207.7 26.5 %collective-permute-start.17 = (bf16[512,128]{1,0:T(8,128)(2,1)S(1)}, bf16[512,128]{1,0:T(8,128)(2,1)S(1)}, u32[]{:S(2)}, u32[]{:S(2)}) collective-permute-start(bf16[512,128]{1,0:T(8,128)(2,1)S(1)} %get-tuple-element.50), channel_id=1, source_target_pairs={{0,12},{1,13},{2,14},{3,15},{4,8},{5,9},{6,10},{7,11},{8,4},{9,5},... | collective-permute-start | bytes 393224 | tf_op jit(solution)/shard_map/ppermute | solution.py:180
  211.7 22.5 %collective-permute-start.18 = (bf16[512,128]{1,0:T(8,128)(2,1)S(1)}, bf16[512,128]{1,0:T(8,128)(2,1)S(1)}, u32[]{:S(2)}, u32[]{:S(2)}) collective-permute-start(bf16[512,128]{1,0:T(8,128)(2,1)S(1)} %get-tuple-element.51), channel_id=1, source_target_pairs={{0,14},{1,15},{2,12},{3,13},{4,10},{5,11},{6,8},{7,9},{8,6},{9,7},... | collective-permute-start | bytes 393224 | tf_op jit(solution)/shard_map/ppermute | solution.py:180

commit v3 on v2

--- a/solution.py
+++ b/solution.py
@@ -195,26 +195,10 @@
 
 def gather_gains(gains, chip):
     shards = lax.axis_size("dp")
-    gains = gains.reshape(2, -1, HEAD_DIM)
-    place = lax.axis_index("dp")
-
-    def partner(array, bit):
-        return lax.ppermute(array, "dp", [(one, one ^ bit) for one in range(shards)])
-
-    bit = 1
-    while gains.shape[1] < HEADS_PER_CHIP:
-        other = partner(gains, bit)
-        mine_first = jnp.concatenate([gains, other], axis=1)
-        mine_last = jnp.concatenate([other, gains], axis=1)
-        gains = jnp.where(place & bit == 0, mine_first, mine_last)
-        bit *= 2
-    if gains.shape[1] > HEADS_PER_CHIP:
-        return lax.dynamic_slice_in_dim(gains, chip * HEADS_PER_CHIP, HEADS_PER_CHIP, axis=1)
-    wanted = chip * bit
-    while bit < shards:
-        gains = jnp.where((place ^ wanted) & bit == 0, gains, partner(gains, bit))
-        bit *= 2
-    return gains
+    gains = jnp.broadcast_to(gains[None], (shards, *gains.shape))
+    gains = lax.all_to_all(gains, "dp", 0, 0, tiled=True)
+    gains = jnp.moveaxis(gains, 0, 1).reshape(2, -1, HEAD_DIM)
+    return lax.dynamic_slice_in_dim(gains, chip * HEADS_PER_CHIP, HEADS_PER_CHIP, axis=1)
 
 
 def local(q, k, v, qd, kd, vd, query_gain, key_gain):
@@ -241,7 +225,7 @@
     late = [exchange(block, STEPS[place]) for block, place in zip(late, LATE)]
 
     gains = jnp.stack([query_gain, key_gain])
-    gains, arrived[2] = after(gains, arrived[2])
+    gains, arrived[3] = after(gains, arrived[3])
     gains = gather_gains(gains, chip)
 
     many = CHIPS * TOKENS

time: 236 us -> 213 us (0.903)
  the two profiles are of different devices: /device:TPU:17 before, /device:TPU:491 now
where the time goes in v3:
time: 213 us
  starting transfers between devices  107 us (50%)
  waiting for transfers between devices  89 us (42%)
  Pallas kernels  14.1 us (7%)
    ppermute x16, starting transfers between devices, exchange(): return lax.ppermute(block, 'ctx', pairs)  84.9 us
    ppermute x16, waiting for transfers between devices, exchange(): return lax.ppermute(block, 'ctx', pairs)  83 us
    all_to_all x1, starting transfers between devices, gather_gains(): gains = lax.all_to_all(gains, 'dp', 0, 0, tiled=True)  16.6 us
    pallas_call x2, Pallas kernels, attend(): pl.pallas_call(functools.partial(attend_kernel, places), out_shape=[shape...  8 us
    all_to_all x1, waiting for transfers between devices, gather_gains(): gains = lax.all_to_all(gains, 'dp', 0, 0, tiled=True)  5.95 us
    ppermute x1, starting transfers between devices, swap(): lax.ppermute(block, 'ctx', [(place, place ^ 1) for place in range(2 * CHI...  5.35 us
    pallas_call x1, Pallas kernels, local(): pl.pallas_call(pack_kernel, out_shape=[shape(size * BLOCK + STAT_ROWS, HE...  4.28 us
  transfers between devices with their start and end apart: 18, of which 5 were waited for; matrix products, arithmetic and copies ran while one was open for 0% of the time, Pallas kernels for 4%

profile of v3, /device:TPU:491, one launch (start us, length us, event | category | flops | bytes accessed | tf_op | source)
XLA Modules:
  0.0 212.5 jit_solution(10839674253403552077)
XLA Ops:
  0.7 4.3 %pack.1 = (bf16[1552,128]{1,0:T(8,128)(2,1)}, bf16[1552,128]{1,0:T(8,128)(2,1)}, bf16[1552,128]{1,0:T(8,128)(2,1)}, bf16[1552,128]{1,0:T(8,128)(2,1)}, bf16[1552...) custom-call(s32[1]{0:T(128)} %bitcast.chip_ref, ...), custom_call_target="tpu_custom_call" | custom-call | tf_op jit(solution)/shard_map/pack/pallas_call | solution.py:210
  4.9 3.1 %collective-permute-start = (bf16[1552,128]{1,0:T(8,128)(2,1)}, bf16[1552,128]{1,0:T(8,128)(2,1)S(1)}, u32[]{:S(2)}, u32[]{:S(2)}) collective-permute-start(bf16[1552,128]{1,0:T(8,128)(2,1)} %get-tuple-element.31), channel_id=1, source_target_pairs={{0,4},{1,5},{2,6},{3,7},{4,0},{5,1},{6,2},{7,3},{8,12},{9,13},{10,... | collective-permute-start | bytes 1191944 | tf_op jit(solution)/shard_map/ppermute | solution.py:180
  8.0 2.6 %collective-permute-start.2 = (bf16[1552,128]{1,0:T(8,128)(2,1)}, bf16[1552,128]{1,0:T(8,128)(2,1)S(1)}, u32[]{:S(2)}, u32[]{:S(2)}) collective-permute-start(bf16[1552,128]{1,0:T(8,128)(2,1)} %get-tuple-element.36), channel_id=1, source_target_pairs={{0,2},{1,3},{2,0},{3,1},{4,6},{5,7},{6,4},{7,5},{8,10},{9,11},{10,... | collective-permute-start | bytes 1191944 | tf_op jit(solution)/shard_map/ppermute | solution.py:180
  10.7 5.2 %collective-permute-start.1 = (bf16[1552,128]{1,0:T(8,128)(2,1)}, bf16[1552,128]{1,0:T(8,128)(2,1)S(1)}, u32[]{:S(2)}, u32[]{:S(2)}) collective-permute-start(bf16[1552,128]{1,0:T(8,128)(2,1)} %get-tuple-element.34), channel_id=1, source_target_pairs={{0,8},{1,9},{2,10},{3,11},{4,12},{5,13},{6,14},{7,15},{8,0},{9,1},... | collective-permute-start | bytes 1191944 | tf_op jit(solution)/shard_map/ppermute | solution.py:180
  15.8 4.5 %collective-permute-start.3 = (bf16[1552,128]{1,0:T(8,128)(2,1)}, bf16[1552,128]{1,0:T(8,128)(2,1)S(1)}, u32[]{:S(2)}, u32[]{:S(2)}) collective-permute-start(bf16[1552,128]{1,0:T(8,128)(2,1)} %get-tuple-element.38), channel_id=1, source_target_pairs={{0,10},{1,11},{2,8},{3,9},{4,14},{5,15},{6,12},{7,13},{8,2},{9,3},... | collective-permute-start | bytes 1191944 | tf_op jit(solution)/shard_map/ppermute | solution.py:180
  20.3 2.6 %collective-permute-start.4 = (bf16[1552,128]{1,0:T(8,128)(2,1)}, bf16[1552,128]{1,0:T(8,128)(2,1)S(1)}, u32[]{:S(2)}, u32[]{:S(2)}) collective-permute-start(bf16[1552,128]{1,0:T(8,128)(2,1)} %get-tuple-element.40), channel_id=1, source_target_pairs={{0,6},{1,7},{2,4},{3,5},{4,2},{5,3},{6,0},{7,1},{8,14},{9,15},{10,... | collective-permute-start | bytes 1191944 | tf_op jit(solution)/shard_map/ppermute | solution.py:180
  23.0 15.5 %collective-permute-done.refs_3_ = bf16[1552,128]{1,0:T(8,128)(2,1)S(1)} collective-permute-done((bf16[1552,128]{1,0:T(8,128)(2,1)}, bf16[1552,128]{1,0:T(8,128)(2,1)S(1)}, u32[]{:S(2)}, u32[]{:S(2)}) %collective-permute-start) | collective-permute-done | bytes 397344 | tf_op jit(solution)/shard_map/ppermute | solution.py:180
  38.4 5.3 %collective-permute-start.6 = (bf16[1040,128]{1,0:T(8,128)(2,1)}, bf16[1040,128]{1,0:T(8,128)(2,1)S(1)}, u32[]{:S(2)}, u32[]{:S(2)}) collective-permute-start(bf16[1040,128]{1,0:T(8,128)(2,1)} %get-tuple-element.42), channel_id=1, source_target_pairs={{0,14},{1,15},{2,12},{3,13},{4,10},{5,11},{6,8},{7,9},{8,6},{9,7},... | collective-permute-start | bytes 798728 | tf_op jit(solution)/shard_map/ppermute | solution.py:180
  43.7 0.0 collective-permute-done.2.refs_1_
  43.8 1.9 collective-permute-start.5
  45.7 0.6 broadcast_in_dim.12
  46.3 16.6 %all-to-all-start = ((bf16[32,2,128]{2,1,0:T(2,128)(2,1)}), bf16[32,2,128]{2,1,0:T(2,128)(2,1)S(1)}, u32[]{:S(2)}, u32[]{:S(2)}) async-start(bf16[32,2,128]{2,1,0:T(2,128)(2,1)} %broadcast_in_dim.12), calls=%async_computation | async-start | bytes 32768 | tf_op jit(solution)/shard_map/all_to_all | solution.py:199
  62.9 6.0 %all-to-all-done = bf16[32,2,128]{2,1,0:T(2,128)(2,1)S(1)} async-done(((bf16[32,2,128]{2,1,0:T(2,128)(2,1)}), bf16[32,2,128]{2,1,0:T(2,128)(2,1)S(1)}, u32[]{:S(2)}, u32[]{:S(2)}) %all-to-all-start) | async-done | bytes 16416 | tf_op jit(solution)/shard_map/all_to_all | solution.py:199
  68.9 44.7 %collective-permute-done.3.refs_2_ = bf16[1552,128]{1,0:T(8,128)(2,1)S(1)} collective-permute-done((bf16[1552,128]{1,0:T(8,128)(2,1)}, bf16[1552,128]{1,0:T(8,128)(2,1)S(1)}, u32[]{:S(2)}, u32[]{:S(2)}) %collective-permute-start.3) | collective-permute-done | bytes 397344 | tf_op jit(solution)/shard_map/ppermute | solution.py:180
  113.6 0.0 collective-permute-done.4.refs_4_
  113.6 1.0 copy-done
  114.6 0.6 norm.1
  115.3 5.3 %collective-permute-start.7 = (bf16[4,4,512,128]{3,2,1,0:T(8,128)(2,1)S(1)}, bf16[4,4,512,128]{3,2,1,0:T(8,128)(2,1)S(1)}, u32[]{:S(2)}, u32[]{:S(2)}) collective-permute-start(bf16[4,4,512,128]{3,2,1,0:T(8,128)(2,1)S(1)} %get-tuple-element.45.own_ref), channel_id=1, source_target_pairs={{0,1},{1,0},{2,3},{3,2},{4,5},{5,4},{6,7},{7,6},{8,9},{9,8},{10,11... | collective-permute-start | bytes 6291464 | tf_op jit(solution)/shard_map/ppermute | solution.py:184
  120.6 1.9 collective-permute-start.10
  122.6 5.4 %collective-permute-start.11 = (bf16[512,128]{1,0:T(8,128)(2,1)S(1)}, bf16[512,128]{1,0:T(8,128)(2,1)S(1)}, u32[]{:S(2)}, u32[]{:S(2)}) collective-permute-start(bf16[512,128]{1,0:T(8,128)(2,1)S(1)} %copy-done.2), channel_id=1, source_target_pairs={{0,14},{1,15},{2,12},{3,13},{4,10},{5,11},{6,8},{7,9},{8,6},{9,7},... | collective-permute-start | bytes 393224 | tf_op jit(solution)/shard_map/ppermute | solution.py:180
  128.0 5.2 %attend.2 = (bf16[512,128]{1,0:T(8,128)(2,1)S(1)}, bf16[512,128]{1,0:T(8,128)(2,1)S(1)}, bf16[512,128]{1,0:T(8,128)(2,1)S(1)}, bf16[512,128]{1,0:T(8,128)(2,1)S(...) custom-call(bf16[2,4,128]{2,1,0:T(4,128)(2,1)S(1)} %bitcast.15, ...), custom_call_target="tpu_custom_call" | custom-call | tf_op jit(solution)/shard_map/attend/pallas_call | solution.py:246
  133.3 32.4 %collective-permute-start.8 = (bf16[512,128]{1,0:T(8,128)(2,1)S(1)}, bf16[512,128]{1,0:T(8,128)(2,1)S(1)}, u32[]{:S(2)}, u32[]{:S(2)}) collective-permute-start(bf16[512,128]{1,0:T(8,128)(2,1)S(1)} %get-tuple-element.46), channel_id=1, source_target_pairs={{0,8},{1,9},{2,10},{3,11},{4,12},{5,13},{6,14},{7,15},{8,0},{9,1},... | collective-permute-start | bytes 393224 | tf_op jit(solution)/shard_map/ppermute | solution.py:180
  165.7 1.9 collective-permute-start.9
  167.6 2.2 %collective-permute-start.14 = (bf16[512,128]{1,0:T(8,128)(2,1)S(1)}, bf16[512,128]{1,0:T(8,128)(2,1)S(1)}, u32[]{:S(2)}, u32[]{:S(2)}) collective-permute-start(bf16[512,128]{1,0:T(8,128)(2,1)S(1)} %get-tuple-element.52), channel_id=1, source_target_pairs={{0,2},{1,3},{2,0},{3,1},{4,6},{5,7},{6,4},{7,5},{8,10},{9,11},{10,... | collective-permute-start | bytes 393224 | tf_op jit(solution)/shard_map/ppermute | solution.py:180
  169.8 5.3 %collective-permute-start.15 = (bf16[512,128]{1,0:T(8,128)(2,1)S(1)}, bf16[512,128]{1,0:T(8,128)(2,1)S(1)}, u32[]{:S(2)}, u32[]{:S(2)}) collective-permute-start(bf16[512,128]{1,0:T(8,128)(2,1)S(1)} %get-tuple-element.53), channel_id=1, source_target_pairs={{0,4},{1,5},{2,6},{3,7},{4,0},{5,1},{6,2},{7,3},{8,12},{9,13},{10,... | collective-permute-start | bytes 393224 | tf_op jit(solution)/shard_map/ppermute | solution.py:180
  175.1 3.1 %collective-permute-start.16 = (bf16[512,128]{1,0:T(8,128)(2,1)S(1)}, bf16[512,128]{1,0:T(8,128)(2,1)S(1)}, u32[]{:S(2)}, u32[]{:S(2)}) collective-permute-start(bf16[512,128]{1,0:T(8,128)(2,1)S(1)} %get-tuple-element.54), channel_id=1, source_target_pairs={{0,6},{1,7},{2,4},{3,5},{4,2},{5,3},{6,0},{7,1},{8,14},{9,15},{10,... | collective-permute-start | bytes 393224 | tf_op jit(solution)/shard_map/ppermute | solution.py:180
  178.2 2.8 %attend.3 = (bf16[512,128]{1,0:T(8,128)(2,1)S(1)}, bf16[512,128]{1,0:T(8,128)(2,1)S(1)}) custom-call(bf16[2,4,128]{2,1,0:T(4,128)(2,1)S(1)} %bitcast.16, f32[512,128]{1,0:T(8,128)S(1)} %get-tuple-element.44.table_ref, bf16[4,4,512,128]{3,2,1,0:T(8,128)(2,1)S(1)} %get-tuple-element.45.own_ref, bf16[4,4,512,128]{3,2,1,0:T(8,128)(2,1)S(1)} %collective-permute-done.7.other_ref, ...), custom_call_target="tpu_custom_call" | custom-call | tf_op jit(solution)/shard_map/attend/pallas_call | solution.py:246
  181.0 5.0 %collective-permute-done.8.refs_0_ = bf16[512,128]{1,0:T(8,128)(2,1)S(1)} collective-permute-done((bf16[512,128]{1,0:T(8,128)(2,1)S(1)}, bf16[512,128]{1,0:T(8,128)(2,1)S(1)}, u32[]{:S(2)}, u32[]{:S(2)}) %collective-permute-start.8) | collective-permute-done | bytes 131104 | tf_op jit(solution)/shard_map/ppermute | solution.py:180
  186.1 1.9 collective-permute-start.12
  188.0 5.5 %collective-permute-start.13 = (bf16[512,128]{1,0:T(8,128)(2,1)S(1)}, bf16[512,128]{1,0:T(8,128)(2,1)S(1)}, u32[]{:S(2)}, u32[]{:S(2)}) collective-permute-start(bf16[512,128]{1,0:T(8,128)(2,1)S(1)} %get-tuple-element.51), channel_id=1, source_target_pairs={{0,14},{1,15},{2,12},{3,13},{4,10},{5,11},{6,8},{7,9},{8,6},{9,7},... | collective-permute-start | bytes 393224 | tf_op jit(solution)/shard_map/ppermute | solution.py:180
  193.6 17.8 %collective-permute-done.16.refs_6_ = bf16[512,128]{1,0:T(8,128)(2,1)S(1)} collective-permute-done((bf16[512,128]{1,0:T(8,128)(2,1)S(1)}, bf16[512,128]{1,0:T(8,128)(2,1)S(1)}, u32[]{:S(2)}, u32[]{:S(2)}) %collective-permute-start.16) | collective-permute-done | bytes 131104 | tf_op jit(solution)/shard_map/ppermute | solution.py:180
  211.3 1.2 unpack.1
  (25 shorter events, 0.1 us)
Async XLA Ops:
  0.6 45.0 %copy-start.4 = (bf16[128]{0:T(256)(128)(2,1)S(1)}, bf16[128]{0:T(256)(128)(2,1)}, u32[]{:S(2)}) copy-start(bf16[128]{0:T(256)(128)(2,1)} %param.15) | copy-start | bytes 772
  0.6 45.0 %copy-start.5 = (bf16[128]{0:T(256)(128)(2,1)S(1)}, bf16[128]{0:T(256)(128)(2,1)}, u32[]{:S(2)}) copy-start(bf16[128]{0:T(256)(128)(2,1)} %param.14) | copy-start | bytes 772
  4.9 33.5 %collective-permute-start = (bf16[1552,128]{1,0:T(8,128)(2,1)}, bf16[1552,128]{1,0:T(8,128)(2,1)S(1)}, u32[]{:S(2)}, u32[]{:S(2)}) collective-permute-start(bf16[1552,128]{1,0:T(8,128)(2,1)} %get-tuple-element.31), channel_id=1, source_target_pairs={{0,4},{1,5},{2,6},{3,7},{4,0},{5,1},{6,2},{7,3},{8,12},{9,13},{10,... | collective-permute-start | bytes 1191944 | tf_op jit(solution)/shard_map/ppermute | solution.py:180
  8.0 35.7 %collective-permute-start.2 = (bf16[1552,128]{1,0:T(8,128)(2,1)}, bf16[1552,128]{1,0:T(8,128)(2,1)S(1)}, u32[]{:S(2)}, u32[]{:S(2)}) collective-permute-start(bf16[1552,128]{1,0:T(8,128)(2,1)} %get-tuple-element.36), channel_id=1, source_target_pairs={{0,2},{1,3},{2,0},{3,1},{4,6},{5,7},{6,4},{7,5},{8,10},{9,11},{10,... | collective-permute-start | bytes 1191944 | tf_op jit(solution)/shard_map/ppermute | solution.py:180
  10.7 58.2 %collective-permute-start.1 = (bf16[1552,128]{1,0:T(8,128)(2,1)}, bf16[1552,128]{1,0:T(8,128)(2,1)S(1)}, u32[]{:S(2)}, u32[]{:S(2)}) collective-permute-start(bf16[1552,128]{1,0:T(8,128)(2,1)} %get-tuple-element.34), channel_id=1, source_target_pairs={{0,8},{1,9},{2,10},{3,11},{4,12},{5,13},{6,14},{7,15},{8,0},{9,1},... | collective-permute-start | bytes 1191944 | tf_op jit(solution)/shard_map/ppermute | solution.py:180
  15.8 97.8 %collective-permute-start.3 = (bf16[1552,128]{1,0:T(8,128)(2,1)}, bf16[1552,128]{1,0:T(8,128)(2,1)S(1)}, u32[]{:S(2)}, u32[]{:S(2)}) collective-permute-start(bf16[1552,128]{1,0:T(8,128)(2,1)} %get-tuple-element.38), channel_id=1, source_target_pairs={{0,10},{1,11},{2,8},{3,9},{4,14},{5,15},{6,12},{7,13},{8,2},{9,3},... | collective-permute-start | bytes 1191944 | tf_op jit(solution)/shard_map/ppermute | solution.py:180
  20.3 93.3 %collective-permute-start.4 = (bf16[1552,128]{1,0:T(8,128)(2,1)}, bf16[1552,128]{1,0:T(8,128)(2,1)S(1)}, u32[]{:S(2)}, u32[]{:S(2)}) collective-permute-start(bf16[1552,128]{1,0:T(8,128)(2,1)} %get-tuple-element.40), channel_id=1, source_target_pairs={{0,6},{1,7},{2,4},{3,5},{4,2},{5,3},{6,0},{7,1},{8,14},{9,15},{10,... | collective-permute-start | bytes 1191944 | tf_op jit(solution)/shard_map/ppermute | solution.py:180
  38.4 75.2 %collective-permute-start.6 = (bf16[1040,128]{1,0:T(8,128)(2,1)}, bf16[1040,128]{1,0:T(8,128)(2,1)S(1)}, u32[]{:S(2)}, u32[]{:S(2)}) collective-permute-start(bf16[1040,128]{1,0:T(8,128)(2,1)} %get-tuple-element.42), channel_id=1, source_target_pairs={{0,14},{1,15},{2,12},{3,13},{4,10},{5,11},{6,8},{7,9},{8,6},{9,7},... | collective-permute-start | bytes 798728 | tf_op jit(solution)/shard_map/ppermute | solution.py:180
  43.8 69.9 %collective-permute-start.5 = (bf16[1040,128]{1,0:T(8,128)(2,1)}, bf16[1040,128]{1,0:T(8,128)(2,1)S(1)}, u32[]{:S(2)}, u32[]{:S(2)}) collective-permute-start(bf16[1040,128]{1,0:T(8,128)(2,1)} %get-tuple-element.41), channel_id=1, source_target_pairs={{0,12},{1,13},{2,14},{3,15},{4,8},{5,9},{6,10},{7,11},{8,4},{9,5},... | collective-permute-start | bytes 798728 | tf_op jit(solution)/shard_map/ppermute | solution.py:180
  46.3 22.6 %all-to-all-start = ((bf16[32,2,128]{2,1,0:T(2,128)(2,1)}), bf16[32,2,128]{2,1,0:T(2,128)(2,1)S(1)}, u32[]{:S(2)}, u32[]{:S(2)}) async-start(bf16[32,2,128]{2,1,0:T(2,128)(2,1)} %broadcast_in_dim.12), calls=%async_computation | async-start | bytes 32768 | tf_op jit(solution)/shard_map/all_to_all | solution.py:199
  113.6 1.0 copy-start
  114.6 6.0 %copy-start.3 = (bf16[512,128]{1,0:T(8,128)(2,1)S(1)}, bf16[512,128]{1,0:T(8,128)(2,1)}, u32[]{:S(2)}) copy-start(bf16[512,128]{1,0:T(8,128)(2,1)} %get-tuple-element.48) | copy-start | bytes 393220
  114.6 7.9 %copy-start.2 = (bf16[512,128]{1,0:T(8,128)(2,1)S(1)}, bf16[512,128]{1,0:T(8,128)(2,1)}, u32[]{:S(2)}) copy-start(bf16[512,128]{1,0:T(8,128)(2,1)} %get-tuple-element.49) | copy-start | bytes 393220
  114.6 13.4 %copy-start.1 = (bf16[1552,128]{1,0:T(8,128)(2,1)S(1)}, bf16[1552,128]{1,0:T(8,128)(2,1)}, u32[]{:S(2)}) copy-start(bf16[1552,128]{1,0:T(8,128)(2,1)} %get-tuple-element.43.refs_7_.refs_5_) | copy-start | bytes 1191940
  115.3 12.7 %collective-permute-start.7 = (bf16[4,4,512,128]{3,2,1,0:T(8,128)(2,1)S(1)}, bf16[4,4,512,128]{3,2,1,0:T(8,128)(2,1)S(1)}, u32[]{:S(2)}, u32[]{:S(2)}) collective-permute-start(bf16[4,4,512,128]{3,2,1,0:T(8,128)(2,1)S(1)} %get-tuple-element.45.own_ref), channel_id=1, source_target_pairs={{0,1},{1,0},{2,3},{3,2},{4,5},{5,4},{6,7},{7,6},{8,9},{9,8},{10,11... | collective-permute-start | bytes 6291464 | tf_op jit(solution)/shard_map/ppermute | solution.py:184
  120.6 49.1 %collective-permute-start.10 = (bf16[512,128]{1,0:T(8,128)(2,1)S(1)}, bf16[512,128]{1,0:T(8,128)(2,1)S(1)}, u32[]{:S(2)}, u32[]{:S(2)}) collective-permute-start(bf16[512,128]{1,0:T(8,128)(2,1)S(1)} %copy-done.3), channel_id=1, source_target_pairs={{0,12},{1,13},{2,14},{3,15},{4,8},{5,9},{6,10},{7,11},{8,4},{9,5},... | collective-permute-start | bytes 393224 | tf_op jit(solution)/shard_map/ppermute | solution.py:180
  122.6 52.6 %collective-permute-start.11 = (bf16[512,128]{1,0:T(8,128)(2,1)S(1)}, bf16[512,128]{1,0:T(8,128)(2,1)S(1)}, u32[]{:S(2)}, u32[]{:S(2)}) collective-permute-start(bf16[512,128]{1,0:T(8,128)(2,1)S(1)} %copy-done.2), channel_id=1, source_target_pairs={{0,14},{1,15},{2,12},{3,13},{4,10},{5,11},{6,8},{7,9},{8,6},{9,7},... | collective-permute-start | bytes 393224 | tf_op jit(solution)/shard_map/ppermute | solution.py:180
  133.3 52.8 %collective-permute-start.8 = (bf16[512,128]{1,0:T(8,128)(2,1)S(1)}, bf16[512,128]{1,0:T(8,128)(2,1)S(1)}, u32[]{:S(2)}, u32[]{:S(2)}) collective-permute-start(bf16[512,128]{1,0:T(8,128)(2,1)S(1)} %get-tuple-element.46), channel_id=1, source_target_pairs={{0,8},{1,9},{2,10},{3,11},{4,12},{5,13},{6,14},{7,15},{8,0},{9,1},... | collective-permute-start | bytes 393224 | tf_op jit(solution)/shard_map/ppermute | solution.py:180
  165.7 22.3 %collective-permute-start.9 = (bf16[512,128]{1,0:T(8,128)(2,1)S(1)}, bf16[512,128]{1,0:T(8,128)(2,1)S(1)}, u32[]{:S(2)}, u32[]{:S(2)}) collective-permute-start(bf16[512,128]{1,0:T(8,128)(2,1)S(1)} %get-tuple-element.47), channel_id=1, source_target_pairs={{0,10},{1,11},{2,8},{3,9},{4,14},{5,15},{6,12},{7,13},{8,2},{9,3},... | collective-permute-start | bytes 393224 | tf_op jit(solution)/shard_map/ppermute | solution.py:180
  167.6 26.0 %collective-permute-start.14 = (bf16[512,128]{1,0:T(8,128)(2,1)S(1)}, bf16[512,128]{1,0:T(8,128)(2,1)S(1)}, u32[]{:S(2)}, u32[]{:S(2)}) collective-permute-start(bf16[512,128]{1,0:T(8,128)(2,1)S(1)} %get-tuple-element.52), channel_id=1, source_target_pairs={{0,2},{1,3},{2,0},{3,1},{4,6},{5,7},{6,4},{7,5},{8,10},{9,11},{10,... | collective-permute-start | bytes 393224 | tf_op jit(solution)/shard_map/ppermute | solution.py:180
  169.8 23.8 %collective-permute-start.15 = (bf16[512,128]{1,0:T(8,128)(2,1)S(1)}, bf16[512,128]{1,0:T(8,128)(2,1)S(1)}, u32[]{:S(2)}, u32[]{:S(2)}) collective-permute-start(bf16[512,128]{1,0:T(8,128)(2,1)S(1)} %get-tuple-element.53), channel_id=1, source_target_pairs={{0,4},{1,5},{2,6},{3,7},{4,0},{5,1},{6,2},{7,3},{8,12},{9,13},{10,... | collective-permute-start | bytes 393224 | tf_op jit(solution)/shard_map/ppermute | solution.py:180
  175.1 36.2 %collective-permute-start.16 = (bf16[512,128]{1,0:T(8,128)(2,1)S(1)}, bf16[512,128]{1,0:T(8,128)(2,1)S(1)}, u32[]{:S(2)}, u32[]{:S(2)}) collective-permute-start(bf16[512,128]{1,0:T(8,128)(2,1)S(1)} %get-tuple-element.54), channel_id=1, source_target_pairs={{0,6},{1,7},{2,4},{3,5},{4,2},{5,3},{6,0},{7,1},{8,14},{9,15},{10,... | collective-permute-start | bytes 393224 | tf_op jit(solution)/shard_map/ppermute | solution.py:180
  186.1 25.3 %collective-permute-start.12 = (bf16[512,128]{1,0:T(8,128)(2,1)S(1)}, bf16[512,128]{1,0:T(8,128)(2,1)S(1)}, u32[]{:S(2)}, u32[]{:S(2)}) collective-permute-start(bf16[512,128]{1,0:T(8,128)(2,1)S(1)} %get-tuple-element.50), channel_id=1, source_target_pairs={{0,12},{1,13},{2,14},{3,15},{4,8},{5,9},{6,10},{7,11},{8,4},{9,5},... | collective-permute-start | bytes 393224 | tf_op jit(solution)/shard_map/ppermute | solution.py:180
  188.0 23.3 %collective-permute-start.13 = (bf16[512,128]{1,0:T(8,128)(2,1)S(1)}, bf16[512,128]{1,0:T(8,128)(2,1)S(1)}, u32[]{:S(2)}, u32[]{:S(2)}) collective-permute-start(bf16[512,128]{1,0:T(8,128)(2,1)S(1)} %get-tuple-element.51), channel_id=1, source_target_pairs={{0,14},{1,15},{2,12},{3,13},{4,10},{5,11},{6,8},{7,9},{8,6},{9,7},... | collective-permute-start | bytes 393224 | tf_op jit(solution)/shard_map/ppermute | solution.py:180

commit v4 on v3

--- a/solution.py
+++ b/solution.py
@@ -15,7 +15,9 @@
 BLOCK = HEADS_PER_CHIP * TOKENS
 STAT_ROWS = 16
 ARRAYS = 6
-STEPS = (4, 1, 5, 2, 3, 6, 7, 0)
+STEPS = (5, 1, 6, 3, 2, 4, 7, 0)
+GATES = (None, None, None, None, None, 1, 3, None)
+GAINS_GATE = 3
 LATE = (5, 6)
 EARLY = (0, 1, 2, 3, 4, 7)
 ORDER = (0, 2, 5, 6, 1, 3, 4, 7)
@@ -217,15 +219,16 @@
         name="pack",
     )(chip_ref, k, kd, v, vd, q, qd)
     blocks, late = blocks[:CHIPS], blocks[CHIPS:]
-    arrived = send(blocks[:5])
-    for place, gate in zip(LATE, (1, 3)):
-        block, arrived[gate] = after(blocks[place], arrived[gate])
-        arrived.append(exchange(block, STEPS[place]))
-    arrived.append(blocks[7])
+    arrived = []
+    for place, gate in enumerate(GATES):
+        block = blocks[place]
+        if gate is not None:
+            block, arrived[gate] = after(block, arrived[gate])
+        arrived.append(exchange(block, STEPS[place]) if STEPS[place] else block)
     late = [exchange(block, STEPS[place]) for block, place in zip(late, LATE)]
 
     gains = jnp.stack([query_gain, key_gain])
-    gains, arrived[3] = after(gains, arrived[3])
+    gains, arrived[GAINS_GATE] = after(gains, arrived[GAINS_GATE])
     gains = gather_gains(gains, chip)
 
     many = CHIPS * TOKENS

time: 213 us -> 223 us (1.047)
  the two profiles are of different devices: /device:TPU:491 before, /device:TPU:8 now
where the time goes in v4:
time: 223 us
  starting transfers between devices  144 us (65%)
  waiting for transfers between devices  61.6 us (28%)
  Pallas kernels  14.1 us (6%)
    ppermute x16, starting transfers between devices, exchange(): return lax.ppermute(block, 'ctx', pairs)  135 us
    ppermute x16, waiting for transfers between devices, exchange(): return lax.ppermute(block, 'ctx', pairs)  45.8 us
    all_to_all x1, waiting for transfers between devices, gather_gains(): gains = lax.all_to_all(gains, 'dp', 0, 0, tiled=True)  15.7 us
    pallas_call x2, Pallas kernels, attend(): pl.pallas_call(functools.partial(attend_kernel, places), out_shape=[shape...  8 us
    all_to_all x1, starting transfers between devices, gather_gains(): gains = lax.all_to_all(gains, 'dp', 0, 0, tiled=True)  7.53 us
  transfers between devices with their start and end apart: 18, of which 4 were waited for; matrix products, arithmetic and copies ran while one was open for 0% of the time, Pallas kernels for 4%

profile of v4, /device:TPU:8, one launch (start us, length us, event | category | flops | bytes accessed | tf_op | source)
XLA Modules:
  0.0 222.8 jit_solution(5913966681082002282)
XLA Ops:
  0.7 4.3 %pack.1 = (bf16[1552,128]{1,0:T(8,128)(2,1)}, bf16[1552,128]{1,0:T(8,128)(2,1)}, bf16[1552,128]{1,0:T(8,128)(2,1)}, bf16[1552,128]{1,0:T(8,128)(2,1)}, bf16[1552...) custom-call(s32[1]{0:T(128)} %bitcast.chip_ref, ...), custom_call_target="tpu_custom_call" | custom-call | tf_op jit(solution)/shard_map/pack/pallas_call | solution.py:212
  4.9 6.5 %collective-permute-start = (bf16[1552,128]{1,0:T(8,128)(2,1)}, bf16[1552,128]{1,0:T(8,128)(2,1)S(1)}, u32[]{:S(2)}, u32[]{:S(2)}) collective-permute-start(bf16[1552,128]{1,0:T(8,128)(2,1)} %get-tuple-element.31), channel_id=1, source_target_pairs={{0,6},{1,7},{2,4},{3,5},{4,2},{5,3},{6,0},{7,1},{8,14},{9,15},{10,... | collective-permute-start | bytes 1191944 | tf_op jit(solution)/shard_map/ppermute | solution.py:182
  11.5 1.9 collective-permute-start.2
  13.4 10.5 %collective-permute-start.1 = (bf16[1552,128]{1,0:T(8,128)(2,1)}, bf16[1552,128]{1,0:T(8,128)(2,1)S(1)}, u32[]{:S(2)}, u32[]{:S(2)}) collective-permute-start(bf16[1552,128]{1,0:T(8,128)(2,1)} %get-tuple-element.34), channel_id=1, source_target_pairs={{0,10},{1,11},{2,8},{3,9},{4,14},{5,15},{6,12},{7,13},{8,2},{9,3},... | collective-permute-start | bytes 1191944 | tf_op jit(solution)/shard_map/ppermute | solution.py:182
  24.0 1.9 collective-permute-start.3
  25.9 1.9 collective-permute-start.4
  27.8 0.0 collective-permute-done.refs_3_
  27.8 41.6 %collective-permute-start.6 = (bf16[1040,128]{1,0:T(8,128)(2,1)}, bf16[1040,128]{1,0:T(8,128)(2,1)S(1)}, u32[]{:S(2)}, u32[]{:S(2)}) collective-permute-start(bf16[1040,128]{1,0:T(8,128)(2,1)} %get-tuple-element.42), channel_id=1, source_target_pairs={{0,14},{1,15},{2,12},{3,13},{4,10},{5,11},{6,8},{7,9},{8,6},{9,7},... | collective-permute-start | bytes 798728 | tf_op jit(solution)/shard_map/ppermute | solution.py:182
  69.5 31.7 %collective-permute-start.5 = (bf16[1040,128]{1,0:T(8,128)(2,1)}, bf16[1040,128]{1,0:T(8,128)(2,1)S(1)}, u32[]{:S(2)}, u32[]{:S(2)}) collective-permute-start(bf16[1040,128]{1,0:T(8,128)(2,1)} %get-tuple-element.41), channel_id=1, source_target_pairs={{0,8},{1,9},{2,10},{3,11},{4,12},{5,13},{6,14},{7,15},{8,0},{9,1},... | collective-permute-start | bytes 798728 | tf_op jit(solution)/shard_map/ppermute | solution.py:182
  101.2 0.6 broadcast_in_dim.12
  101.8 7.5 %all-to-all-start = ((bf16[32,2,128]{2,1,0:T(2,128)(2,1)}), bf16[32,2,128]{2,1,0:T(2,128)(2,1)S(1)}, u32[]{:S(2)}, u32[]{:S(2)}) async-start(bf16[32,2,128]{2,1,0:T(2,128)(2,1)} %broadcast_in_dim.12), calls=%async_computation | async-start | bytes 32768 | tf_op jit(solution)/shard_map/all_to_all | solution.py:201
  109.4 15.7 %all-to-all-done = bf16[32,2,128]{2,1,0:T(2,128)(2,1)S(1)} async-done(((bf16[32,2,128]{2,1,0:T(2,128)(2,1)}), bf16[32,2,128]{2,1,0:T(2,128)(2,1)S(1)}, u32[]{:S(2)}, u32[]{:S(2)}) %all-to-all-start) | async-done | bytes 16416 | tf_op jit(solution)/shard_map/all_to_all | solution.py:201
  125.2 0.0 collective-permute-done.6.refs_6_
  125.2 12.5 %collective-permute-done.5.refs_5_ = bf16[1040,128]{1,0:T(8,128)(2,1)S(1)} collective-permute-done((bf16[1040,128]{1,0:T(8,128)(2,1)}, bf16[1040,128]{1,0:T(8,128)(2,1)S(1)}, u32[]{:S(2)}, u32[]{:S(2)}) %collective-permute-start.5) | collective-permute-done | bytes 266272 | tf_op jit(solution)/shard_map/ppermute | solution.py:182
  137.7 1.0 copy-done
  138.7 0.6 norm.1
  139.3 1.9 collective-permute-start.7
  141.3 1.9 collective-permute-start.10
  143.2 7.5 %collective-permute-start.11 = (bf16[512,128]{1,0:T(8,128)(2,1)S(1)}, bf16[512,128]{1,0:T(8,128)(2,1)S(1)}, u32[]{:S(2)}, u32[]{:S(2)}) collective-permute-start(bf16[512,128]{1,0:T(8,128)(2,1)S(1)} %copy-done.2), channel_id=1, source_target_pairs={{0,14},{1,15},{2,12},{3,13},{4,10},{5,11},{6,8},{7,9},{8,6},{9,7},... | collective-permute-start | bytes 393224 | tf_op jit(solution)/shard_map/ppermute | solution.py:182
  150.8 5.2 %attend.2 = (bf16[512,128]{1,0:T(8,128)(2,1)S(1)}, bf16[512,128]{1,0:T(8,128)(2,1)S(1)}, bf16[512,128]{1,0:T(8,128)(2,1)S(1)}, bf16[512,128]{1,0:T(8,128)(2,1)S(...) custom-call(bf16[2,4,128]{2,1,0:T(4,128)(2,1)S(1)} %bitcast.15, ...), custom_call_target="tpu_custom_call" | custom-call | tf_op jit(solution)/shard_map/attend/pallas_call | solution.py:249
  156.0 4.6 %collective-permute-start.8 = (bf16[512,128]{1,0:T(8,128)(2,1)S(1)}, bf16[512,128]{1,0:T(8,128)(2,1)S(1)}, u32[]{:S(2)}, u32[]{:S(2)}) collective-permute-start(bf16[512,128]{1,0:T(8,128)(2,1)S(1)} %get-tuple-element.46), channel_id=1, source_target_pairs={{0,10},{1,11},{2,8},{3,9},{4,14},{5,15},{6,12},{7,13},{8,2},{9,3},... | collective-permute-start | bytes 393224 | tf_op jit(solution)/shard_map/ppermute | solution.py:182
  160.6 5.5 %collective-permute-start.9 = (bf16[512,128]{1,0:T(8,128)(2,1)S(1)}, bf16[512,128]{1,0:T(8,128)(2,1)S(1)}, u32[]{:S(2)}, u32[]{:S(2)}) collective-permute-start(bf16[512,128]{1,0:T(8,128)(2,1)S(1)} %get-tuple-element.47), channel_id=1, source_target_pairs={{0,12},{1,13},{2,14},{3,15},{4,8},{5,9},{6,10},{7,11},{8,4},{9,5},... | collective-permute-start | bytes 393224 | tf_op jit(solution)/shard_map/ppermute | solution.py:182
  166.1 2.5 %collective-permute-start.14 = (bf16[512,128]{1,0:T(8,128)(2,1)S(1)}, bf16[512,128]{1,0:T(8,128)(2,1)S(1)}, u32[]{:S(2)}, u32[]{:S(2)}) collective-permute-start(bf16[512,128]{1,0:T(8,128)(2,1)S(1)} %get-tuple-element.52), channel_id=1, source_target_pairs={{0,2},{1,3},{2,0},{3,1},{4,6},{5,7},{6,4},{7,5},{8,10},{9,11},{10,... | collective-permute-start | bytes 393224 | tf_op jit(solution)/shard_map/ppermute | solution.py:182
  168.6 17.6 %collective-permute-done.10.refs_0_ = bf16[512,128]{1,0:T(8,128)(2,1)S(1)} collective-permute-done((bf16[512,128]{1,0:T(8,128)(2,1)S(1)}, bf16[512,128]{1,0:T(8,128)(2,1)S(1)}, u32[]{:S(2)}, u32[]{:S(2)}) %collective-permute-start.10) | collective-permute-done | bytes 131104 | tf_op jit(solution)/shard_map/ppermute | solution.py:182
  186.2 1.9 collective-permute-start.15
  188.2 1.9 collective-permute-start.16
  190.1 2.8 %attend.3 = (bf16[512,128]{1,0:T(8,128)(2,1)S(1)}, bf16[512,128]{1,0:T(8,128)(2,1)S(1)}) custom-call(bf16[2,4,128]{2,1,0:T(4,128)(2,1)S(1)} %bitcast.16, f32[512,128]{1,0:T(8,128)S(1)} %get-tuple-element.44.table_ref, bf16[4,4,512,128]{3,2,1,0:T(8,128)(2,1)S(1)} %get-tuple-element.45.own_ref, bf16[4,4,512,128]{3,2,1,0:T(8,128)(2,1)S(1)} %collective-permute-done.7.other_ref, ...), custom_call_target="tpu_custom_call" | custom-call | tf_op jit(solution)/shard_map/attend/pallas_call | solution.py:249
  192.9 0.0 collective-permute-done.8.refs_0_
  192.9 5.9 %collective-permute-start.12 = (bf16[512,128]{1,0:T(8,128)(2,1)S(1)}, bf16[512,128]{1,0:T(8,128)(2,1)S(1)}, u32[]{:S(2)}, u32[]{:S(2)}) collective-permute-start(bf16[512,128]{1,0:T(8,128)(2,1)S(1)} %get-tuple-element.50), channel_id=1, source_target_pairs={{0,8},{1,9},{2,10},{3,11},{4,12},{5,13},{6,14},{7,15},{8,0},{9,1},... | collective-permute-start | bytes 393224 | tf_op jit(solution)/shard_map/ppermute | solution.py:182
  198.8 7.1 %collective-permute-start.13 = (bf16[512,128]{1,0:T(8,128)(2,1)S(1)}, bf16[512,128]{1,0:T(8,128)(2,1)S(1)}, u32[]{:S(2)}, u32[]{:S(2)}) collective-permute-start(bf16[512,128]{1,0:T(8,128)(2,1)S(1)} %get-tuple-element.51), channel_id=1, source_target_pairs={{0,14},{1,15},{2,12},{3,13},{4,10},{5,11},{6,8},{7,9},{8,6},{9,7},... | collective-permute-start | bytes 393224 | tf_op jit(solution)/shard_map/ppermute | solution.py:182
  205.9 15.6 %collective-permute-done.12.refs_2_ = bf16[512,128]{1,0:T(8,128)(2,1)S(1)} collective-permute-done((bf16[512,128]{1,0:T(8,128)(2,1)S(1)}, bf16[512,128]{1,0:T(8,128)(2,1)S(1)}, u32[]{:S(2)}, u32[]{:S(2)}) %collective-permute-start.12) | collective-permute-done | bytes 131104 | tf_op jit(solution)/shard_map/ppermute | solution.py:182
  221.5 1.2 unpack.1
  (25 shorter events, 0.1 us)
Async XLA Ops:
  0.6 100.5 %copy-start.4 = (bf16[128]{0:T(256)(128)(2,1)S(1)}, bf16[128]{0:T(256)(128)(2,1)}, u32[]{:S(2)}) copy-start(bf16[128]{0:T(256)(128)(2,1)} %param.15) | copy-start | bytes 772
  0.6 100.5 %copy-start.5 = (bf16[128]{0:T(256)(128)(2,1)S(1)}, bf16[128]{0:T(256)(128)(2,1)}, u32[]{:S(2)}) copy-start(bf16[128]{0:T(256)(128)(2,1)} %param.14) | copy-start | bytes 772
  4.9 22.9 %collective-permute-start = (bf16[1552,128]{1,0:T(8,128)(2,1)}, bf16[1552,128]{1,0:T(8,128)(2,1)S(1)}, u32[]{:S(2)}, u32[]{:S(2)}) collective-permute-start(bf16[1552,128]{1,0:T(8,128)(2,1)} %get-tuple-element.31), channel_id=1, source_target_pairs={{0,6},{1,7},{2,4},{3,5},{4,2},{5,3},{6,0},{7,1},{8,14},{9,15},{10,... | collective-permute-start | bytes 1191944 | tf_op jit(solution)/shard_map/ppermute | solution.py:182
  11.5 58.0 %collective-permute-start.2 = (bf16[1552,128]{1,0:T(8,128)(2,1)}, bf16[1552,128]{1,0:T(8,128)(2,1)S(1)}, u32[]{:S(2)}, u32[]{:S(2)}) collective-permute-start(bf16[1552,128]{1,0:T(8,128)(2,1)} %get-tuple-element.36), channel_id=1, source_target_pairs={{0,2},{1,3},{2,0},{3,1},{4,6},{5,7},{6,4},{7,5},{8,10},{9,11},{10,... | collective-permute-start | bytes 1191944 | tf_op jit(solution)/shard_map/ppermute | solution.py:182
  13.4 111.7 %collective-permute-start.1 = (bf16[1552,128]{1,0:T(8,128)(2,1)}, bf16[1552,128]{1,0:T(8,128)(2,1)S(1)}, u32[]{:S(2)}, u32[]{:S(2)}) collective-permute-start(bf16[1552,128]{1,0:T(8,128)(2,1)} %get-tuple-element.34), channel_id=1, source_target_pairs={{0,10},{1,11},{2,8},{3,9},{4,14},{5,15},{6,12},{7,13},{8,2},{9,3},... | collective-permute-start | bytes 1191944 | tf_op jit(solution)/shard_map/ppermute | solution.py:182
  24.0 101.2 %collective-permute-start.3 = (bf16[1552,128]{1,0:T(8,128)(2,1)}, bf16[1552,128]{1,0:T(8,128)(2,1)S(1)}, u32[]{:S(2)}, u32[]{:S(2)}) collective-permute-start(bf16[1552,128]{1,0:T(8,128)(2,1)} %get-tuple-element.38), channel_id=1, source_target_pairs={{0,12},{1,13},{2,14},{3,15},{4,8},{5,9},{6,10},{7,11},{8,4},{9,5},... | collective-permute-start | bytes 1191944 | tf_op jit(solution)/shard_map/ppermute | solution.py:182
  25.9 99.3 %collective-permute-start.4 = (bf16[1552,128]{1,0:T(8,128)(2,1)}, bf16[1552,128]{1,0:T(8,128)(2,1)S(1)}, u32[]{:S(2)}, u32[]{:S(2)}) collective-permute-start(bf16[1552,128]{1,0:T(8,128)(2,1)} %get-tuple-element.40), channel_id=1, source_target_pairs={{0,4},{1,5},{2,6},{3,7},{4,0},{5,1},{6,2},{7,3},{8,12},{9,13},{10,... | collective-permute-start | bytes 1191944 | tf_op jit(solution)/shard_map/ppermute | solution.py:182
  27.8 97.3 %collective-permute-start.6 = (bf16[1040,128]{1,0:T(8,128)(2,1)}, bf16[1040,128]{1,0:T(8,128)(2,1)S(1)}, u32[]{:S(2)}, u32[]{:S(2)}) collective-permute-start(bf16[1040,128]{1,0:T(8,128)(2,1)} %get-tuple-element.42), channel_id=1, source_target_pairs={{0,14},{1,15},{2,12},{3,13},{4,10},{5,11},{6,8},{7,9},{8,6},{9,7},... | collective-permute-start | bytes 798728 | tf_op jit(solution)/shard_map/ppermute | solution.py:182
  69.5 68.2 %collective-permute-start.5 = (bf16[1040,128]{1,0:T(8,128)(2,1)}, bf16[1040,128]{1,0:T(8,128)(2,1)S(1)}, u32[]{:S(2)}, u32[]{:S(2)}) collective-permute-start(bf16[1040,128]{1,0:T(8,128)(2,1)} %get-tuple-element.41), channel_id=1, source_target_pairs={{0,8},{1,9},{2,10},{3,11},{4,12},{5,13},{6,14},{7,15},{8,0},{9,1},... | collective-permute-start | bytes 798728 | tf_op jit(solution)/shard_map/ppermute | solution.py:182
  101.8 23.3 %all-to-all-start = ((bf16[32,2,128]{2,1,0:T(2,128)(2,1)}), bf16[32,2,128]{2,1,0:T(2,128)(2,1)S(1)}, u32[]{:S(2)}, u32[]{:S(2)}) async-start(bf16[32,2,128]{2,1,0:T(2,128)(2,1)} %broadcast_in_dim.12), calls=%async_computation | async-start | bytes 32768 | tf_op jit(solution)/shard_map/all_to_all | solution.py:201
  137.7 1.0 copy-start
  138.7 2.6 %copy-start.3 = (bf16[512,128]{1,0:T(8,128)(2,1)S(1)}, bf16[512,128]{1,0:T(8,128)(2,1)}, u32[]{:S(2)}) copy-start(bf16[512,128]{1,0:T(8,128)(2,1)} %get-tuple-element.48) | copy-start | bytes 393220
  138.7 4.5 %copy-start.2 = (bf16[512,128]{1,0:T(8,128)(2,1)S(1)}, bf16[512,128]{1,0:T(8,128)(2,1)}, u32[]{:S(2)}) copy-start(bf16[512,128]{1,0:T(8,128)(2,1)} %get-tuple-element.49) | copy-start | bytes 393220
  138.7 12.1 %copy-start.1 = (bf16[1552,128]{1,0:T(8,128)(2,1)S(1)}, bf16[1552,128]{1,0:T(8,128)(2,1)}, u32[]{:S(2)}) copy-start(bf16[1552,128]{1,0:T(8,128)(2,1)} %get-tuple-element.43.refs_7_.refs_5_) | copy-start | bytes 1191940
  139.3 11.4 %collective-permute-start.7 = (bf16[4,4,512,128]{3,2,1,0:T(8,128)(2,1)S(1)}, bf16[4,4,512,128]{3,2,1,0:T(8,128)(2,1)S(1)}, u32[]{:S(2)}, u32[]{:S(2)}) collective-permute-start(bf16[4,4,512,128]{3,2,1,0:T(8,128)(2,1)S(1)} %get-tuple-element.45.own_ref), channel_id=1, source_target_pairs={{0,1},{1,0},{2,3},{3,2},{4,5},{5,4},{6,7},{7,6},{8,9},{9,8},{10,11... | collective-permute-start | bytes 6291464 | tf_op jit(solution)/shard_map/ppermute | solution.py:186
  141.3 45.0 %collective-permute-start.10 = (bf16[512,128]{1,0:T(8,128)(2,1)S(1)}, bf16[512,128]{1,0:T(8,128)(2,1)S(1)}, u32[]{:S(2)}, u32[]{:S(2)}) collective-permute-start(bf16[512,128]{1,0:T(8,128)(2,1)S(1)} %copy-done.3), channel_id=1, source_target_pairs={{0,8},{1,9},{2,10},{3,11},{4,12},{5,13},{6,14},{7,15},{8,0},{9,1},... | collective-permute-start | bytes 393224 | tf_op jit(solution)/shard_map/ppermute | solution.py:182
  143.2 44.9 %collective-permute-start.11 = (bf16[512,128]{1,0:T(8,128)(2,1)S(1)}, bf16[512,128]{1,0:T(8,128)(2,1)S(1)}, u32[]{:S(2)}, u32[]{:S(2)}) collective-permute-start(bf16[512,128]{1,0:T(8,128)(2,1)S(1)} %copy-done.2), channel_id=1, source_target_pairs={{0,14},{1,15},{2,12},{3,13},{4,10},{5,11},{6,8},{7,9},{8,6},{9,7},... | collective-permute-start | bytes 393224 | tf_op jit(solution)/shard_map/ppermute | solution.py:182
  156.0 36.9 %collective-permute-start.8 = (bf16[512,128]{1,0:T(8,128)(2,1)S(1)}, bf16[512,128]{1,0:T(8,128)(2,1)S(1)}, u32[]{:S(2)}, u32[]{:S(2)}) collective-permute-start(bf16[512,128]{1,0:T(8,128)(2,1)S(1)} %get-tuple-element.46), channel_id=1, source_target_pairs={{0,10},{1,11},{2,8},{3,9},{4,14},{5,15},{6,12},{7,13},{8,2},{9,3},... | collective-permute-start | bytes 393224 | tf_op jit(solution)/shard_map/ppermute | solution.py:182
  160.6 38.3 %collective-permute-start.9 = (bf16[512,128]{1,0:T(8,128)(2,1)S(1)}, bf16[512,128]{1,0:T(8,128)(2,1)S(1)}, u32[]{:S(2)}, u32[]{:S(2)}) collective-permute-start(bf16[512,128]{1,0:T(8,128)(2,1)S(1)} %get-tuple-element.47), channel_id=1, source_target_pairs={{0,12},{1,13},{2,14},{3,15},{4,8},{5,9},{6,10},{7,11},{8,4},{9,5},... | collective-permute-start | bytes 393224 | tf_op jit(solution)/shard_map/ppermute | solution.py:182
  166.1 39.8 %collective-permute-start.14 = (bf16[512,128]{1,0:T(8,128)(2,1)S(1)}, bf16[512,128]{1,0:T(8,128)(2,1)S(1)}, u32[]{:S(2)}, u32[]{:S(2)}) collective-permute-start(bf16[512,128]{1,0:T(8,128)(2,1)S(1)} %get-tuple-element.52), channel_id=1, source_target_pairs={{0,2},{1,3},{2,0},{3,1},{4,6},{5,7},{6,4},{7,5},{8,10},{9,11},{10,... | collective-permute-start | bytes 393224 | tf_op jit(solution)/shard_map/ppermute | solution.py:182
  186.2 19.7 %collective-permute-start.15 = (bf16[512,128]{1,0:T(8,128)(2,1)S(1)}, bf16[512,128]{1,0:T(8,128)(2,1)S(1)}, u32[]{:S(2)}, u32[]{:S(2)}) collective-permute-start(bf16[512,128]{1,0:T(8,128)(2,1)S(1)} %get-tuple-element.53), channel_id=1, source_target_pairs={{0,6},{1,7},{2,4},{3,5},{4,2},{5,3},{6,0},{7,1},{8,14},{9,15},{10,... | collective-permute-start | bytes 393224 | tf_op jit(solution)/shard_map/ppermute | solution.py:182
  188.2 17.8 %collective-permute-start.16 = (bf16[512,128]{1,0:T(8,128)(2,1)S(1)}, bf16[512,128]{1,0:T(8,128)(2,1)S(1)}, u32[]{:S(2)}, u32[]{:S(2)}) collective-permute-start(bf16[512,128]{1,0:T(8,128)(2,1)S(1)} %get-tuple-element.54), channel_id=1, source_target_pairs={{0,4},{1,5},{2,6},{3,7},{4,0},{5,1},{6,2},{7,3},{8,12},{9,13},{10,... | collective-permute-start | bytes 393224 | tf_op jit(solution)/shard_map/ppermute | solution.py:182
  192.9 28.7 %collective-permute-start.12 = (bf16[512,128]{1,0:T(8,128)(2,1)S(1)}, bf16[512,128]{1,0:T(8,128)(2,1)S(1)}, u32[]{:S(2)}, u32[]{:S(2)}) collective-permute-start(bf16[512,128]{1,0:T(8,128)(2,1)S(1)} %get-tuple-element.50), channel_id=1, source_target_pairs={{0,8},{1,9},{2,10},{3,11},{4,12},{5,13},{6,14},{7,15},{8,0},{9,1},... | collective-permute-start | bytes 393224 | tf_op jit(solution)/shard_map/ppermute | solution.py:182
  198.8 22.7 %collective-permute-start.13 = (bf16[512,128]{1,0:T(8,128)(2,1)S(1)}, bf16[512,128]{1,0:T(8,128)(2,1)S(1)}, u32[]{:S(2)}, u32[]{:S(2)}) collective-permute-start(bf16[512,128]{1,0:T(8,128)(2,1)S(1)} %get-tuple-element.51), channel_id=1, source_target_pairs={{0,14},{1,15},{2,12},{3,13},{4,10},{5,11},{6,8},{7,9},{8,6},{9,7},... | collective-permute-start | bytes 393224 | tf_op jit(solution)/shard_map/ppermute | solution.py:182

commit v5 on v4

--- a/solution.py
+++ b/solution.py
@@ -15,7 +15,7 @@
 BLOCK = HEADS_PER_CHIP * TOKENS
 STAT_ROWS = 16
 ARRAYS = 6
-STEPS = (5, 1, 6, 3, 2, 4, 7, 0)
+STEPS = (4, 1, 5, 2, 3, 7, 6, 0)
 GATES = (None, None, None, None, None, 1, 3, None)
 GAINS_GATE = 3
 LATE = (5, 6)

time: 223 us -> 213 us (0.955)
  the two profiles are of different devices: /device:TPU:8 before, /device:TPU:1 now
where the time goes in v5:
time: 213 us; the launch traced here: 212 us
  starting transfers between devices  111 us (52%)
  waiting for transfers between devices  83.6 us (39%)
  Pallas kernels  14.1 us (7%)
    ppermute x16, starting transfers between devices, exchange(): return lax.ppermute(block, 'ctx', pairs)  90.4 us
    ppermute x16, waiting for transfers between devices, exchange(): return lax.ppermute(block, 'ctx', pairs)  67.7 us
    all_to_all x1, starting transfers between devices, gather_gains(): gains = lax.all_to_all(gains, 'dp', 0, 0, tiled=True)  16.2 us
    all_to_all x1, waiting for transfers between devices, gather_gains(): gains = lax.all_to_all(gains, 'dp', 0, 0, tiled=True)  15.9 us
    pallas_call x2, Pallas kernels, attend(): pl.pallas_call(functools.partial(attend_kernel, places), out_shape=[shape...  8 us
    ppermute x1, starting transfers between devices, swap(): lax.ppermute(block, 'ctx', [(place, place ^ 1) for place in range(2 * CHI...  4.86 us
    pallas_call x1, Pallas kernels, local(): pl.pallas_call(pack_kernel, out_shape=[shape(size * BLOCK + STAT_ROWS, HE...  4.28 us
  transfers between devices with their start and end apart: 18, of which 5 were waited for; matrix products, arithmetic and copies ran while one was open for 0% of the time, Pallas kernels for 4%

profile of v5, /device:TPU:1, one launch (start us, length us, event | category | flops | bytes accessed | tf_op | source)
XLA Modules:
  0.0 211.8 jit_solution(1087260696510488650)
XLA Ops:
  0.7 4.3 %pack.1 = (bf16[1552,128]{1,0:T(8,128)(2,1)}, bf16[1552,128]{1,0:T(8,128)(2,1)}, bf16[1552,128]{1,0:T(8,128)(2,1)}, bf16[1552,128]{1,0:T(8,128)(2,1)}, bf16[1552...) custom-call(s32[1]{0:T(128)} %bitcast.chip_ref, ...), custom_call_target="tpu_custom_call" | custom-call | tf_op jit(solution)/shard_map/pack/pallas_call | solution.py:212
  4.9 5.7 %collective-permute-start = (bf16[1552,128]{1,0:T(8,128)(2,1)}, bf16[1552,128]{1,0:T(8,128)(2,1)S(1)}, u32[]{:S(2)}, u32[]{:S(2)}) collective-permute-start(bf16[1552,128]{1,0:T(8,128)(2,1)} %get-tuple-element.31), channel_id=1, source_target_pairs={{0,4},{1,5},{2,6},{3,7},{4,0},{5,1},{6,2},{7,3},{8,12},{9,13},{10,... | collective-permute-start | bytes 1191944 | tf_op jit(solution)/shard_map/ppermute | solution.py:182
  10.7 3.5 %collective-permute-start.2 = (bf16[1552,128]{1,0:T(8,128)(2,1)}, bf16[1552,128]{1,0:T(8,128)(2,1)S(1)}, u32[]{:S(2)}, u32[]{:S(2)}) collective-permute-start(bf16[1552,128]{1,0:T(8,128)(2,1)} %get-tuple-element.36), channel_id=1, source_target_pairs={{0,2},{1,3},{2,0},{3,1},{4,6},{5,7},{6,4},{7,5},{8,10},{9,11},{10,... | collective-permute-start | bytes 1191944 | tf_op jit(solution)/shard_map/ppermute | solution.py:182
  14.2 8.8 %collective-permute-start.1 = (bf16[1552,128]{1,0:T(8,128)(2,1)}, bf16[1552,128]{1,0:T(8,128)(2,1)S(1)}, u32[]{:S(2)}, u32[]{:S(2)}) collective-permute-start(bf16[1552,128]{1,0:T(8,128)(2,1)} %get-tuple-element.34), channel_id=1, source_target_pairs={{0,8},{1,9},{2,10},{3,11},{4,12},{5,13},{6,14},{7,15},{8,0},{9,1},... | collective-permute-start | bytes 1191944 | tf_op jit(solution)/shard_map/ppermute | solution.py:182
  23.0 1.9 collective-permute-start.3
  25.0 1.9 collective-permute-start.4
  26.9 12.1 %collective-permute-done.refs_3_ = bf16[1552,128]{1,0:T(8,128)(2,1)S(1)} collective-permute-done((bf16[1552,128]{1,0:T(8,128)(2,1)}, bf16[1552,128]{1,0:T(8,128)(2,1)S(1)}, u32[]{:S(2)}, u32[]{:S(2)}) %collective-permute-start) | collective-permute-done | bytes 397344 | tf_op jit(solution)/shard_map/ppermute | solution.py:182
  39.0 1.9 collective-permute-start.6
  40.9 0.0 collective-permute-done.2.refs_1_
  40.9 9.8 %collective-permute-start.5 = (bf16[1040,128]{1,0:T(8,128)(2,1)}, bf16[1040,128]{1,0:T(8,128)(2,1)S(1)}, u32[]{:S(2)}, u32[]{:S(2)}) collective-permute-start(bf16[1040,128]{1,0:T(8,128)(2,1)} %get-tuple-element.41), channel_id=1, source_target_pairs={{0,14},{1,15},{2,12},{3,13},{4,10},{5,11},{6,8},{7,9},{8,6},{9,7},... | collective-permute-start | bytes 798728 | tf_op jit(solution)/shard_map/ppermute | solution.py:182
  50.8 0.6 broadcast_in_dim.12
  51.4 16.2 %all-to-all-start = ((bf16[32,2,128]{2,1,0:T(2,128)(2,1)}), bf16[32,2,128]{2,1,0:T(2,128)(2,1)S(1)}, u32[]{:S(2)}, u32[]{:S(2)}) async-start(bf16[32,2,128]{2,1,0:T(2,128)(2,1)} %broadcast_in_dim.12), calls=%async_computation | async-start | bytes 32768 | tf_op jit(solution)/shard_map/all_to_all | solution.py:201
  67.5 15.9 %all-to-all-done = bf16[32,2,128]{2,1,0:T(2,128)(2,1)S(1)} async-done(((bf16[32,2,128]{2,1,0:T(2,128)(2,1)}), bf16[32,2,128]{2,1,0:T(2,128)(2,1)S(1)}, u32[]{:S(2)}, u32[]{:S(2)}) %all-to-all-start) | async-done | bytes 16416 | tf_op jit(solution)/shard_map/all_to_all | solution.py:201
  83.5 0.0 collective-permute-done.1.refs_0_
  83.5 35.9 %collective-permute-done.3.refs_2_ = bf16[1552,128]{1,0:T(8,128)(2,1)S(1)} collective-permute-done((bf16[1552,128]{1,0:T(8,128)(2,1)}, bf16[1552,128]{1,0:T(8,128)(2,1)S(1)}, u32[]{:S(2)}, u32[]{:S(2)}) %collective-permute-start.3) | collective-permute-done | bytes 397344 | tf_op jit(solution)/shard_map/ppermute | solution.py:182
  119.4 1.0 copy-done
  120.4 0.6 norm.1
  121.0 4.9 %collective-permute-start.7 = (bf16[4,4,512,128]{3,2,1,0:T(8,128)(2,1)S(1)}, bf16[4,4,512,128]{3,2,1,0:T(8,128)(2,1)S(1)}, u32[]{:S(2)}, u32[]{:S(2)}) collective-permute-start(bf16[4,4,512,128]{3,2,1,0:T(8,128)(2,1)S(1)} %get-tuple-element.45.own_ref), channel_id=1, source_target_pairs={{0,1},{1,0},{2,3},{3,2},{4,5},{5,4},{6,7},{7,6},{8,9},{9,8},{10,11... | collective-permute-start | bytes 6291464 | tf_op jit(solution)/shard_map/ppermute | solution.py:186
  125.9 3.4 %collective-permute-start.10 = (bf16[512,128]{1,0:T(8,128)(2,1)S(1)}, bf16[512,128]{1,0:T(8,128)(2,1)S(1)}, u32[]{:S(2)}, u32[]{:S(2)}) collective-permute-start(bf16[512,128]{1,0:T(8,128)(2,1)S(1)} %copy-done.3), channel_id=1, source_target_pairs={{0,14},{1,15},{2,12},{3,13},{4,10},{5,11},{6,8},{7,9},{8,6},{9,7},... | collective-permute-start | bytes 393224 | tf_op jit(solution)/shard_map/ppermute | solution.py:182
  129.3 11.4 %collective-permute-start.11 = (bf16[512,128]{1,0:T(8,128)(2,1)S(1)}, bf16[512,128]{1,0:T(8,128)(2,1)S(1)}, u32[]{:S(2)}, u32[]{:S(2)}) collective-permute-start(bf16[512,128]{1,0:T(8,128)(2,1)S(1)} %copy-done.2), channel_id=1, source_target_pairs={{0,12},{1,13},{2,14},{3,15},{4,8},{5,9},{6,10},{7,11},{8,4},{9,5},... | collective-permute-start | bytes 393224 | tf_op jit(solution)/shard_map/ppermute | solution.py:182
  140.7 5.2 %attend.2 = (bf16[512,128]{1,0:T(8,128)(2,1)S(1)}, bf16[512,128]{1,0:T(8,128)(2,1)S(1)}, bf16[512,128]{1,0:T(8,128)(2,1)S(1)}, bf16[512,128]{1,0:T(8,128)(2,1)S(...) custom-call(bf16[2,4,128]{2,1,0:T(4,128)(2,1)S(1)} %bitcast.15, ...), custom_call_target="tpu_custom_call" | custom-call | tf_op jit(solution)/shard_map/attend/pallas_call | solution.py:249
  146.0 20.5 %collective-permute-start.8 = (bf16[512,128]{1,0:T(8,128)(2,1)S(1)}, bf16[512,128]{1,0:T(8,128)(2,1)S(1)}, u32[]{:S(2)}, u32[]{:S(2)}) collective-permute-start(bf16[512,128]{1,0:T(8,128)(2,1)S(1)} %get-tuple-element.46), channel_id=1, source_target_pairs={{0,8},{1,9},{2,10},{3,11},{4,12},{5,13},{6,14},{7,15},{8,0},{9,1},... | collective-permute-start | bytes 393224 | tf_op jit(solution)/shard_map/ppermute | solution.py:182
  166.5 1.9 collective-permute-start.9
  168.4 2.2 %collective-permute-start.14 = (bf16[512,128]{1,0:T(8,128)(2,1)S(1)}, bf16[512,128]{1,0:T(8,128)(2,1)S(1)}, u32[]{:S(2)}, u32[]{:S(2)}) collective-permute-start(bf16[512,128]{1,0:T(8,128)(2,1)S(1)} %get-tuple-element.52), channel_id=1, source_target_pairs={{0,2},{1,3},{2,0},{3,1},{4,6},{5,7},{6,4},{7,5},{8,10},{9,11},{10,... | collective-permute-start | bytes 393224 | tf_op jit(solution)/shard_map/ppermute | solution.py:182
  170.6 6.5 %collective-permute-start.15 = (bf16[512,128]{1,0:T(8,128)(2,1)S(1)}, bf16[512,128]{1,0:T(8,128)(2,1)S(1)}, u32[]{:S(2)}, u32[]{:S(2)}) collective-permute-start(bf16[512,128]{1,0:T(8,128)(2,1)S(1)} %get-tuple-element.53), channel_id=1, source_target_pairs={{0,4},{1,5},{2,6},{3,7},{4,0},{5,1},{6,2},{7,3},{8,12},{9,13},{10,... | collective-permute-start | bytes 393224 | tf_op jit(solution)/shard_map/ppermute | solution.py:182
  177.2 3.1 %collective-permute-start.16 = (bf16[512,128]{1,0:T(8,128)(2,1)S(1)}, bf16[512,128]{1,0:T(8,128)(2,1)S(1)}, u32[]{:S(2)}, u32[]{:S(2)}) collective-permute-start(bf16[512,128]{1,0:T(8,128)(2,1)S(1)} %get-tuple-element.54), channel_id=1, source_target_pairs={{0,6},{1,7},{2,4},{3,5},{4,2},{5,3},{6,0},{7,1},{8,14},{9,15},{10,... | collective-permute-start | bytes 393224 | tf_op jit(solution)/shard_map/ppermute | solution.py:182
  180.2 2.8 %attend.3 = (bf16[512,128]{1,0:T(8,128)(2,1)S(1)}, bf16[512,128]{1,0:T(8,128)(2,1)S(1)}) custom-call(bf16[2,4,128]{2,1,0:T(4,128)(2,1)S(1)} %bitcast.16, f32[512,128]{1,0:T(8,128)S(1)} %get-tuple-element.44.table_ref, bf16[4,4,512,128]{3,2,1,0:T(8,128)(2,1)S(1)} %get-tuple-element.45.own_ref, bf16[4,4,512,128]{3,2,1,0:T(8,128)(2,1)S(1)} %collective-permute-done.7.other_ref, ...), custom_call_target="tpu_custom_call" | custom-call | tf_op jit(solution)/shard_map/attend/pallas_call | solution.py:249
  183.0 4.2 %collective-permute-done.8.refs_0_ = bf16[512,128]{1,0:T(8,128)(2,1)S(1)} collective-permute-done((bf16[512,128]{1,0:T(8,128)(2,1)S(1)}, bf16[512,128]{1,0:T(8,128)(2,1)S(1)}, u32[]{:S(2)}, u32[]{:S(2)}) %collective-permute-start.8) | collective-permute-done | bytes 131104 | tf_op jit(solution)/shard_map/ppermute | solution.py:182
  187.2 5.9 %collective-permute-start.12 = (bf16[512,128]{1,0:T(8,128)(2,1)S(1)}, bf16[512,128]{1,0:T(8,128)(2,1)S(1)}, u32[]{:S(2)}, u32[]{:S(2)}) collective-permute-start(bf16[512,128]{1,0:T(8,128)(2,1)S(1)} %get-tuple-element.50), channel_id=1, source_target_pairs={{0,14},{1,15},{2,12},{3,13},{4,10},{5,11},{6,8},{7,9},{8,6},{9,7},... | collective-permute-start | bytes 393224 | tf_op jit(solution)/shard_map/ppermute | solution.py:182
  193.1 1.9 collective-permute-start.13
  195.1 15.5 %collective-permute-done.16.refs_6_ = bf16[512,128]{1,0:T(8,128)(2,1)S(1)} collective-permute-done((bf16[512,128]{1,0:T(8,128)(2,1)S(1)}, bf16[512,128]{1,0:T(8,128)(2,1)S(1)}, u32[]{:S(2)}, u32[]{:S(2)}) %collective-permute-start.16) | collective-permute-done | bytes 131104 | tf_op jit(solution)/shard_map/ppermute | solution.py:182
  210.6 1.2 unpack.1
  (25 shorter events, 0.1 us)
Async XLA Ops:
  0.6 50.1 %copy-start.4 = (bf16[128]{0:T(256)(128)(2,1)S(1)}, bf16[128]{0:T(256)(128)(2,1)}, u32[]{:S(2)}) copy-start(bf16[128]{0:T(256)(128)(2,1)} %param.15) | copy-start | bytes 772
  0.6 50.1 %copy-start.5 = (bf16[128]{0:T(256)(128)(2,1)S(1)}, bf16[128]{0:T(256)(128)(2,1)}, u32[]{:S(2)}) copy-start(bf16[128]{0:T(256)(128)(2,1)} %param.14) | copy-start | bytes 772
  4.9 34.1 %collective-permute-start = (bf16[1552,128]{1,0:T(8,128)(2,1)}, bf16[1552,128]{1,0:T(8,128)(2,1)S(1)}, u32[]{:S(2)}, u32[]{:S(2)}) collective-permute-start(bf16[1552,128]{1,0:T(8,128)(2,1)} %get-tuple-element.31), channel_id=1, source_target_pairs={{0,4},{1,5},{2,6},{3,7},{4,0},{5,1},{6,2},{7,3},{8,12},{9,13},{10,... | collective-permute-start | bytes 1191944 | tf_op jit(solution)/shard_map/ppermute | solution.py:182
  10.7 30.3 %collective-permute-start.2 = (bf16[1552,128]{1,0:T(8,128)(2,1)}, bf16[1552,128]{1,0:T(8,128)(2,1)S(1)}, u32[]{:S(2)}, u32[]{:S(2)}) collective-permute-start(bf16[1552,128]{1,0:T(8,128)(2,1)} %get-tuple-element.36), channel_id=1, source_target_pairs={{0,2},{1,3},{2,0},{3,1},{4,6},{5,7},{6,4},{7,5},{8,10},{9,11},{10,... | collective-permute-start | bytes 1191944 | tf_op jit(solution)/shard_map/ppermute | solution.py:182
  14.2 69.3 %collective-permute-start.1 = (bf16[1552,128]{1,0:T(8,128)(2,1)}, bf16[1552,128]{1,0:T(8,128)(2,1)S(1)}, u32[]{:S(2)}, u32[]{:S(2)}) collective-permute-start(bf16[1552,128]{1,0:T(8,128)(2,1)} %get-tuple-element.34), channel_id=1, source_target_pairs={{0,8},{1,9},{2,10},{3,11},{4,12},{5,13},{6,14},{7,15},{8,0},{9,1},... | collective-permute-start | bytes 1191944 | tf_op jit(solution)/shard_map/ppermute | solution.py:182
  23.0 96.3 %collective-permute-start.3 = (bf16[1552,128]{1,0:T(8,128)(2,1)}, bf16[1552,128]{1,0:T(8,128)(2,1)S(1)}, u32[]{:S(2)}, u32[]{:S(2)}) collective-permute-start(bf16[1552,128]{1,0:T(8,128)(2,1)} %get-tuple-element.38), channel_id=1, source_target_pairs={{0,10},{1,11},{2,8},{3,9},{4,14},{5,15},{6,12},{7,13},{8,2},{9,3},... | collective-permute-start | bytes 1191944 | tf_op jit(solution)/shard_map/ppermute | solution.py:182
  25.0 94.4 %collective-permute-start.4 = (bf16[1552,128]{1,0:T(8,128)(2,1)}, bf16[1552,128]{1,0:T(8,128)(2,1)S(1)}, u32[]{:S(2)}, u32[]{:S(2)}) collective-permute-start(bf16[1552,128]{1,0:T(8,128)(2,1)} %get-tuple-element.40), channel_id=1, source_target_pairs={{0,6},{1,7},{2,4},{3,5},{4,2},{5,3},{6,0},{7,1},{8,14},{9,15},{10,... | collective-permute-start | bytes 1191944 | tf_op jit(solution)/shard_map/ppermute | solution.py:182
  39.0 80.4 %collective-permute-start.6 = (bf16[1040,128]{1,0:T(8,128)(2,1)}, bf16[1040,128]{1,0:T(8,128)(2,1)S(1)}, u32[]{:S(2)}, u32[]{:S(2)}) collective-permute-start(bf16[1040,128]{1,0:T(8,128)(2,1)} %get-tuple-element.42), channel_id=1, source_target_pairs={{0,12},{1,13},{2,14},{3,15},{4,8},{5,9},{6,10},{7,11},{8,4},{9,5},... | collective-permute-start | bytes 798728 | tf_op jit(solution)/shard_map/ppermute | solution.py:182
  40.9 78.5 %collective-permute-start.5 = (bf16[1040,128]{1,0:T(8,128)(2,1)}, bf16[1040,128]{1,0:T(8,128)(2,1)S(1)}, u32[]{:S(2)}, u32[]{:S(2)}) collective-permute-start(bf16[1040,128]{1,0:T(8,128)(2,1)} %get-tuple-element.41), channel_id=1, source_target_pairs={{0,14},{1,15},{2,12},{3,13},{4,10},{5,11},{6,8},{7,9},{8,6},{9,7},... | collective-permute-start | bytes 798728 | tf_op jit(solution)/shard_map/ppermute | solution.py:182
  51.4 32.1 %all-to-all-start = ((bf16[32,2,128]{2,1,0:T(2,128)(2,1)}), bf16[32,2,128]{2,1,0:T(2,128)(2,1)S(1)}, u32[]{:S(2)}, u32[]{:S(2)}) async-start(bf16[32,2,128]{2,1,0:T(2,128)(2,1)} %broadcast_in_dim.12), calls=%async_computation | async-start | bytes 32768 | tf_op jit(solution)/shard_map/all_to_all | solution.py:201
  119.4 1.0 copy-start
  120.4 5.5 %copy-start.3 = (bf16[512,128]{1,0:T(8,128)(2,1)S(1)}, bf16[512,128]{1,0:T(8,128)(2,1)}, u32[]{:S(2)}) copy-start(bf16[512,128]{1,0:T(8,128)(2,1)} %get-tuple-element.48) | copy-start | bytes 393220
  120.4 8.9 %copy-start.2 = (bf16[512,128]{1,0:T(8,128)(2,1)S(1)}, bf16[512,128]{1,0:T(8,128)(2,1)}, u32[]{:S(2)}) copy-start(bf16[512,128]{1,0:T(8,128)(2,1)} %get-tuple-element.49) | copy-start | bytes 393220
  120.4 20.3 %copy-start.1 = (bf16[1552,128]{1,0:T(8,128)(2,1)S(1)}, bf16[1552,128]{1,0:T(8,128)(2,1)}, u32[]{:S(2)}) copy-start(bf16[1552,128]{1,0:T(8,128)(2,1)} %get-tuple-element.43.refs_7_.refs_5_) | copy-start | bytes 1191940
  121.0 19.7 %collective-permute-start.7 = (bf16[4,4,512,128]{3,2,1,0:T(8,128)(2,1)S(1)}, bf16[4,4,512,128]{3,2,1,0:T(8,128)(2,1)S(1)}, u32[]{:S(2)}, u32[]{:S(2)}) collective-permute-start(bf16[4,4,512,128]{3,2,1,0:T(8,128)(2,1)S(1)} %get-tuple-element.45.own_ref), channel_id=1, source_target_pairs={{0,1},{1,0},{2,3},{3,2},{4,5},{5,4},{6,7},{7,6},{8,9},{9,8},{10,11... | collective-permute-start | bytes 6291464 | tf_op jit(solution)/shard_map/ppermute | solution.py:186
  125.9 44.7 %collective-permute-start.10 = (bf16[512,128]{1,0:T(8,128)(2,1)S(1)}, bf16[512,128]{1,0:T(8,128)(2,1)S(1)}, u32[]{:S(2)}, u32[]{:S(2)}) collective-permute-start(bf16[512,128]{1,0:T(8,128)(2,1)S(1)} %copy-done.3), channel_id=1, source_target_pairs={{0,14},{1,15},{2,12},{3,13},{4,10},{5,11},{6,8},{7,9},{8,6},{9,7},... | collective-permute-start | bytes 393224 | tf_op jit(solution)/shard_map/ppermute | solution.py:182
  129.3 47.8 %collective-permute-start.11 = (bf16[512,128]{1,0:T(8,128)(2,1)S(1)}, bf16[512,128]{1,0:T(8,128)(2,1)S(1)}, u32[]{:S(2)}, u32[]{:S(2)}) collective-permute-start(bf16[512,128]{1,0:T(8,128)(2,1)S(1)} %copy-done.2), channel_id=1, source_target_pairs={{0,12},{1,13},{2,14},{3,15},{4,8},{5,9},{6,10},{7,11},{8,4},{9,5},... | collective-permute-start | bytes 393224 | tf_op jit(solution)/shard_map/ppermute | solution.py:182
  146.0 41.2 %collective-permute-start.8 = (bf16[512,128]{1,0:T(8,128)(2,1)S(1)}, bf16[512,128]{1,0:T(8,128)(2,1)S(1)}, u32[]{:S(2)}, u32[]{:S(2)}) collective-permute-start(bf16[512,128]{1,0:T(8,128)(2,1)S(1)} %get-tuple-element.46), channel_id=1, source_target_pairs={{0,8},{1,9},{2,10},{3,11},{4,12},{5,13},{6,14},{7,15},{8,0},{9,1},... | collective-permute-start | bytes 393224 | tf_op jit(solution)/shard_map/ppermute | solution.py:182
  166.5 26.6 %collective-permute-start.9 = (bf16[512,128]{1,0:T(8,128)(2,1)S(1)}, bf16[512,128]{1,0:T(8,128)(2,1)S(1)}, u32[]{:S(2)}, u32[]{:S(2)}) collective-permute-start(bf16[512,128]{1,0:T(8,128)(2,1)S(1)} %get-tuple-element.47), channel_id=1, source_target_pairs={{0,10},{1,11},{2,8},{3,9},{4,14},{5,15},{6,12},{7,13},{8,2},{9,3},... | collective-permute-start | bytes 393224 | tf_op jit(solution)/shard_map/ppermute | solution.py:182
  168.4 26.7 %collective-permute-start.14 = (bf16[512,128]{1,0:T(8,128)(2,1)S(1)}, bf16[512,128]{1,0:T(8,128)(2,1)S(1)}, u32[]{:S(2)}, u32[]{:S(2)}) collective-permute-start(bf16[512,128]{1,0:T(8,128)(2,1)S(1)} %get-tuple-element.52), channel_id=1, source_target_pairs={{0,2},{1,3},{2,0},{3,1},{4,6},{5,7},{6,4},{7,5},{8,10},{9,11},{10,... | collective-permute-start | bytes 393224 | tf_op jit(solution)/shard_map/ppermute | solution.py:182
  170.6 24.5 %collective-permute-start.15 = (bf16[512,128]{1,0:T(8,128)(2,1)S(1)}, bf16[512,128]{1,0:T(8,128)(2,1)S(1)}, u32[]{:S(2)}, u32[]{:S(2)}) collective-permute-start(bf16[512,128]{1,0:T(8,128)(2,1)S(1)} %get-tuple-element.53), channel_id=1, source_target_pairs={{0,4},{1,5},{2,6},{3,7},{4,0},{5,1},{6,2},{7,3},{8,12},{9,13},{10,... | collective-permute-start | bytes 393224 | tf_op jit(solution)/shard_map/ppermute | solution.py:182
  177.2 33.5 %collective-permute-start.16 = (bf16[512,128]{1,0:T(8,128)(2,1)S(1)}, bf16[512,128]{1,0:T(8,128)(2,1)S(1)}, u32[]{:S(2)}, u32[]{:S(2)}) collective-permute-start(bf16[512,128]{1,0:T(8,128)(2,1)S(1)} %get-tuple-element.54), channel_id=1, source_target_pairs={{0,6},{1,7},{2,4},{3,5},{4,2},{5,3},{6,0},{7,1},{8,14},{9,15},{10,... | collective-permute-start | bytes 393224 | tf_op jit(solution)/shard_map/ppermute | solution.py:182
  187.2 23.4 %collective-permute-start.12 = (bf16[512,128]{1,0:T(8,128)(2,1)S(1)}, bf16[512,128]{1,0:T(8,128)(2,1)S(1)}, u32[]{:S(2)}, u32[]{:S(2)}) collective-permute-start(bf16[512,128]{1,0:T(8,128)(2,1)S(1)} %get-tuple-element.50), channel_id=1, source_target_pairs={{0,14},{1,15},{2,12},{3,13},{4,10},{5,11},{6,8},{7,9},{8,6},{9,7},... | collective-permute-start | bytes 393224 | tf_op jit(solution)/shard_map/ppermute | solution.py:182
  193.1 17.5 %collective-permute-start.13 = (bf16[512,128]{1,0:T(8,128)(2,1)S(1)}, bf16[512,128]{1,0:T(8,128)(2,1)S(1)}, u32[]{:S(2)}, u32[]{:S(2)}) collective-permute-start(bf16[512,128]{1,0:T(8,128)(2,1)S(1)} %get-tuple-element.51), channel_id=1, source_target_pairs={{0,12},{1,13},{2,14},{3,15},{4,8},{5,9},{6,10},{7,11},{8,4},{9,5},... | collective-permute-start | bytes 393224 | tf_op jit(solution)/shard_map/ppermute | solution.py:182

commit v6 on v5

--- a/solution.py
+++ b/solution.py
@@ -96,14 +96,34 @@
 
 
 def pack_kernel(chip_ref, *refs):
-    arrays, outs, late = refs[:ARRAYS], refs[ARRAYS : ARRAYS + CHIPS], refs[ARRAYS + CHIPS :]
+    sources, refs = refs[:ARRAYS], refs[ARRAYS:]
+    count = CHIPS + len(LATE)
+    targets, arrays, blocks = refs[:count], refs[count : count + ARRAYS], refs[count + ARRAYS : -2]
+    loaded, stored = refs[-2:]
+    loads = [
+        pltpu.make_async_copy(source, array, loaded.at[index])
+        for index, (source, array) in enumerate(zip(sources, arrays))
+    ]
+    for index in (4, 5, 0, 1, 2, 3):
+        loads[index].start()
+    for index in (4, 5, 0, 1):
+        loads[index].wait()
     stats = statistics((arrays[4:], arrays[:2]))
-    for place, out in enumerate(outs):
-        kept = arrays[:4] if place in LATE else arrays
-        copy_columns(chip_ref[0], kept, out, place)
-        out[len(kept) * BLOCK :, :] = stats
-    for place, out in zip(LATE, late):
-        copy_columns(chip_ref[0], arrays[4:], out, place)
+    for index in (2, 3):
+        loads[index].wait()
+    stores = []
+    for index, (block, target) in enumerate(zip(blocks, targets)):
+        if index < CHIPS:
+            kept = arrays[:4] if index in LATE else arrays
+            copy_columns(chip_ref[0], kept, block, index)
+            block[len(kept) * BLOCK :, :] = stats
+        else:
+            copy_columns(chip_ref[0], arrays[4:], block, LATE[index - CHIPS])
+        store = pltpu.make_async_copy(block, target, stored.at[index])
+        store.start()
+        stores.append(store)
+    for store in stores:
+        store.wait()
 
 
 def norm_kernel(gain_ref, *refs):
@@ -208,16 +228,20 @@
     chip = (lax.axis_index("ctx") // 2).astype(jnp.int32)
     chip_ref = chip.reshape(1)
 
-    sizes = [4 if place in LATE else ARRAYS for place in range(CHIPS)]
+    sizes = [4 * BLOCK + STAT_ROWS if place in LATE else ARRAYS * BLOCK + STAT_ROWS for place in range(CHIPS)]
+    sizes += [2 * BLOCK] * len(LATE)
+    arrays = (k, kd, v, vd, q, qd)
     blocks = pl.pallas_call(
         pack_kernel,
-        out_shape=[shape(size * BLOCK + STAT_ROWS, HEAD_DIM) for size in sizes]
-        + [shape(2 * BLOCK, HEAD_DIM)] * len(LATE),
-        in_specs=smem() + vmem(ARRAYS),
-        out_specs=vmem(CHIPS + len(LATE)),
+        out_shape=[shape(size, HEAD_DIM) for size in sizes],
+        in_specs=smem() + [pl.BlockSpec(memory_space=pl.ANY)] * ARRAYS,
+        out_specs=[pl.BlockSpec(memory_space=pl.ANY)] * len(sizes),
+        scratch_shapes=[pltpu.VMEM(array.shape, array.dtype) for array in arrays]
+        + [pltpu.VMEM((size, HEAD_DIM), jnp.bfloat16) for size in sizes]
+        + [pltpu.SemaphoreType.DMA((ARRAYS,)), pltpu.SemaphoreType.DMA((len(sizes),))],
         compiler_params=params(PACK_MIB),
         name="pack",
-    )(chip_ref, k, kd, v, vd, q, qd)
+    )(chip_ref, *arrays)
     blocks, late = blocks[:CHIPS], blocks[CHIPS:]
     arrived = []
     for place, gate in enumerate(GATES):

time: 213 us -> 212 us (level)
  no operation moved by 1% of the time
where the time goes in v6:
time: 212 us
  starting transfers between devices  111 us (52%)
  waiting for transfers between devices  83.6 us (39%)
  Pallas kernels  13.8 us (7%)
    ppermute x16, starting transfers between devices, exchange(): return lax.ppermute(block, 'ctx', pairs)  90.5 us
    ppermute x16, waiting for transfers between devices, exchange(): return lax.ppermute(block, 'ctx', pairs)  67.7 us
    all_to_all x1, starting transfers between devices, gather_gains(): gains = lax.all_to_all(gains, 'dp', 0, 0, tiled=True)  16.2 us
    all_to_all x1, waiting for transfers between devices, gather_gains(): gains = lax.all_to_all(gains, 'dp', 0, 0, tiled=True)  15.9 us
    pallas_call x2, Pallas kernels, attend(): pl.pallas_call(functools.partial(attend_kernel, places), out_shape=[shape...  8 us
    ppermute x1, starting transfers between devices, swap(): lax.ppermute(block, 'ctx', [(place, place ^ 1) for place in range(2 * CHI...  4.86 us
  transfers between devices with their start and end apart: 18, of which 5 were waited for; matrix products, arithmetic and copies ran while one was open for 0% of the time, Pallas kernels for 4%

profile of v6, /device:TPU:1, one launch (start us, length us, event | category | flops | bytes accessed | tf_op | source)
XLA Modules:
  0.0 211.6 jit_solution(17625218498562629874)
XLA Ops:
  0.7 4.0 %pack.1 = (bf16[1552,128]{1,0:T(8,128)(2,1)}, bf16[1552,128]{1,0:T(8,128)(2,1)}, bf16[1552,128]{1,0:T(8,128)(2,1)}, bf16[1552,128]{1,0:T(8,128)(2,1)}, bf16[1552...) custom-call(s32[1]{0:T(128)} %bitcast.chip_ref, ...), custom_call_target="tpu_custom_call" | custom-call | tf_op jit(solution)/shard_map/pack/pallas_call | solution.py:234
  4.7 5.7 %collective-permute-start = (bf16[1552,128]{1,0:T(8,128)(2,1)}, bf16[1552,128]{1,0:T(8,128)(2,1)S(1)}, u32[]{:S(2)}, u32[]{:S(2)}) collective-permute-start(bf16[1552,128]{1,0:T(8,128)(2,1)} %get-tuple-element.31), channel_id=1, source_target_pairs={{0,4},{1,5},{2,6},{3,7},{4,0},{5,1},{6,2},{7,3},{8,12},{9,13},{10,... | collective-permute-start | bytes 1191944 | tf_op jit(solution)/shard_map/ppermute | solution.py:202
  10.4 3.5 %collective-permute-start.2 = (bf16[1552,128]{1,0:T(8,128)(2,1)}, bf16[1552,128]{1,0:T(8,128)(2,1)S(1)}, u32[]{:S(2)}, u32[]{:S(2)}) collective-permute-start(bf16[1552,128]{1,0:T(8,128)(2,1)} %get-tuple-element.36), channel_id=1, source_target_pairs={{0,2},{1,3},{2,0},{3,1},{4,6},{5,7},{6,4},{7,5},{8,10},{9,11},{10,... | collective-permute-start | bytes 1191944 | tf_op jit(solution)/shard_map/ppermute | solution.py:202
  13.9 8.8 %collective-permute-start.1 = (bf16[1552,128]{1,0:T(8,128)(2,1)}, bf16[1552,128]{1,0:T(8,128)(2,1)S(1)}, u32[]{:S(2)}, u32[]{:S(2)}) collective-permute-start(bf16[1552,128]{1,0:T(8,128)(2,1)} %get-tuple-element.34), channel_id=1, source_target_pairs={{0,8},{1,9},{2,10},{3,11},{4,12},{5,13},{6,14},{7,15},{8,0},{9,1},... | collective-permute-start | bytes 1191944 | tf_op jit(solution)/shard_map/ppermute | solution.py:202
  22.8 1.9 collective-permute-start.3
  24.7 1.9 collective-permute-start.4
  26.6 12.1 %collective-permute-done.refs_3_ = bf16[1552,128]{1,0:T(8,128)(2,1)S(1)} collective-permute-done((bf16[1552,128]{1,0:T(8,128)(2,1)}, bf16[1552,128]{1,0:T(8,128)(2,1)S(1)}, u32[]{:S(2)}, u32[]{:S(2)}) %collective-permute-start) | collective-permute-done | bytes 397344 | tf_op jit(solution)/shard_map/ppermute | solution.py:202
  38.7 1.9 collective-permute-start.6
  40.6 9.8 %collective-permute-start.5 = (bf16[1040,128]{1,0:T(8,128)(2,1)}, bf16[1040,128]{1,0:T(8,128)(2,1)S(1)}, u32[]{:S(2)}, u32[]{:S(2)}) collective-permute-start(bf16[1040,128]{1,0:T(8,128)(2,1)} %get-tuple-element.41), channel_id=1, source_target_pairs={{0,14},{1,15},{2,12},{3,13},{4,10},{5,11},{6,8},{7,9},{8,6},{9,7},... | collective-permute-start | bytes 798728 | tf_op jit(solution)/shard_map/ppermute | solution.py:202
  50.5 0.6 broadcast_in_dim.12
  51.1 16.2 %all-to-all-start = ((bf16[32,2,128]{2,1,0:T(2,128)(2,1)}), bf16[32,2,128]{2,1,0:T(2,128)(2,1)S(1)}, u32[]{:S(2)}, u32[]{:S(2)}) async-start(bf16[32,2,128]{2,1,0:T(2,128)(2,1)} %broadcast_in_dim.12), calls=%async_computation | async-start | bytes 32768 | tf_op jit(solution)/shard_map/all_to_all | solution.py:221
  67.3 15.9 %all-to-all-done = bf16[32,2,128]{2,1,0:T(2,128)(2,1)S(1)} async-done(((bf16[32,2,128]{2,1,0:T(2,128)(2,1)}), bf16[32,2,128]{2,1,0:T(2,128)(2,1)S(1)}, u32[]{:S(2)}, u32[]{:S(2)}) %all-to-all-start) | async-done | bytes 16416 | tf_op jit(solution)/shard_map/all_to_all | solution.py:221
  83.2 0.0 collective-permute-done.1.refs_0_
  83.2 35.9 %collective-permute-done.3.refs_2_ = bf16[1552,128]{1,0:T(8,128)(2,1)S(1)} collective-permute-done((bf16[1552,128]{1,0:T(8,128)(2,1)}, bf16[1552,128]{1,0:T(8,128)(2,1)S(1)}, u32[]{:S(2)}, u32[]{:S(2)}) %collective-permute-start.3) | collective-permute-done | bytes 397344 | tf_op jit(solution)/shard_map/ppermute | solution.py:202
  119.1 0.0 collective-permute-done.4.refs_4_
  119.1 1.0 copy-done
  120.1 0.6 norm.1
  120.8 4.9 %collective-permute-start.7 = (bf16[4,4,512,128]{3,2,1,0:T(8,128)(2,1)S(1)}, bf16[4,4,512,128]{3,2,1,0:T(8,128)(2,1)S(1)}, u32[]{:S(2)}, u32[]{:S(2)}) collective-permute-start(bf16[4,4,512,128]{3,2,1,0:T(8,128)(2,1)S(1)} %get-tuple-element.45.own_ref), channel_id=1, source_target_pairs={{0,1},{1,0},{2,3},{3,2},{4,5},{5,4},{6,7},{7,6},{8,9},{9,8},{10,11... | collective-permute-start | bytes 6291464 | tf_op jit(solution)/shard_map/ppermute | solution.py:206
  125.6 3.4 %collective-permute-start.10 = (bf16[512,128]{1,0:T(8,128)(2,1)S(1)}, bf16[512,128]{1,0:T(8,128)(2,1)S(1)}, u32[]{:S(2)}, u32[]{:S(2)}) collective-permute-start(bf16[512,128]{1,0:T(8,128)(2,1)S(1)} %copy-done.3), channel_id=1, source_target_pairs={{0,14},{1,15},{2,12},{3,13},{4,10},{5,11},{6,8},{7,9},{8,6},{9,7},... | collective-permute-start | bytes 393224 | tf_op jit(solution)/shard_map/ppermute | solution.py:202
  129.1 11.4 %collective-permute-start.11 = (bf16[512,128]{1,0:T(8,128)(2,1)S(1)}, bf16[512,128]{1,0:T(8,128)(2,1)S(1)}, u32[]{:S(2)}, u32[]{:S(2)}) collective-permute-start(bf16[512,128]{1,0:T(8,128)(2,1)S(1)} %copy-done.2), channel_id=1, source_target_pairs={{0,12},{1,13},{2,14},{3,15},{4,8},{5,9},{6,10},{7,11},{8,4},{9,5},... | collective-permute-start | bytes 393224 | tf_op jit(solution)/shard_map/ppermute | solution.py:202
  140.5 5.2 %attend.2 = (bf16[512,128]{1,0:T(8,128)(2,1)S(1)}, bf16[512,128]{1,0:T(8,128)(2,1)S(1)}, bf16[512,128]{1,0:T(8,128)(2,1)S(1)}, bf16[512,128]{1,0:T(8,128)(2,1)S(...) custom-call(bf16[2,4,128]{2,1,0:T(4,128)(2,1)S(1)} %bitcast.15, ...), custom_call_target="tpu_custom_call" | custom-call | tf_op jit(solution)/shard_map/attend/pallas_call | solution.py:273
  145.7 20.5 %collective-permute-start.8 = (bf16[512,128]{1,0:T(8,128)(2,1)S(1)}, bf16[512,128]{1,0:T(8,128)(2,1)S(1)}, u32[]{:S(2)}, u32[]{:S(2)}) collective-permute-start(bf16[512,128]{1,0:T(8,128)(2,1)S(1)} %get-tuple-element.46), channel_id=1, source_target_pairs={{0,8},{1,9},{2,10},{3,11},{4,12},{5,13},{6,14},{7,15},{8,0},{9,1},... | collective-permute-start | bytes 393224 | tf_op jit(solution)/shard_map/ppermute | solution.py:202
  166.2 1.9 collective-permute-start.9
  168.1 2.2 %collective-permute-start.14 = (bf16[512,128]{1,0:T(8,128)(2,1)S(1)}, bf16[512,128]{1,0:T(8,128)(2,1)S(1)}, u32[]{:S(2)}, u32[]{:S(2)}) collective-permute-start(bf16[512,128]{1,0:T(8,128)(2,1)S(1)} %get-tuple-element.52), channel_id=1, source_target_pairs={{0,2},{1,3},{2,0},{3,1},{4,6},{5,7},{6,4},{7,5},{8,10},{9,11},{10,... | collective-permute-start | bytes 393224 | tf_op jit(solution)/shard_map/ppermute | solution.py:202
  170.3 6.5 %collective-permute-start.15 = (bf16[512,128]{1,0:T(8,128)(2,1)S(1)}, bf16[512,128]{1,0:T(8,128)(2,1)S(1)}, u32[]{:S(2)}, u32[]{:S(2)}) collective-permute-start(bf16[512,128]{1,0:T(8,128)(2,1)S(1)} %get-tuple-element.53), channel_id=1, source_target_pairs={{0,4},{1,5},{2,6},{3,7},{4,0},{5,1},{6,2},{7,3},{8,12},{9,13},{10,... | collective-permute-start | bytes 393224 | tf_op jit(solution)/shard_map/ppermute | solution.py:202
  176.9 3.1 %collective-permute-start.16 = (bf16[512,128]{1,0:T(8,128)(2,1)S(1)}, bf16[512,128]{1,0:T(8,128)(2,1)S(1)}, u32[]{:S(2)}, u32[]{:S(2)}) collective-permute-start(bf16[512,128]{1,0:T(8,128)(2,1)S(1)} %get-tuple-element.54), channel_id=1, source_target_pairs={{0,6},{1,7},{2,4},{3,5},{4,2},{5,3},{6,0},{7,1},{8,14},{9,15},{10,... | collective-permute-start | bytes 393224 | tf_op jit(solution)/shard_map/ppermute | solution.py:202
  180.0 2.8 %attend.3 = (bf16[512,128]{1,0:T(8,128)(2,1)S(1)}, bf16[512,128]{1,0:T(8,128)(2,1)S(1)}) custom-call(bf16[2,4,128]{2,1,0:T(4,128)(2,1)S(1)} %bitcast.16, f32[512,128]{1,0:T(8,128)S(1)} %get-tuple-element.44.table_ref, bf16[4,4,512,128]{3,2,1,0:T(8,128)(2,1)S(1)} %get-tuple-element.45.own_ref, bf16[4,4,512,128]{3,2,1,0:T(8,128)(2,1)S(1)} %collective-permute-done.7.other_ref, ...), custom_call_target="tpu_custom_call" | custom-call | tf_op jit(solution)/shard_map/attend/pallas_call | solution.py:273
  182.8 4.2 %collective-permute-done.8.refs_0_ = bf16[512,128]{1,0:T(8,128)(2,1)S(1)} collective-permute-done((bf16[512,128]{1,0:T(8,128)(2,1)S(1)}, bf16[512,128]{1,0:T(8,128)(2,1)S(1)}, u32[]{:S(2)}, u32[]{:S(2)}) %collective-permute-start.8) | collective-permute-done | bytes 131104 | tf_op jit(solution)/shard_map/ppermute | solution.py:202
  186.9 5.9 %collective-permute-start.12 = (bf16[512,128]{1,0:T(8,128)(2,1)S(1)}, bf16[512,128]{1,0:T(8,128)(2,1)S(1)}, u32[]{:S(2)}, u32[]{:S(2)}) collective-permute-start(bf16[512,128]{1,0:T(8,128)(2,1)S(1)} %get-tuple-element.50), channel_id=1, source_target_pairs={{0,14},{1,15},{2,12},{3,13},{4,10},{5,11},{6,8},{7,9},{8,6},{9,7},... | collective-permute-start | bytes 393224 | tf_op jit(solution)/shard_map/ppermute | solution.py:202
  192.8 1.9 collective-permute-start.13
  194.8 15.5 %collective-permute-done.16.refs_6_ = bf16[512,128]{1,0:T(8,128)(2,1)S(1)} collective-permute-done((bf16[512,128]{1,0:T(8,128)(2,1)S(1)}, bf16[512,128]{1,0:T(8,128)(2,1)S(1)}, u32[]{:S(2)}, u32[]{:S(2)}) %collective-permute-start.16) | collective-permute-done | bytes 131104 | tf_op jit(solution)/shard_map/ppermute | solution.py:202
  210.3 1.2 unpack.1
  (25 shorter events, 0.1 us)
Async XLA Ops:
  0.6 49.8 %copy-start.4 = (bf16[128]{0:T(256)(128)(2,1)S(1)}, bf16[128]{0:T(256)(128)(2,1)}, u32[]{:S(2)}) copy-start(bf16[128]{0:T(256)(128)(2,1)} %param.15) | copy-start | bytes 772
  0.6 49.8 %copy-start.5 = (bf16[128]{0:T(256)(128)(2,1)S(1)}, bf16[128]{0:T(256)(128)(2,1)}, u32[]{:S(2)}) copy-start(bf16[128]{0:T(256)(128)(2,1)} %param.14) | copy-start | bytes 772
  4.7 34.1 %collective-permute-start = (bf16[1552,128]{1,0:T(8,128)(2,1)}, bf16[1552,128]{1,0:T(8,128)(2,1)S(1)}, u32[]{:S(2)}, u32[]{:S(2)}) collective-permute-start(bf16[1552,128]{1,0:T(8,128)(2,1)} %get-tuple-element.31), channel_id=1, source_target_pairs={{0,4},{1,5},{2,6},{3,7},{4,0},{5,1},{6,2},{7,3},{8,12},{9,13},{10,... | collective-permute-start | bytes 1191944 | tf_op jit(solution)/shard_map/ppermute | solution.py:202
  10.4 30.3 %collective-permute-start.2 = (bf16[1552,128]{1,0:T(8,128)(2,1)}, bf16[1552,128]{1,0:T(8,128)(2,1)S(1)}, u32[]{:S(2)}, u32[]{:S(2)}) collective-permute-start(bf16[1552,128]{1,0:T(8,128)(2,1)} %get-tuple-element.36), channel_id=1, source_target_pairs={{0,2},{1,3},{2,0},{3,1},{4,6},{5,7},{6,4},{7,5},{8,10},{9,11},{10,... | collective-permute-start | bytes 1191944 | tf_op jit(solution)/shard_map/ppermute | solution.py:202
  13.9 69.3 %collective-permute-start.1 = (bf16[1552,128]{1,0:T(8,128)(2,1)}, bf16[1552,128]{1,0:T(8,128)(2,1)S(1)}, u32[]{:S(2)}, u32[]{:S(2)}) collective-permute-start(bf16[1552,128]{1,0:T(8,128)(2,1)} %get-tuple-element.34), channel_id=1, source_target_pairs={{0,8},{1,9},{2,10},{3,11},{4,12},{5,13},{6,14},{7,15},{8,0},{9,1},... | collective-permute-start | bytes 1191944 | tf_op jit(solution)/shard_map/ppermute | solution.py:202
  22.8 96.3 %collective-permute-start.3 = (bf16[1552,128]{1,0:T(8,128)(2,1)}, bf16[1552,128]{1,0:T(8,128)(2,1)S(1)}, u32[]{:S(2)}, u32[]{:S(2)}) collective-permute-start(bf16[1552,128]{1,0:T(8,128)(2,1)} %get-tuple-element.38), channel_id=1, source_target_pairs={{0,10},{1,11},{2,8},{3,9},{4,14},{5,15},{6,12},{7,13},{8,2},{9,3},... | collective-permute-start | bytes 1191944 | tf_op jit(solution)/shard_map/ppermute | solution.py:202
  24.7 94.4 %collective-permute-start.4 = (bf16[1552,128]{1,0:T(8,128)(2,1)}, bf16[1552,128]{1,0:T(8,128)(2,1)S(1)}, u32[]{:S(2)}, u32[]{:S(2)}) collective-permute-start(bf16[1552,128]{1,0:T(8,128)(2,1)} %get-tuple-element.40), channel_id=1, source_target_pairs={{0,6},{1,7},{2,4},{3,5},{4,2},{5,3},{6,0},{7,1},{8,14},{9,15},{10,... | collective-permute-start | bytes 1191944 | tf_op jit(solution)/shard_map/ppermute | solution.py:202
  38.7 80.4 %collective-permute-start.6 = (bf16[1040,128]{1,0:T(8,128)(2,1)}, bf16[1040,128]{1,0:T(8,128)(2,1)S(1)}, u32[]{:S(2)}, u32[]{:S(2)}) collective-permute-start(bf16[1040,128]{1,0:T(8,128)(2,1)} %get-tuple-element.42), channel_id=1, source_target_pairs={{0,12},{1,13},{2,14},{3,15},{4,8},{5,9},{6,10},{7,11},{8,4},{9,5},... | collective-permute-start | bytes 798728 | tf_op jit(solution)/shard_map/ppermute | solution.py:202
  40.6 78.5 %collective-permute-start.5 = (bf16[1040,128]{1,0:T(8,128)(2,1)}, bf16[1040,128]{1,0:T(8,128)(2,1)S(1)}, u32[]{:S(2)}, u32[]{:S(2)}) collective-permute-start(bf16[1040,128]{1,0:T(8,128)(2,1)} %get-tuple-element.41), channel_id=1, source_target_pairs={{0,14},{1,15},{2,12},{3,13},{4,10},{5,11},{6,8},{7,9},{8,6},{9,7},... | collective-permute-start | bytes 798728 | tf_op jit(solution)/shard_map/ppermute | solution.py:202
  51.1 32.1 %all-to-all-start = ((bf16[32,2,128]{2,1,0:T(2,128)(2,1)}), bf16[32,2,128]{2,1,0:T(2,128)(2,1)S(1)}, u32[]{:S(2)}, u32[]{:S(2)}) async-start(bf16[32,2,128]{2,1,0:T(2,128)(2,1)} %broadcast_in_dim.12), calls=%async_computation | async-start | bytes 32768 | tf_op jit(solution)/shard_map/all_to_all | solution.py:221
  119.1 1.0 copy-start
  120.1 5.5 %copy-start.3 = (bf16[512,128]{1,0:T(8,128)(2,1)S(1)}, bf16[512,128]{1,0:T(8,128)(2,1)}, u32[]{:S(2)}) copy-start(bf16[512,128]{1,0:T(8,128)(2,1)} %get-tuple-element.48) | copy-start | bytes 393220
  120.1 8.9 %copy-start.2 = (bf16[512,128]{1,0:T(8,128)(2,1)S(1)}, bf16[512,128]{1,0:T(8,128)(2,1)}, u32[]{:S(2)}) copy-start(bf16[512,128]{1,0:T(8,128)(2,1)} %get-tuple-element.49) | copy-start | bytes 393220
  120.1 20.3 %copy-start.1 = (bf16[1552,128]{1,0:T(8,128)(2,1)S(1)}, bf16[1552,128]{1,0:T(8,128)(2,1)}, u32[]{:S(2)}) copy-start(bf16[1552,128]{1,0:T(8,128)(2,1)} %get-tuple-element.43.refs_7_.refs_5_) | copy-start | bytes 1191940
  120.8 19.7 %collective-permute-start.7 = (bf16[4,4,512,128]{3,2,1,0:T(8,128)(2,1)S(1)}, bf16[4,4,512,128]{3,2,1,0:T(8,128)(2,1)S(1)}, u32[]{:S(2)}, u32[]{:S(2)}) collective-permute-start(bf16[4,4,512,128]{3,2,1,0:T(8,128)(2,1)S(1)} %get-tuple-element.45.own_ref), channel_id=1, source_target_pairs={{0,1},{1,0},{2,3},{3,2},{4,5},{5,4},{6,7},{7,6},{8,9},{9,8},{10,11... | collective-permute-start | bytes 6291464 | tf_op jit(solution)/shard_map/ppermute | solution.py:206
  125.6 44.7 %collective-permute-start.10 = (bf16[512,128]{1,0:T(8,128)(2,1)S(1)}, bf16[512,128]{1,0:T(8,128)(2,1)S(1)}, u32[]{:S(2)}, u32[]{:S(2)}) collective-permute-start(bf16[512,128]{1,0:T(8,128)(2,1)S(1)} %copy-done.3), channel_id=1, source_target_pairs={{0,14},{1,15},{2,12},{3,13},{4,10},{5,11},{6,8},{7,9},{8,6},{9,7},... | collective-permute-start | bytes 393224 | tf_op jit(solution)/shard_map/ppermute | solution.py:202
  129.1 47.8 %collective-permute-start.11 = (bf16[512,128]{1,0:T(8,128)(2,1)S(1)}, bf16[512,128]{1,0:T(8,128)(2,1)S(1)}, u32[]{:S(2)}, u32[]{:S(2)}) collective-permute-start(bf16[512,128]{1,0:T(8,128)(2,1)S(1)} %copy-done.2), channel_id=1, source_target_pairs={{0,12},{1,13},{2,14},{3,15},{4,8},{5,9},{6,10},{7,11},{8,4},{9,5},... | collective-permute-start | bytes 393224 | tf_op jit(solution)/shard_map/ppermute | solution.py:202
  145.7 41.2 %collective-permute-start.8 = (bf16[512,128]{1,0:T(8,128)(2,1)S(1)}, bf16[512,128]{1,0:T(8,128)(2,1)S(1)}, u32[]{:S(2)}, u32[]{:S(2)}) collective-permute-start(bf16[512,128]{1,0:T(8,128)(2,1)S(1)} %get-tuple-element.46), channel_id=1, source_target_pairs={{0,8},{1,9},{2,10},{3,11},{4,12},{5,13},{6,14},{7,15},{8,0},{9,1},... | collective-permute-start | bytes 393224 | tf_op jit(solution)/shard_map/ppermute | solution.py:202
  166.2 26.6 %collective-permute-start.9 = (bf16[512,128]{1,0:T(8,128)(2,1)S(1)}, bf16[512,128]{1,0:T(8,128)(2,1)S(1)}, u32[]{:S(2)}, u32[]{:S(2)}) collective-permute-start(bf16[512,128]{1,0:T(8,128)(2,1)S(1)} %get-tuple-element.47), channel_id=1, source_target_pairs={{0,10},{1,11},{2,8},{3,9},{4,14},{5,15},{6,12},{7,13},{8,2},{9,3},... | collective-permute-start | bytes 393224 | tf_op jit(solution)/shard_map/ppermute | solution.py:202
  168.1 26.7 %collective-permute-start.14 = (bf16[512,128]{1,0:T(8,128)(2,1)S(1)}, bf16[512,128]{1,0:T(8,128)(2,1)S(1)}, u32[]{:S(2)}, u32[]{:S(2)}) collective-permute-start(bf16[512,128]{1,0:T(8,128)(2,1)S(1)} %get-tuple-element.52), channel_id=1, source_target_pairs={{0,2},{1,3},{2,0},{3,1},{4,6},{5,7},{6,4},{7,5},{8,10},{9,11},{10,... | collective-permute-start | bytes 393224 | tf_op jit(solution)/shard_map/ppermute | solution.py:202
  170.3 24.5 %collective-permute-start.15 = (bf16[512,128]{1,0:T(8,128)(2,1)S(1)}, bf16[512,128]{1,0:T(8,128)(2,1)S(1)}, u32[]{:S(2)}, u32[]{:S(2)}) collective-permute-start(bf16[512,128]{1,0:T(8,128)(2,1)S(1)} %get-tuple-element.53), channel_id=1, source_target_pairs={{0,4},{1,5},{2,6},{3,7},{4,0},{5,1},{6,2},{7,3},{8,12},{9,13},{10,... | collective-permute-start | bytes 393224 | tf_op jit(solution)/shard_map/ppermute | solution.py:202
  176.9 33.5 %collective-permute-start.16 = (bf16[512,128]{1,0:T(8,128)(2,1)S(1)}, bf16[512,128]{1,0:T(8,128)(2,1)S(1)}, u32[]{:S(2)}, u32[]{:S(2)}) collective-permute-start(bf16[512,128]{1,0:T(8,128)(2,1)S(1)} %get-tuple-element.54), channel_id=1, source_target_pairs={{0,6},{1,7},{2,4},{3,5},{4,2},{5,3},{6,0},{7,1},{8,14},{9,15},{10,... | collective-permute-start | bytes 393224 | tf_op jit(solution)/shard_map/ppermute | solution.py:202
  186.9 23.4 %collective-permute-start.12 = (bf16[512,128]{1,0:T(8,128)(2,1)S(1)}, bf16[512,128]{1,0:T(8,128)(2,1)S(1)}, u32[]{:S(2)}, u32[]{:S(2)}) collective-permute-start(bf16[512,128]{1,0:T(8,128)(2,1)S(1)} %get-tuple-element.50), channel_id=1, source_target_pairs={{0,14},{1,15},{2,12},{3,13},{4,10},{5,11},{6,8},{7,9},{8,6},{9,7},... | collective-permute-start | bytes 393224 | tf_op jit(solution)/shard_map/ppermute | solution.py:202
  192.8 17.5 %collective-permute-start.13 = (bf16[512,128]{1,0:T(8,128)(2,1)S(1)}, bf16[512,128]{1,0:T(8,128)(2,1)S(1)}, u32[]{:S(2)}, u32[]{:S(2)}) collective-permute-start(bf16[512,128]{1,0:T(8,128)(2,1)S(1)} %get-tuple-element.51), channel_id=1, source_target_pairs={{0,12},{1,13},{2,14},{3,15},{4,8},{5,9},{6,10},{7,11},{8,4},{9,5},... | collective-permute-start | bytes 393224 | tf_op jit(solution)/shard_map/ppermute | solution.py:202
